TPU v7x, 128 devices: a whole 4x4x4 slice. The times are simulated.
128 devices in a mesh: ty: 8 (over z, core), tx: 16 (over y, x).
Axes of the slice: x: 4, y: 4, z: 4, core: 2. Of those that a mesh axis runs over, the one named last changes fastest.
Arguments:
- lam_tracer: float32 [16, 256, 4096], P(None, 'ty', 'tx'), may hold values from -6 to 6
- lam_eta: float32 [256, 4096], P('ty', 'tx'), may hold values from -60 to 60
- land: int32 [256, 4096], P('ty', 'tx'), may hold values 0 or 1
- zonal_flow: float32 [2, 16, 256, 4096], P(None, None, 'ty', 'tx'), may hold values from -1.5 to 1.5
- merid_flow: float32 [2, 16, 256, 4096], P(None, None, 'ty', 'tx'), may hold values from -1.5 to 1.5
- zonal_mixing: float32 [16, 256, 4096], P(None, 'ty', 'tx'), may hold values from 0.02 to 0.12
- merid_mixing: float32 [16, 256, 4096], P(None, 'ty', 'tx'), may hold values from 0.02 to 0.12
- surface_east: float32 [256, 4096], P('ty', 'tx'), may hold values from 1 to 8
- surface_north: float32 [256, 4096], P('ty', 'tx'), may hold values from 1 to 8
- surface_diag: float32 [256, 4096], P('ty', 'tx'), may hold values from 0.2 to 1
- steric: float32 [16], replicated, may hold values from 0.2 to 1
- eta_saved: float32 [256, 4096], P('ty', 'tx'), may hold values from -6 to 6
- obs_sla: float32 [131072, 128], P(('ty', 'tx')), may hold values from -6 to 6
- obs_weight: float32 [131072, 128], P(('ty', 'tx')), may hold values from 0.05 to 0.5
- obs_tile: int32 [131072, 1], P(('ty', 'tx')), may hold values from 0 to 127; in each aligned block of 1024 rows (0 to 1023, 1024 to 2047, ...) at most 16 rows name the same one
- obs_start: int32 [131072], P(('ty', 'tx')), may hold values from 0 to 8064, as said below
- obs_count: int32 [131072], P(('ty', 'tx')), may hold values from 1 to 128
Outputs:
- lam_tracer_start: float32 [16, 256, 4096], P(None, 'ty', 'tx')
- lam_eta_start: float32 [256, 4096], P('ty', 'tx')
Inputs may be any that keep to these rules, and one draw needn't show every extreme that they name: `obs_tile`: in the rows of one device no tile is named by more than 16 segments, a bound that some block reaches; every tile is named somewhere. `obs_start`: A segment's 128 cells lie in one row of its tile.
All inputs are finite; a program needn't handle non-finite values. No bound on the sum of `land` on one device may be relied on, other than what follows from the above.
Results may differ from a plain program's by a relative error of at most 0.0003.
Values sent between devices are 32-bit elements; how exact they have to be, the bound alone decides.
No kernel may reach another device: no remote copies, remote signals or barrier semaphores. Data moves between devices by JAX's collectives and lax.ppermute only.
A program may use at most 64 MiB of HBM per device.

v0:
```python
import jax
import jax.numpy as jnp
from jax import lax
from jax.sharding import PartitionSpec as P

ITERS = 3


def extended_2(cells, sides, width):
    for axis, dim in sides:
        count = lax.axis_size(axis)
        head = lax.slice_in_dim(cells, 0, width, axis=dim)
        tail = lax.slice_in_dim(cells, cells.shape[dim] - width, cells.shape[dim], axis=dim)
        cells = jnp.concatenate(
            [
                lax.ppermute(tail, axis, [(i, (i + 1) % count) for i in range(count)]),
                cells,
                lax.ppermute(head, axis, [((i + 1) % count, i) for i in range(count)]),
            ],
            axis=dim,
        )
    return cells


def extended(field):
    return extended_2(field, (("ty", 1), ("tx", 2)), 1)


def square_sum(resid):
    return lax.psum(jnp.sum(resid * resid), ("ty", "tx"))


def tracer_back(masked, zonal, merid, zonal_mix, merid_mix):
    levels = masked.shape[0]
    padded = extended(masked)
    diff_x = masked - padded[:, 1:-1, 2:]
    diff_y = masked - padded[:, 2:, 1:-1]
    carried = jnp.concatenate(
        [(0.5 * zonal - zonal_mix) * diff_x, (0.5 * merid - merid_mix) * diff_y], axis=0
    )
    carried_pad = extended(carried)
    from_west = carried_pad[:levels, 1:-1, :-2]
    from_south = carried_pad[levels:, :-2, 1:-1]
    result = (0.5 * zonal + zonal_mix) * diff_x + from_west
    result = result + (0.5 * merid + merid_mix) * diff_y + from_south
    return masked - result


def on_device(
    lam_tracer,
    lam_eta,
    land,
    zonal_flow,
    merid_flow,
    zonal_mixing,
    merid_mixing,
    surface_east,
    surface_north,
    surface_diag,
    steric,
    eta_saved,
    obs_sla,
    obs_weight,
    obs_tile,
    obs_start,
    obs_count,
):
    levels, rows, cols = lam_tracer.shape
    n_rows = lax.axis_size("ty")
    n_cols = lax.axis_size("tx")
    devices = n_rows * n_cols
    row_ids = lax.broadcasted_iota(jnp.int32, (rows, 1), 0) + lax.axis_index("ty") * rows
    open_rows = (row_ids < rows * n_rows - 1).astype(jnp.float32)
    merid_flow = merid_flow * open_rows
    merid_mixing = merid_mixing * open_rows
    surface_north = surface_north * open_rows
    ocean = land.astype(jnp.float32)
    highest = lax.Precision.HIGHEST
    seg_dev, points = obs_sla.shape
    capacity = 2 * seg_dev // devices
    slots = devices * capacity
    target = obs_tile[:, 0]
    tile_hit = target[:, None] == jnp.arange(devices, dtype=jnp.int32)[None, :]
    tile_flag = tile_hit.astype(jnp.bfloat16)
    seg_ids = jnp.arange(seg_dev, dtype=jnp.int32)
    earlier = (seg_ids[None, :] < seg_ids[:, None]).astype(jnp.bfloat16)
    before = jnp.dot(earlier, tile_flag, preferred_element_type=jnp.float32)
    slot = jnp.sum(jnp.where(tile_hit, before, jnp.float32(0.0)), axis=1).astype(jnp.int32)
    where_to = target * capacity + slot
    placed = where_to[None, :] == jnp.arange(slots, dtype=jnp.int32)[:, None]
    stacked = jnp.concatenate([obs_sla, obs_weight], axis=1)
    packed = jnp.dot(placed.astype(jnp.float32), stacked, precision=highest)
    send_sla = packed[:, :points]
    send_weight = packed[:, points:]
    send_start = jnp.sum(jnp.where(placed, obs_start[None, :], 0), axis=1)
    send_count = jnp.sum(jnp.where(placed, obs_count[None, :], 0), axis=1)
    got = (
        lax.all_to_all(
            send_sla.reshape(devices, capacity, points),
            ("ty", "tx"),
            split_axis=0,
            concat_axis=0,
            tiled=True,
        ),
        lax.all_to_all(
            send_weight.reshape(devices, capacity, points),
            ("ty", "tx"),
            split_axis=0,
            concat_axis=0,
            tiled=True,
        ),
        lax.all_to_all(
            send_start.reshape(devices, capacity),
            ("ty", "tx"),
            split_axis=0,
            concat_axis=0,
            tiled=True,
        ),
        lax.all_to_all(
            send_count.reshape(devices, capacity),
            ("ty", "tx"),
            split_axis=0,
            concat_axis=0,
            tiled=True,
        ),
    )
    got_sla = got[0].reshape(slots, points)
    got_weight = got[1].reshape(slots, points)
    got_start = got[2].reshape(slots)
    got_count = got[3].reshape(slots)
    row_of = got_start // cols
    col_of = got_start % cols
    row_pick = (row_of[:, None] == jnp.arange(rows, dtype=jnp.int32)[None, :]).astype(jnp.float32)
    eta_rows = jnp.dot(row_pick, eta_saved, precision=highest)
    obs_pair = jnp.concatenate(
        [
            jnp.stack([got_sla, got_weight], axis=0),
            jnp.zeros((2, slots, cols - points), jnp.float32),
        ],
        axis=2,
    )
    for bit in range((cols - 1).bit_length()):
        moved = jnp.roll(obs_pair, 1 << bit, axis=2)
        flag = ((col_of >> bit) % 2 == 1)[None, :, None]
        obs_pair = jnp.where(flag, moved, obs_pair)
    column = jnp.arange(cols, dtype=jnp.int32)[None, :]
    live = (column >= col_of[:, None]) & (column < (col_of + got_count)[:, None])
    term = jnp.where(live, obs_pair[1] * (eta_rows - obs_pair[0]), jnp.float32(0.0))
    forcing = jnp.dot(row_pick.T, term, precision=highest)
    faces_pad = extended(jnp.stack([surface_east, surface_north], axis=0))
    east_from_west = faces_pad[0, 1:-1, :-2]
    north_from_south = faces_pad[1, :-2, 1:-1]
    mu_eta = lam_eta + forcing
    mu_tracer = lam_tracer
    for step in (1, 0):
        rhs = ocean * mu_eta
        solved = jnp.zeros_like(rhs)
        resid = rhs
        direction = rhs
        norm_now = square_sum(resid)
        for conjugate_step in range(ITERS):
            padded = extended(direction[None])[0]
            total = (
                (1.0 + surface_diag) * direction
                + surface_east * (direction - padded[1:-1, 2:])
                + east_from_west * (direction - padded[1:-1, :-2])
            )
            image = (
                total
                + surface_north * (direction - padded[2:, 1:-1])
                + north_from_south * (direction - padded[:-2, 1:-1])
            )
            alpha = norm_now / lax.psum(jnp.sum(direction * image), ("ty", "tx"))
            solved = solved + alpha * direction
            resid = resid - alpha * image
            norm_next = square_sum(resid)
            direction = resid + norm_next / norm_now * direction
            norm_now = norm_next
        mu_eta = solved
        masked = ocean[None] * (mu_tracer + steric[:, None, None] * solved[None])
        mu_tracer = tracer_back(
            masked, zonal_flow[step], merid_flow[step], zonal_mixing, merid_mixing
        )
    return (mu_tracer, mu_eta)


def solution(mesh):
    in_specs = (
        P(None, "ty", "tx"),
        P("ty", "tx"),
        P("ty", "tx"),
        P(None, None, "ty", "tx"),
        P(None, None, "ty", "tx"),
        P(None, "ty", "tx"),
        P(None, "ty", "tx"),
        P("ty", "tx"),
        P("ty", "tx"),
        P("ty", "tx"),
        P(),
        P("ty", "tx"),
        P(("ty", "tx"), None),
        P(("ty", "tx"), None),
        P(("ty", "tx"), None),
        P(("ty", "tx")),
        P(("ty", "tx")),
    )
    out_specs = (P(None, "ty", "tx"), P("ty", "tx"))
    return jax.shard_map(
        on_device, mesh=mesh, in_specs=in_specs, out_specs=out_specs, check_vma=False
    )
```

profile of v0, /device:TPU:1, one launch (start us, length us, event | category | flops | bytes accessed | tf_op | source)
XLA Modules:
  0.0 914.9 jit_solution(4086396995662425874)
XLA Ops:
  2.7 3.1 select_reduce_fusion
  6.5 11.5 %all-to-all-start = ((s32[128,1,16]{2,1,0:T(1,128)}), s32[128,1,16]{2,1,0:T(1,128)S(1)}, u32[]{:S(2)}, u32[]{:S(2)}) async-start(s32[128,1,16]{2,1,0:T(1,128)} %bitcast.1), calls=%async_computation | async-start | bytes 131072 | tf_op jit(solution)/shard_map/all_to_all | solution.py:112
  18.0 6.5 fusion
  25.3 2.4 all-to-all-done
  27.6 7.4 all-to-all-start.1
  35.1 2.7 fusion.115
  37.7 6.8 all-to-all-done.1
  44.5 23.1 %all_to_all.28 = f32[128,16,128]{2,1,0:T(8,128)S(1)} all-to-all(f32[128,16,128]{2,1,0:T(8,128)S(1)} %bitcast.89), channel_id=1, replica_groups=mesh['ty'=8,'tx'=16] {'ty','tx'}, dimensions={0} | all-to-all | bytes 2097152 | tf_op jit(solution)/shard_map/all_to_all | solution.py:98
  67.6 5.3 all-to-all-start.3
  73.1 1.9 collective-permute-start.4
  77.3 14.4 %all-to-all-done.3 = f32[128,16,128]{2,1,0:T(8,128)S(1)} async-done(((f32[128,16,128]{2,1,0:T(8,128)}), f32[128,16,128]{2,1,0:T(8,128)S(1)}, u32[]{:S(2)}, u32[]{:S(2)}) %all-to-all-start.3) | async-done | bytes 1048608 | tf_op jit(solution)/shard_map/all_to_all | solution.py:105
  92.0 1.8 pad_select_fusion
  94.5 3.1 maximum_select_fusion
  98.2 1.8 maximum_select_fusion.1
  100.6 1.8 maximum_select_fusion.2
  102.9 1.8 maximum_select_fusion.3
  105.3 1.8 maximum_select_fusion.4
  107.7 1.8 maximum_select_fusion.5
  110.4 3.4 fusion.4
  113.8 1.4 fusion.8
  115.2 1.8 collective-permute-start
  117.7 2.6 collective-permute-done.1
  120.7 4.5 collective-permute-start.3
  126.4 5.1 collective-permute-done.6
  132.2 64.7 %all-reduce.3 = (f32[]{:T(128)}, f32[]{:T(128)}) all-reduce(f32[]{:T(128)} %get-tuple-element.11, f32[]{:T(128)} %get-tuple-element.10), channel_id=1, replica_groups=mesh['ty'=8,'tx'=16] {'ty','tx'}, use_global_device_ids=true, to_apply=%region_4.5 | all-reduce | flops 2 | bytes 16 | tf_op jit(solution)/shard_map/psum | solution.py:30
  198.9 62.5 %psum.86 = f32[]{:T(128)} all-reduce(f32[]{:T(128)} %get-tuple-element.27), channel_id=1, replica_groups=mesh['ty'=8,'tx'=16] {'ty','tx'}, use_global_device_ids=true, to_apply=%region_8.9 | all-reduce | flops 1 | bytes 8 | tf_op jit(solution)/shard_map/psum | solution.py:30
  262.8 1.6 collective-permute-start.7
  265.1 2.3 collective-permute-done.8
  267.5 2.4 collective-permute-start.10
  270.8 5.0 collective-permute-done.9
  276.7 64.3 %psum.87 = f32[]{:T(128)} all-reduce(f32[]{:T(128)} %get-tuple-element.25), channel_id=1, replica_groups=mesh['ty'=8,'tx'=16] {'ty','tx'}, use_global_device_ids=true, to_apply=%region_10.11 | all-reduce | flops 1 | bytes 8 | tf_op jit(solution)/shard_map/psum | solution.py:173
  342.9 62.5 %psum.88 = f32[]{:T(128)} all-reduce(f32[]{:T(128)} %multiply_reduce_fusion.5), channel_id=1, replica_groups=mesh['ty'=8,'tx'=16] {'ty','tx'}, use_global_device_ids=true, to_apply=%region_12.13 | all-reduce | flops 1 | bytes 8 | tf_op jit(solution)/shard_map/psum | solution.py:30
  406.8 1.6 collective-permute-start.11
  409.2 2.3 collective-permute-done.12
  411.5 4.8 collective-permute-start.14
  418.3 66.7 %psum.89 = f32[]{:T(128)} all-reduce(f32[]{:T(128)} %fusion.63), channel_id=1, replica_groups=mesh['ty'=8,'tx'=16] {'ty','tx'}, use_global_device_ids=true, to_apply=%region_14.15 | all-reduce | flops 1 | bytes 8 | tf_op jit(solution)/shard_map/psum | solution.py:173
  490.4 4.1 collective-permute-start.24
  496.4 68.8 %all-reduce.2 = (f32[]{:T(128)}, f32[]{:T(128)}) all-reduce(f32[]{:T(128)} %get-tuple-element.9, f32[]{:T(128)} %get-tuple-element.8), channel_id=1, replica_groups=mesh['ty'=8,'tx'=16] {'ty','tx'}, use_global_device_ids=true, to_apply=%region_16.17 | all-reduce | flops 2 | bytes 16 | tf_op jit(solution)/shard_map/psum | solution.py:30
  567.1 62.7 %psum.92 = f32[]{:T(128)} all-reduce(f32[]{:T(128)} %get-tuple-element.20), channel_id=1, replica_groups=mesh['ty'=8,'tx'=16] {'ty','tx'}, use_global_device_ids=true, to_apply=%region_20.21 | all-reduce | flops 1 | bytes 8 | tf_op jit(solution)/shard_map/psum | solution.py:30
  631.2 1.6 collective-permute-start.25
  632.8 2.3 fusion.116
  635.9 4.8 collective-permute-start.28
  642.8 66.8 %psum.93 = f32[]{:T(128)} all-reduce(f32[]{:T(128)} %get-tuple-element.18), channel_id=1, replica_groups=mesh['ty'=8,'tx'=16] {'ty','tx'}, use_global_device_ids=true, to_apply=%region_22.23 | all-reduce | flops 1 | bytes 8 | tf_op jit(solution)/shard_map/psum | solution.py:173
  711.6 1.4 fusion.30
  712.9 62.6 %psum.94 = f32[]{:T(128)} all-reduce(f32[]{:T(128)} %multiply_reduce_fusion), channel_id=1, replica_groups=mesh['ty'=8,'tx'=16] {'ty','tx'}, use_global_device_ids=true, to_apply=%region_24.25 | all-reduce | flops 1 | bytes 8 | tf_op jit(solution)/shard_map/psum | solution.py:30
  776.9 1.6 collective-permute-start.29
  778.5 1.7 collective-permute-start.15
  781.7 4.6 collective-permute-start.32
  787.6 4.2 collective-permute-done.17
  791.8 2.4 subtract_multiply_fusion.3
  794.3 3.6 collective-permute-start.18
  798.7 65.6 %psum.95 = f32[]{:T(128)} all-reduce(f32[]{:T(128)} %fusion.37), channel_id=1, replica_groups=mesh['ty'=8,'tx'=16] {'ty','tx'}, use_global_device_ids=true, to_apply=%region_26.27 | all-reduce | flops 1 | bytes 8 | tf_op jit(solution)/shard_map/psum | solution.py:173
  866.7 1.4 copy.70
  868.2 5.8 collective-permute-done.20
  875.4 2.8 fusion.22
  878.2 2.7 collective-permute-start.33
  881.8 2.3 collective-permute-done.34
  884.5 7.9 collective-permute-done.35
  892.4 2.4 subtract_multiply_fusion.1
  897.0 2.6 collective-permute-done.37
  900.6 2.0 copy.75
  902.6 6.2 collective-permute-done.38
  908.8 2.1 copy.76
  910.9 2.5 fusion.13
  (156 shorter events, 41.9 us)
Async XLA Ops:
  0.6 109.7 %copy-start = (f32[32,256]{1,0:T(8,128)S(1)}, f32[32,256]{1,0:T(8,128)}, u32[]{:S(2)}) copy-start(f32[32,256]{1,0:T(8,128)} %param.28) | copy-start | bytes 98308
  6.5 21.1 %all-to-all-start = ((s32[128,1,16]{2,1,0:T(1,128)}), s32[128,1,16]{2,1,0:T(1,128)S(1)}, u32[]{:S(2)}, u32[]{:S(2)}) async-start(s32[128,1,16]{2,1,0:T(1,128)} %bitcast.1), calls=%async_computation | async-start | bytes 131072 | tf_op jit(solution)/shard_map/all_to_all | solution.py:112
  27.6 16.9 %all-to-all-start.1 = ((s32[128,1,16]{2,1,0:T(1,128)}), s32[128,1,16]{2,1,0:T(1,128)S(1)}, u32[]{:S(2)}, u32[]{:S(2)}) async-start(s32[128,1,16]{2,1,0:T(1,128)} %bitcast.2), calls=%async_computation.1 | async-start | bytes 131072 | tf_op jit(solution)/shard_map/all_to_all | solution.py:119
  35.0 37.9 %copy-start.4 = (f32[32,256]{1,0:T(8,128)S(1)}, f32[32,256]{1,0:T(8,128)}, u32[]{:S(2)}) copy-start(f32[32,256]{1,0:T(8,128)} %param.25) | copy-start | bytes 98308
  35.0 38.0 %copy-start.3 = (f32[32,256]{1,0:T(8,128)S(1)}, f32[32,256]{1,0:T(8,128)}, u32[]{:S(2)}) copy-start(f32[32,256]{1,0:T(8,128)} %param.24) | copy-start | bytes 98308
  67.6 24.1 %all-to-all-start.3 = ((f32[128,16,128]{2,1,0:T(8,128)}), f32[128,16,128]{2,1,0:T(8,128)S(1)}, u32[]{:S(2)}, u32[]{:S(2)}) async-start(f32[128,16,128]{2,1,0:T(8,128)} %bitcast.5), calls=%async_computation.3 | async-start | bytes 2097152 | tf_op jit(solution)/shard_map/all_to_all | solution.py:105
  73.0 819.4 %copy-start.11 = (f32[32]{0:T(128)}, f32[32]{0:T(128)S(1)}, u32[]{:S(2)}) copy-start(f32[32]{0:T(128)S(1)} %compare_convert_fusion) | copy-start | bytes 388
  73.1 43.9 %collective-permute-start.4 = (f32[2,1,256]{2,1,0:T(1,128)S(1)}, f32[2,1,256]{2,1,0:T(1,128)S(1)}, u32[]{:S(2)}, u32[]{:S(2)}) collective-permute-start(f32[2,1,256]{2,1,0:T(1,128)S(1)} %get-tuple-element.52), channel_id=1, source_target_pairs={{0,16},{16,32},{32,48},{48,64},{64,80},{80,96},{96,112},{112,0},{1... | collective-permute-start | bytes 6152 | tf_op jit(solution)/shard_map/ppermute | solution.py:16
  75.0 42.0 %collective-permute-start.5 = (f32[2,1,256]{2,1,0:T(1,128)S(1)}, f32[2,1,256]{2,1,0:T(1,128)S(1)}, u32[]{:S(2)}, u32[]{:S(2)}) collective-permute-start(f32[2,1,256]{2,1,0:T(1,128)S(1)} %get-tuple-element.53), channel_id=1, source_target_pairs={{16,0},{32,16},{48,32},{64,48},{80,64},{96,80},{112,96},{0,112},{1... | collective-permute-start | bytes 6152 | tf_op jit(solution)/shard_map/ppermute | solution.py:18
  110.3 3.4 copy-start.8
  110.3 3.4 copy-start.12
  110.3 21.1 %copy-start.5 = (f32[32,256]{1,0:T(8,128)S(1)}, f32[32,256]{1,0:T(8,128)}, u32[]{:S(2)}) copy-start(f32[32,256]{1,0:T(8,128)} %param.26) | copy-start | bytes 98308
  110.4 384.0 %copy-start.7 = (f32[2,16,32,256]{3,2,1,0:T(8,128)S(1)}, f32[2,16,32,256]{3,2,1,0:T(8,128)}, u32[]{:S(2)}) copy-start(f32[2,16,32,256]{3,2,1,0:T(8,128)} %param.21) | copy-start | bytes 3145732
  115.2 2.5 collective-permute-start
  117.0 3.3 collective-permute-start.1
  120.3 6.0 collective-permute-start.2
  120.7 590.8 %copy-start.13 = (f32[16]{0:T(128)S(1)}, f32[16]{0:T(128)}, u32[]{:S(2)}) copy-start(f32[16]{0:T(128)} %param.27) | copy-start | bytes 196
  120.7 5.6 collective-permute-start.3
  125.3 6.2 collective-permute-start.6
  262.8 2.3 collective-permute-start.7
  264.4 3.0 collective-permute-start.8
  267.5 3.3 collective-permute-start.10
  269.9 6.0 collective-permute-start.9
  406.8 2.3 collective-permute-start.11
  408.4 3.0 collective-permute-start.12
  411.5 6.0 collective-permute-start.13
  411.5 5.9 collective-permute-start.14
  486.4 305.5 %copy-start.1 = (f32[16,32,256]{2,1,0:T(8,128)S(1)}, f32[16,32,256]{2,1,0:T(8,128)}, u32[]{:S(2)}) copy-start(f32[16,32,256]{2,1,0:T(8,128)} %param.22) | copy-start | bytes 1572868
  486.4 1.8 collective-permute-start.21
  486.5 3.0 collective-permute-start.22
  489.6 6.0 collective-permute-start.23
  490.4 5.2 collective-permute-start.24
  631.2 3.9 collective-permute-start.25
  632.8 3.0 collective-permute-start.26
  635.9 6.0 collective-permute-start.27
  635.9 5.9 collective-permute-start.28
  776.9 3.5 collective-permute-start.29
  778.5 3.0 collective-permute-start.30
  778.5 7.9 collective-permute-start.15
  780.2 6.1 collective-permute-start.16
  781.5 6.0 collective-permute-start.31
  781.7 5.8 collective-permute-start.32
  786.4 5.5 collective-permute-start.17
  791.8 2.4 copy-start.6
  794.3 71.4 %collective-permute-start.18 = (f32[32,1,256]{2,0,1:T(8,128)S(1)}, f32[32,1,256]{2,0,1:T(8,128)S(1)}, u32[]{:S(2)}, u32[]{:S(2)}) collective-permute-start(f32[32,1,256]{2,0,1:T(8,128)S(1)} %get-tuple-element.43), channel_id=1, source_target_pairs={{0,16},{16,32},{32,48},{48,64},{64,80},{80,96},{96,112},{112,0},{1... | collective-permute-start | bytes 98312 | tf_op jit(solution)/shard_map/ppermute | solution.py:16
  797.9 67.8 %collective-permute-start.19 = (f32[32,1,256]{2,0,1:T(8,128)S(1)}, f32[32,1,256]{2,0,1:T(8,128)S(1)}, u32[]{:S(2)}, u32[]{:S(2)}) collective-permute-start(f32[32,1,256]{2,0,1:T(8,128)S(1)} %get-tuple-element.42), channel_id=1, source_target_pairs={{16,0},{32,16},{48,32},{64,48},{80,64},{96,80},{112,96},{0,112},{1... | collective-permute-start | bytes 98312 | tf_op jit(solution)/shard_map/ppermute | solution.py:18
  865.7 8.4 copy-start.9
  868.1 6.0 collective-permute-start.20
  868.2 15.9 %copy-start.10 = (f32[32,256]{1,0:T(8,128)}, f32[32,256]{1,0:T(8,128)S(1)}, u32[]{:S(2)}) copy-start(f32[32,256]{1,0:T(8,128)S(1)} %multiply_add_fusion) | copy-start | bytes 98308
  878.2 3.6 collective-permute-start.33
  880.9 30.0 %copy-start.2 = (f32[16,32,256]{2,1,0:T(8,128)S(1)}, f32[16,32,256]{2,1,0:T(8,128)}, u32[]{:S(2)}) copy-start(f32[16,32,256]{2,1,0:T(8,128)} %param.22) | copy-start | bytes 1572868
  880.9 3.2 collective-permute-start.34
  884.1 8.3 collective-permute-start.35
  894.8 2.1 collective-permute-start.36
  895.9 3.6 collective-permute-start.37
  902.6 6.2 collective-permute-start.38
where the time goes:
time: 925 us; the launch traced here: 915 us
  blocking collectives  671 us (73%)
  waiting for transfers between devices  83.4 us (9%)
  starting transfers between devices  72.1 us (8%)
  other arithmetic  41.8 us (5%)
  local copies, waits for them, and re-layouts  19.5 us (2%)
  between operations  15 us (2%)
  matrix products  12.7 us (1%)
    psum x6, blocking collectives, square_sum(): return lax.psum(jnp.sum(resid * resid), ('ty', 'tx'))  384 us
    psum x4, blocking collectives, on_device(): alpha = norm_now / lax.psum(jnp.sum(direction * image), ('ty', 'tx'))  264 us
    ppermute x20, waiting for transfers between devices, extended_2(): lax.ppermute(tail, axis, [(i, (i + 1) % count) for i in range(count)])  31.6 us
    ppermute x19, waiting for transfers between devices, extended_2(): lax.ppermute(head, axis, [((i + 1) % count, i) for i in range(count)])  28.2 us
    ppermute x19, starting transfers between devices, extended_2(): lax.ppermute(head, axis, [((i + 1) % count, i) for i in range(count)])  27 us
    all_to_all x1, blocking collectives, on_device(): lax.all_to_all(send_sla.reshape(devices, capacity, points), ('ty', 'tx'),...  23.1 us
    ppermute x20, starting transfers between devices, extended_2(): lax.ppermute(tail, axis, [(i, (i + 1) % count) for i in range(count)])  20.8 us
  transfers between devices with their start and end apart: 42, of which 29 were waited for; matrix products, arithmetic and copies ran while one was open for 4% of the time, Pallas kernels for 0%

commit v1 on v0

v1 whole, which is shorter than its diff:
```python
import jax
import jax.numpy as jnp
from jax import lax
from jax.sharding import PartitionSpec as P

AXES = ("ty", "tx")
SHIFT_0 = 1.6
SHIFT_1 = 35.0
SCALE_0 = 1.0 / 32.0
SCALE_1 = 1.0 / 16.0


def beside(cells, axis, step):
    count = lax.axis_size(axis)
    return lax.ppermute(cells, axis, [((i + step) % count, i) for i in range(count)])


def ringed(field, rows, cols):
    north = beside(field[..., :rows, :], "ty", 1)
    south = beside(field[..., -rows:, :], "ty", -1)
    field = jnp.concatenate([field, north, south], axis=-2)
    east = beside(field[..., :cols], "tx", 1)
    west = beside(field[..., -cols:], "tx", -1)
    return jnp.concatenate([field, east, west], axis=-1)


def east(v):
    return jnp.roll(v, -1, axis=-1)


def west(v):
    return jnp.roll(v, 1, axis=-1)


def north(v):
    return jnp.roll(v, -1, axis=-2)


def south(v):
    return jnp.roll(v, 1, axis=-2)


def krylov(apply, start):
    first = apply(start)
    one = SCALE_0 * (first - SHIFT_0 * start)
    second = apply(one)
    two = SCALE_1 * (second - SHIFT_1 * one)
    return (start, one, two), (first, second, apply(two))


def small_solve(g, b):
    d0 = g[0][0]
    l1 = g[1][0] / d0
    l2 = g[2][0] / d0
    d1 = g[1][1] - l1 * g[1][0]
    t = g[2][1] - l1 * g[2][0]
    d1_ok = d1 > 1e-6 * g[1][1]
    m2 = jnp.where(d1_ok, t / d1, 0.0)
    d2 = g[2][2] - l2 * g[2][0] - m2 * t
    y1 = b[1] - l1 * b[0]
    y2 = b[2] - l2 * b[0] - m2 * y1
    x2 = jnp.where(d2 > 1e-6 * g[2][2], y2 / d2, 0.0)
    x1 = jnp.where(d1_ok, y1 / d1, 0.0) - m2 * x2
    x0 = b[0] / d0 - l1 * x1 - l2 * x2
    return (x0, x1, x2)


def pack(obs_sla, obs_weight, obs_tile, obs_start, obs_count, devices, capacity):
    seg_dev, points = obs_sla.shape
    slots = devices * capacity
    target = obs_tile[:, 0]
    tile_hit = target[:, None] == jnp.arange(devices, dtype=jnp.int32)[None, :]
    seg_ids = jnp.arange(seg_dev, dtype=jnp.int32)
    earlier = (seg_ids[None, :] < seg_ids[:, None]).astype(jnp.bfloat16)
    before = jnp.dot(earlier, tile_hit.astype(jnp.bfloat16), preferred_element_type=jnp.float32)
    slot = jnp.sum(jnp.where(tile_hit, before, 0.0), axis=1).astype(jnp.int32)
    where_to = target * capacity + slot
    placed = where_to[None, :] == jnp.arange(slots, dtype=jnp.int32)[:, None]
    lane = jnp.arange(points, dtype=jnp.int32)[None, :]
    weight = jnp.where(lane < obs_count[:, None], obs_weight, 0.0)
    stacked = jnp.concatenate([weight, weight * obs_sla], axis=1)
    packed = jnp.dot(placed.astype(jnp.float32), stacked, precision=lax.Precision.HIGHEST)
    start = jnp.sum(jnp.where(placed, obs_start[None, :], 0), axis=1).astype(jnp.float32)
    packed = packed.reshape(devices, capacity, 2, points).transpose(0, 2, 1, 3)
    start = jnp.pad(start.reshape(devices, 1, capacity), ((0, 0), (0, 0), (0, points - capacity)))
    return jnp.concatenate(
        [packed.reshape(devices, 2 * capacity, points), start], axis=1
    ).reshape(devices, 1, (2 * capacity + 1) * points)


def unpack(got, rows, cols, capacity):
    devices = got.shape[0]
    got = got.reshape(devices, 2 * capacity + 1, -1)
    points = got.shape[2]
    slots = devices * capacity
    start = got[:, 2 * capacity, :capacity].reshape(slots).astype(jnp.int32)
    row_of = start // cols
    col_of = start % cols
    row_pick = (row_of[:, None] == jnp.arange(rows, dtype=jnp.int32)[None, :]).astype(jnp.float32)
    pair = got[:, : 2 * capacity].reshape(devices, 2, capacity, points).transpose(1, 0, 2, 3)
    pair = jnp.pad(pair.reshape(2, slots, points), ((0, 0), (0, 0), (0, cols - points)))
    for bit in range((cols - 1).bit_length()):
        flag = ((col_of >> bit) % 2 == 1)[None, :, None]
        pair = jnp.where(flag, jnp.roll(pair, 1 << bit, axis=2), pair)
    total = jnp.dot(
        row_pick.T,
        pair.transpose(1, 0, 2).reshape(slots, 2 * cols),
        precision=lax.Precision.HIGHEST,
    )
    return total[:, :cols], total[:, cols:]


def on_device(
    lam_tracer,
    lam_eta,
    land,
    zonal_flow,
    merid_flow,
    zonal_mixing,
    merid_mixing,
    surface_east,
    surface_north,
    surface_diag,
    steric,
    eta_saved,
    obs_sla,
    obs_weight,
    obs_tile,
    obs_start,
    obs_count,
):
    levels, rows, cols = lam_tracer.shape
    n_rows = lax.axis_size("ty")
    devices = n_rows * lax.axis_size("tx")
    capacity = 2 * obs_sla.shape[0] // devices
    row_ids = lax.broadcasted_iota(jnp.int32, (rows, 1), 0) + lax.axis_index("ty") * rows
    open_rows = (row_ids < rows * n_rows - 1).astype(jnp.float32)
    merid_flow = merid_flow * open_rows
    merid_mixing = merid_mixing * open_rows
    surface_north = surface_north * open_rows
    ocean = land.astype(jnp.float32)

    sent = pack(obs_sla, obs_weight, obs_tile, obs_start, obs_count, devices, capacity)
    got = lax.all_to_all(sent, AXES, split_axis=0, concat_axis=0, tiled=True)

    faces = ringed(jnp.stack([surface_diag, surface_east, surface_north, ocean]), 6, 6)
    diag, f_east, f_north, ocean_5 = faces[0], faces[1], faces[2], faces[3]
    f_west, f_south = west(f_east), south(f_north)
    centre = (1.0 + diag) + f_east + f_west + f_north + f_south

    def apply(v):
        return centre * v - f_east * east(v) - f_west * west(v) - f_north * north(v) - f_south * south(v)

    half_x, half_y = 0.5 * zonal_flow, 0.5 * merid_flow
    tracers = ringed(
        jnp.concatenate(
            [
                lam_tracer,
                half_x[1] + zonal_mixing,
                half_x[1] - zonal_mixing,
                half_y[1] + merid_mixing,
                half_y[1] - merid_mixing,
                half_x[0] - zonal_mixing,
                half_y[0] - merid_mixing,
            ]
        ),
        2,
        2,
    ).reshape(7, levels, rows + 4, cols + 4)

    weight_sum, value_sum = unpack(got, rows, cols, capacity)
    rhs = ocean * (lam_eta + (weight_sum * eta_saved - value_sum))
    rhs = ringed(rhs, 6, 6)
    w, aw = krylov(apply, rhs)
    y, ay = zip(*[krylov(apply, ocean_5 * v) for v in w])
    inner = lambda a, b: jnp.sum(a[:rows, :cols] * b[:rows, :cols])
    sums = [inner(w[i], aw[j]) for i in range(3) for j in range(i + 1)]
    sums += [inner(w[i], rhs) for i in range(3)]
    pairs = [(i, k) for k in range(3) for i in range(3)]
    sums += [inner(y[i][k], ay[j][l]) for (i, k) in pairs for (j, l) in pairs if l <= k]
    sums += [inner(y[i][k], y[j][0]) for (i, k) in pairs for j in range(3)]
    mine = jnp.pad(jnp.stack(sums), (0, 128 - len(sums)))
    every = lax.all_to_all(
        jnp.broadcast_to(mine, (devices, 1, 128)), AXES, split_axis=0, concat_axis=0, tiled=True
    )
    total = jnp.sum(every.reshape(devices, 128), axis=0)
    at = iter(range(128))
    g1 = [[total[next(at)] for j in range(i + 1)] for i in range(3)]
    b1 = [total[next(at)] for i in range(3)]
    c = small_solve(g1, b1)
    g2 = [[0.0] * 3 for k in range(3)]
    b2 = [0.0] * 3
    for i, k in pairs:
        for j, l in pairs:
            if l <= k:
                g2[k][l] = g2[k][l] + c[i] * c[j] * total[next(at)]
    for i, k in pairs:
        for j in range(3):
            b2[k] = b2[k] + c[i] * c[j] * total[next(at)]
    e = small_solve(g2, b2)
    rho_1 = c[0] * w[0] + c[1] * w[1] + c[2] * w[2]
    v = [c[0] * y[0][k] + c[1] * y[1][k] + c[2] * y[2][k] for k in range(3)]
    rho_0 = e[0] * v[0] + e[1] * v[1] + e[2] * v[2]

    def cut(field):
        field = jnp.concatenate([field[: rows + 2], field[-2:]], axis=0)
        return jnp.concatenate([field[:, : cols + 2], field[:, -2:]], axis=1)

    ocean_2 = cut(ocean_5)

    def step(tracer, rho, plus_x, minus_x, plus_y, minus_y, mask):
        g = mask * (tracer + steric[:, None, None] * rho)
        dx, dy = g - east(g), g - north(g)
        return g - (plus_x * dx + west(minus_x * dx) + plus_y * dy + south(minus_y * dy))

    mu = step(tracers[0], cut(rho_1), *tracers[1:5], ocean_2)
    out_pad = lambda f: jnp.pad(f, ((0, 0), (0, 4), (0, 4)))
    plus_x0 = out_pad(half_x[0] + zonal_mixing)
    plus_y0 = out_pad(half_y[0] + merid_mixing)
    mu = step(mu, cut(rho_0), plus_x0, tracers[5], plus_y0, tracers[6], ocean_2)
    return mu[:, :rows, :cols], rho_0[:rows, :cols]


def solution(mesh):
    in_specs = (
        P(None, "ty", "tx"),
        P("ty", "tx"),
        P("ty", "tx"),
        P(None, None, "ty", "tx"),
        P(None, None, "ty", "tx"),
        P(None, "ty", "tx"),
        P(None, "ty", "tx"),
        P("ty", "tx"),
        P("ty", "tx"),
        P("ty", "tx"),
        P(),
        P("ty", "tx"),
        P(AXES, None),
        P(AXES, None),
        P(AXES, None),
        P(AXES),
        P(AXES),
    )
    out_specs = (P(None, "ty", "tx"), P("ty", "tx"))
    return jax.shard_map(
        on_device, mesh=mesh, in_specs=in_specs, out_specs=out_specs, check_vma=False
    )
```

time: 925 us -> 315 us (0.34)
  blocking collectives: 671 us -> 0 us
  local copies, waits for them, and re-layouts: 19.5 us -> 114 us
  waiting for transfers between devices: 83.4 us -> 15.6 us
  between operations: 15 us -> 64.8 us
  starting transfers between devices: 72.1 us -> 62.6 us
    psum x10 -> x0, blocking collectives: 647 us -> none  [the longest x6 384 us: square_sum(): return lax.psum(jnp.sum(resid * resid), ('ty', 'tx'))]
    another operation x0 -> x1, local copies, waits for them, and re-layouts: none -> 57.8 us  [on_device(): mine = jnp.pad(jnp.stack(sums), (0, 128 - len(sums)))]
    ppermute x39 -> x12, waiting for transfers between devices: 59.8 us -> 11.2 us  [beside(): lax.ppermute(cells, axis, [((i + step) % count, i) for i in range(count)])]
    all_to_all x1 -> x0, blocking collectives: 23.1 us -> none  [on_device(): lax.all_to_all(send_sla.reshape(devices, capacity, points), ('ty', 'tx'),...]
    all_to_all x3 -> x2, waiting for transfers between devices: 23.6 us -> 4.32 us  [the longest x1 4.32 us: on_device(): lax.all_to_all(jnp.broadcast_to(mine, (devices, 1, 128)), AXES, split_axi...]
    ppermute x39 -> x12, starting transfers between devices: 47.9 us -> 32.9 us  [beside(): lax.ppermute(cells, axis, [((i + step) % count, i) for i in range(count)])]
    reshape x2 -> x4, local copies, waits for them, and re-layouts: 0.16 us -> 11.9 us  [the longest x1 5.83 us: pack(): return jnp.concatenate([packed.reshape(devices, 2 * capacity, points), st...]
    slice x25 -> x91, local copies, waits for them, and re-layouts: 12.8 us -> 20.6 us  [the longest x4 5 us: ringed(): east = beside(field[..., :cols], 'tx', 1)]
  transfers between devices with their start and end apart: 42 -> 14, of which waited for: 29 -> 5; matrix products, arithmetic and copies ran while one was open for 4% -> 7% of each run, Pallas kernels for 0% -> 0%
where the time goes in v1:
time: 315 us; the launch traced here: 311 us
  local copies, waits for them, and re-layouts  114 us (36%)
  between operations  64.8 us (21%)
  starting transfers between devices  62.6 us (20%)
  other arithmetic  43.5 us (14%)
  waiting for transfers between devices  15.6 us (5%)
  matrix products  11.3 us (4%)
    another operation x1, local copies, waits for them, and re-layouts, on_device(): mine = jnp.pad(jnp.stack(sums), (0, 128 - len(sums)))  57.8 us
    ppermute x12, starting transfers between devices, beside(): lax.ppermute(cells, axis, [((i + step) % count, i) for i in range(count)])  32.9 us
    all_to_all x1, starting transfers between devices, on_device(): got = lax.all_to_all(sent, AXES, split_axis=0, concat_axis=0, tiled=True)  23 us
    select_n x7, other arithmetic, unpack(): pair = jnp.where(flag, jnp.roll(pair, 1 << bit, axis=2), pair)  12.2 us
    ppermute x12, waiting for transfers between devices, beside(): lax.ppermute(cells, axis, [((i + step) % count, i) for i in range(count)])  11.2 us
    all_to_all x1, starting transfers between devices, on_device(): lax.all_to_all(jnp.broadcast_to(mine, (devices, 1, 128)), AXES, split_axi...  6.69 us
  transfers between devices with their start and end apart: 14, of which 5 were waited for; matrix products, arithmetic and copies ran while one was open for 7% of the time, Pallas kernels for 0%

profile of v1, /device:TPU:1, one launch (start us, length us, event | category | flops | bytes accessed | tf_op | source)
XLA Modules:
  0.0 311.3 jit_solution(9852680411409597897)
XLA Ops:
  0.6 1.4 fusion.5
  2.0 0.7 convert_add_fusion
  2.7 1.2 copy.86
  4.0 1.2 copy.87
  5.4 5.3 %fusion = f32[2048,256]{1,0:T(8,128)} fusion(s32[1024]{0:T(1024)S(1)} %convert_add_fusion, f32[1024,128]{0,1:T(8,128)S(1)} %get-tuple-element.125, f32[1024,128]{0,1:T(8,128)S(1)} %get-tuple-element.126), kind=kOutput, calls=%fused_computation.2 | convolution fusion | flops 6444810240 | bytes 3149824 | tf_op jit(solution)/shard_map/dot_general | solution.py:82
  10.7 2.3 reshape.258
  13.0 1.5 copy.88
  14.5 0.9 select_reduce_fusion
  15.6 1.8 select_maximum_fusion
  17.4 2.0 copy.90
  19.4 5.8 %copy.91 = f32[128,1,4224]{2,1,0:T(1,128)} copy(f32[128,1,4224]{0,2,1:T(8,128)} %bitcast.328) | data formatting | bytes 4325376 | tf_op jit(solution)/shard_map/reshape | solution.py:88
  25.3 23.0 %all-to-all-start = ((f32[128,1,4224]{2,1,0:T(1,128)}), f32[128,1,4224]{2,1,0:T(1,128)}, u32[]{:S(2)}, u32[]{:S(2)}) async-start(f32[128,1,4224]{2,1,0:T(1,128)} %copy.91), calls=%async_computation | async-start | bytes 4325376 | tf_op jit(solution)/shard_map/all_to_all | solution.py:144
  48.5 1.2 collective-permute-start
  51.0 0.7 copy_multiply_fusion.1
  53.0 1.1 fusion.26
  54.8 2.6 collective-permute-done
  57.5 20.8 %collective-permute-start.2 = (f32[4,44,6]{2,1,0:T(8,128)S(1)}, f32[4,44,6]{2,1,0:T(8,128)S(1)}, u32[]{:S(2)}, u32[]{:S(2)}) collective-permute-start(f32[4,44,6]{2,1,0:T(8,128)S(1)} %get-tuple-element.172), channel_id=1, source_target_pairs={{1,0},{2,1},{3,2},{4,3},{5,4},{6,5},{7,6},{8,7},{9,8},{10,9},{11,1... | collective-permute-start | bytes 12680 | tf_op jit(solution)/shard_map/ppermute | solution.py:15
  78.4 1.7 collective-permute-start.5
  80.6 5.7 %collective-permute-done.3 = f32[4,44,6]{2,1,0:T(8,128)S(1)} collective-permute-done((f32[4,44,6]{2,1,0:T(8,128)S(1)}, f32[4,44,6]{2,1,0:T(8,128)S(1)}, u32[]{:S(2)}, u32[]{:S(2)}) %collective-permute-start.3) | collective-permute-done | bytes 4256 | tf_op jit(solution)/shard_map/ppermute | solution.py:15
  87.7 0.7 copy-done.12
  88.4 2.2 pad_maximum_fusion.1
  90.7 5.7 %copy.92 = f32[128,1,4224]{0,2,1:T(8,128)} copy(f32[128,1,4224]{2,1,0:T(1,128)} %all-to-all-done) | data formatting | bytes 4325376 | tf_op jit(solution)/shard_map/all_to_all | solution.py:144
  96.3 0.7 slice_convert_fusion
  97.0 3.2 %slice.1380 = f32[128,32,128]{0,2,1:T(8,128)} slice(f32[128,33,128]{0,2,1:T(8,128)} %bitcast.330), slice={[0:128], [0:32], [0:128]} | slice | bytes 4194304 | tf_op jit(solution)/shard_map/slice | solution.py:100
  100.5 2.2 copy.94
  103.0 1.6 pad_select_fusion
  105.2 1.8 maximum_select_fusion
  107.6 1.8 maximum_select_fusion.1
  110.0 1.8 maximum_select_fusion.2
  112.3 1.8 maximum_select_fusion.3
  114.7 1.8 maximum_select_fusion.4
  117.1 1.8 maximum_select_fusion.5
  119.1 2.2 fusion.1
  121.4 5.4 %copy.95 = f32[2048,2,256]{0,2,1:T(8,128)} copy(f32[2048,2,256]{2,0,1:T(8,128)} %fusion.1) | data formatting | bytes 8388608 | tf_op jit(solution)/shard_map/transpose | solution.py:107
  126.8 4.6 %fusion.18 = f32[32,512]{1,0:T(8,128)S(1)} fusion(f32[2048,512]{0,1:T(8,128)} %bitcast.327, s32[2048]{0:T(1024)S(1)} %add_select_fusion.9), kind=kOutput, calls=%fused_computation.48 | convolution fusion | flops 402784256 | bytes 4268032 | tf_op jit(solution)/shard_map/dot_general | solution.py:105
  131.9 1.4 collective-permute-start.9
  133.2 2.0 fusion.150
  135.2 2.2 copy.82
  137.4 1.9 collective-permute-start.6
  140.8 4.8 %collective-permute-start.10 = (f32[44,6]{1,0:T(8,128)}, f32[44,6]{1,0:T(8,128)S(1)}, u32[]{:S(2)}, u32[]{:S(2)}) collective-permute-start(f32[44,6]{1,0:T(8,128)} %get-tuple-element.273), channel_id=1, source_target_pairs={{1,0},{2,1},{3,2},{4,3},{5,4},{6,5},{7,6},{8,7},{9,8},{10,9},{11,1... | collective-permute-start | bytes 3176 | tf_op jit(solution)/shard_map/ppermute | solution.py:15
  145.6 0.7 fusion.74
  147.0 2.0 copy.85
  149.6 2.6 collective-permute-done.11
  152.1 0.8 fusion.71
  155.9 0.8 multiply_reduce_fusion.5
  156.9 0.8 multiply_reduce_fusion.12
  157.7 0.8 multiply_reduce_fusion.10
  158.5 0.7 multiply_reduce_fusion.14
  159.2 0.8 multiply_reduce_fusion.13
  160.0 0.8 multiply_reduce_fusion.78
  160.8 57.8 %stack.374 = f32[90]{0:T(128)S(1)} concatenate(f32[1]{0:T(128)} %bitcast.26, f32[1]{0:T(128)} %bitcast.27, f32[1]{0:T(128)} %bitcast.28, f32[1]{0:T(128)} %bitcast.29, f32[1]{0:T(128)} %bitcast.30, f32[1]{0:T(128)} %bitcast.31, f32[1]{0:T(128)} %bitcast.32, f32[1]{0:T(128)} %bitcast.33, f32[1]{0:T(128)} %bitcast.34, f32[1]{0:T(128)} %bitcast.36, f32[1]{0:T(128)} %bitcast.37, ...), dimensions={0} | concatenate | bytes 720 | tf_op jit(solution)/shard_map/stack | solution.py:182
  219.2 6.7 %all-to-all-start.1 = ((f32[128,1,128]{2,1,0:T(1,128)}), f32[128,1,128]{2,1,0:T(1,128)}, u32[]{:S(2)}, u32[]{:S(2)}) async-start(f32[128,1,128]{2,1,0:T(1,128)} %broadcast_in_dim.100), calls=%async_computation.1 | async-start | bytes 131072 | tf_op jit(solution)/shard_map/all_to_all | solution.py:183
  226.0 5.2 %pad_maximum_fusion = f32[112,36,260]{2,0,1:T(8,128)} fusion(f32[112,36,2]{2,0,1:T(8,128)} %copy.85, f32[112,36,2]{2,0,1:T(8,128)S(1)} %copy.84, f32[112,2,256]{2,0,1:T(8,128)} %copy-done.12, f32[112,2,256]{2,0,1:T(8,128)} %copy-done.11, f32[112,32,256]{2,0,1:T(8,128)} %copy-done.1), kind=kLoop, calls=%fused_computation.3 | loop fusion | flops 4193280 | bytes 8386560 | tf_op jit(solution)/shard_map/concatenate | solution.py:24
  231.2 4.3 %all-to-all-done.1 = f32[128,1,128]{2,1,0:T(1,128)} async-done(((f32[128,1,128]{2,1,0:T(1,128)}), f32[128,1,128]{2,1,0:T(1,128)}, u32[]{:S(2)}, u32[]{:S(2)}) %all-to-all-start.1) | async-done | bytes 65568 | tf_op jit(solution)/shard_map/all_to_all | solution.py:183
  235.5 0.9 reduce_sum.911
  236.4 0.7 fusion.206
  242.7 0.7 fusion.205
  249.3 0.7 fusion.204
  250.1 0.7 fusion.202
  250.8 0.7 fusion.203
  302.9 1.1 multiply_add_fusion.1
  304.1 1.7 fusion.17
  307.0 0.8 fusion.15
  309.8 1.1 copy.98
  (210 shorter events, 20.1 us)
Async XLA Ops:
  0.6 4.6 %copy-start.32 = (s32[1024]{0:T(1024)S(1)}, s32[1024]{0:T(1024)}, u32[]{:S(2)}) copy-start(s32[1024]{0:T(1024)} %param.33) | copy-start | bytes 12292
  10.7 3.8 %copy-start.33 = (s32[1024]{0:T(1024)S(1)}, s32[1024]{0:T(1024)}, u32[]{:S(2)}) copy-start(s32[1024]{0:T(1024)} %param.32) | copy-start | bytes 12292
  19.4 28.9 %copy-start.26 = (s32[32,256]{1,0:T(8,128)S(1)}, s32[32,256]{1,0:T(8,128)}, u32[]{:S(2)}) copy-start(s32[32,256]{1,0:T(8,128)} %param.19) | copy-start | bytes 98308
  19.4 28.9 %copy-start.27 = (f32[32,256]{1,0:T(8,128)S(1)}, f32[32,256]{1,0:T(8,128)}, u32[]{:S(2)}) copy-start(f32[32,256]{1,0:T(8,128)} %param.25) | copy-start | bytes 98308
  19.4 29.0 %copy-start.24 = (f32[32,256]{1,0:T(8,128)S(1)}, f32[32,256]{1,0:T(8,128)}, u32[]{:S(2)}) copy-start(f32[32,256]{1,0:T(8,128)} %param.24) | copy-start | bytes 98308
  19.4 29.0 %copy-start.25 = (f32[32,256]{1,0:T(8,128)S(1)}, f32[32,256]{1,0:T(8,128)}, u32[]{:S(2)}) copy-start(f32[32,256]{1,0:T(8,128)} %param.26) | copy-start | bytes 98308
  19.4 30.8 %copy-start.8 = (f32[2,16,32,256]{3,2,1,0:T(8,128)S(1)}, f32[2,16,32,256]{3,2,1,0:T(8,128)}, u32[]{:S(2)}) copy-start(f32[2,16,32,256]{3,2,1,0:T(8,128)} %param.21) | copy-start | bytes 3145732
  25.3 25.7 %copy-start.9 = (f32[2,16,32,256]{3,2,1,0:T(8,128)S(1)}, f32[2,16,32,256]{3,2,1,0:T(8,128)}, u32[]{:S(2)}) copy-start(f32[2,16,32,256]{3,2,1,0:T(8,128)} %param.20) | copy-start | bytes 3145732
  25.3 26.4 %copy-start.19 = (f32[16,32,256]{2,1,0:T(8,128)S(1)}, f32[16,32,256]{2,1,0:T(8,128)}, u32[]{:S(2)}) copy-start(f32[16,32,256]{2,1,0:T(8,128)} %param.17) | copy-start | bytes 1572868
  25.3 26.7 %copy-start.3 = (f32[16,32,256]{2,1,0:T(8,128)S(1)}, f32[16,32,256]{2,1,0:T(8,128)}, u32[]{:S(2)}) copy-start(f32[16,32,256]{2,1,0:T(8,128)} %param.22) | copy-start | bytes 1572868
  25.3 65.4 %all-to-all-start = ((f32[128,1,4224]{2,1,0:T(1,128)}), f32[128,1,4224]{2,1,0:T(1,128)}, u32[]{:S(2)}, u32[]{:S(2)}) async-start(f32[128,1,4224]{2,1,0:T(1,128)} %copy.91), calls=%async_computation | async-start | bytes 4325376 | tf_op jit(solution)/shard_map/all_to_all | solution.py:144
  48.5 8.9 %collective-permute-start = (f32[4,6,256]{2,1,0:T(8,128)S(1)}, f32[4,6,256]{2,1,0:T(8,128)S(1)}, u32[]{:S(2)}, u32[]{:S(2)}) collective-permute-start(f32[4,6,256]{2,1,0:T(8,128)S(1)} %get-tuple-element.175), channel_id=1, source_target_pairs={{16,0},{32,16},{48,32},{64,48},{80,64},{96,80},{112,96},{0,112},{1... | collective-permute-start | bytes 73736 | tf_op jit(solution)/shard_map/ppermute | solution.py:15
  49.7 7.7 %collective-permute-start.1 = (f32[4,6,256]{2,1,0:T(8,128)S(1)}, f32[4,6,256]{2,1,0:T(8,128)S(1)}, u32[]{:S(2)}, u32[]{:S(2)}) collective-permute-start(f32[4,6,256]{2,1,0:T(8,128)S(1)} %get-tuple-element.176), channel_id=1, source_target_pairs={{112,0},{0,16},{16,32},{32,48},{48,64},{64,80},{80,96},{96,112},{1... | collective-permute-start | bytes 73736 | tf_op jit(solution)/shard_map/ppermute | solution.py:15
  51.0 1.7 copy-start.4
  54.8 32.3 %copy-start.1 = (f32[112,32,256]{2,0,1:T(8,128)}, f32[112,32,256]{2,0,1:T(8,128)S(1)}, u32[]{:S(2)}) copy-start(f32[112,32,256]{2,0,1:T(8,128)S(1)} %subtract_dynamic-update-slice_fusion) | copy-start | bytes 11010052
  57.5 23.1 %collective-permute-start.2 = (f32[4,44,6]{2,1,0:T(8,128)S(1)}, f32[4,44,6]{2,1,0:T(8,128)S(1)}, u32[]{:S(2)}, u32[]{:S(2)}) collective-permute-start(f32[4,44,6]{2,1,0:T(8,128)S(1)} %get-tuple-element.172), channel_id=1, source_target_pairs={{1,0},{2,1},{3,2},{4,3},{5,4},{6,5},{7,6},{8,7},{9,8},{10,9},{11,1... | collective-permute-start | bytes 12680 | tf_op jit(solution)/shard_map/ppermute | solution.py:15
  78.3 7.9 %collective-permute-start.3 = (f32[4,44,6]{2,1,0:T(8,128)S(1)}, f32[4,44,6]{2,1,0:T(8,128)S(1)}, u32[]{:S(2)}, u32[]{:S(2)}) collective-permute-start(f32[4,44,6]{2,1,0:T(8,128)S(1)} %get-tuple-element.173), channel_id=1, source_target_pairs={{15,0},{0,1},{1,2},{2,3},{3,4},{4,5},{5,6},{6,7},{7,8},{8,9},{9,10... | collective-permute-start | bytes 12680 | tf_op jit(solution)/shard_map/ppermute | solution.py:15
  78.4 8.7 %collective-permute-start.4 = (f32[112,2,256]{2,0,1:T(8,128)S(1)}, f32[112,2,256]{2,0,1:T(8,128)S(1)}, u32[]{:S(2)}, u32[]{:S(2)}) collective-permute-start(f32[112,2,256]{2,0,1:T(8,128)S(1)} %get-tuple-element.135), channel_id=1, source_target_pairs={{16,0},{32,16},{48,32},{64,48},{80,64},{96,80},{112,96},{0,112},{1... | collective-permute-start | bytes 688136 | tf_op jit(solution)/shard_map/ppermute | solution.py:15
  78.4 8.7 %collective-permute-start.5 = (f32[112,2,256]{2,0,1:T(8,128)S(1)}, f32[112,2,256]{2,0,1:T(8,128)S(1)}, u32[]{:S(2)}, u32[]{:S(2)}) collective-permute-start(f32[112,2,256]{2,0,1:T(8,128)S(1)} %get-tuple-element.136), channel_id=1, source_target_pairs={{112,0},{0,16},{16,32},{32,48},{48,64},{64,80},{80,96},{96,112},{1... | collective-permute-start | bytes 688136 | tf_op jit(solution)/shard_map/ppermute | solution.py:15
  87.1 0.7 copy-start.11
  87.7 0.7 copy-start.12
  126.8 4.6 %copy-start.28 = (f32[32,256]{1,0:T(8,128)S(1)}, f32[32,256]{1,0:T(8,128)}, u32[]{:S(2)}) copy-start(f32[32,256]{1,0:T(8,128)} %param.18) | copy-start | bytes 98308
  126.8 4.6 %copy-start.29 = (f32[32,256]{1,0:T(8,128)S(1)}, f32[32,256]{1,0:T(8,128)}, u32[]{:S(2)}) copy-start(f32[32,256]{1,0:T(8,128)} %param.28) | copy-start | bytes 98308
  126.8 6.4 %copy-start.2 = (f32[112,36,256]{2,0,1:T(8,128)S(1)}, f32[112,36,256]{2,0,1:T(8,128)}, u32[]{:S(2)}) copy-start(f32[112,36,256]{2,0,1:T(8,128)} %pad_maximum_fusion.1) | copy-start | bytes 12386308
  131.4 8.6 %collective-permute-start.8 = (f32[6,256]{1,0:T(8,128)S(1)}, f32[6,256]{1,0:T(8,128)S(1)}, u32[]{:S(2)}, u32[]{:S(2)}) collective-permute-start(f32[6,256]{1,0:T(8,128)S(1)} %get-tuple-element.275), channel_id=1, source_target_pairs={{16,0},{32,16},{48,32},{64,48},{80,64},{96,80},{112,96},{0,112},{1... | collective-permute-start | bytes 18440 | tf_op jit(solution)/shard_map/ppermute | solution.py:15
  131.9 8.2 %collective-permute-start.9 = (f32[6,256]{1,0:T(8,128)S(1)}, f32[6,256]{1,0:T(8,128)S(1)}, u32[]{:S(2)}, u32[]{:S(2)}) collective-permute-start(f32[6,256]{1,0:T(8,128)S(1)} %get-tuple-element.276), channel_id=1, source_target_pairs={{112,0},{0,16},{16,32},{32,48},{48,64},{64,80},{80,96},{96,112},{1... | collective-permute-start | bytes 18440 | tf_op jit(solution)/shard_map/ppermute | solution.py:15
  137.4 8.9 %collective-permute-start.6 = (f32[112,36,2]{0,1,2:T(8,128)S(1)}, f32[112,36,2]{0,1,2:T(8,128)S(1)}, u32[]{:S(2)}, u32[]{:S(2)}) collective-permute-start(f32[112,36,2]{0,1,2:T(8,128)S(1)} %copy.82), channel_id=1, source_target_pairs={{1,0},{2,1},{3,2},{4,3},{5,4},{6,5},{7,6},{8,7},{9,8},{10,9},{11,1... | collective-permute-start | bytes 96776 | tf_op jit(solution)/shard_map/ppermute | solution.py:15
  140.0 7.0 %collective-permute-start.7 = (f32[112,36,2]{0,1,2:T(8,128)S(1)}, f32[112,36,2]{0,1,2:T(8,128)S(1)}, u32[]{:S(2)}, u32[]{:S(2)}) collective-permute-start(f32[112,36,2]{0,1,2:T(8,128)S(1)} %copy.83), channel_id=1, source_target_pairs={{15,0},{0,1},{1,2},{2,3},{3,4},{4,5},{5,6},{6,7},{7,8},{8,9},{9,10... | collective-permute-start | bytes 96776 | tf_op jit(solution)/shard_map/ppermute | solution.py:15
  140.8 8.2 %collective-permute-start.10 = (f32[44,6]{1,0:T(8,128)}, f32[44,6]{1,0:T(8,128)S(1)}, u32[]{:S(2)}, u32[]{:S(2)}) collective-permute-start(f32[44,6]{1,0:T(8,128)} %get-tuple-element.273), channel_id=1, source_target_pairs={{1,0},{2,1},{3,2},{4,3},{5,4},{6,5},{7,6},{8,7},{9,8},{10,9},{11,1... | collective-permute-start | bytes 3176 | tf_op jit(solution)/shard_map/ppermute | solution.py:15
  145.6 6.6 %collective-permute-start.11 = (f32[44,6]{1,0:T(8,128)}, f32[44,6]{1,0:T(8,128)S(1)}, u32[]{:S(2)}, u32[]{:S(2)}) collective-permute-start(f32[44,6]{1,0:T(8,128)} %get-tuple-element.274), channel_id=1, source_target_pairs={{15,0},{0,1},{1,2},{2,3},{3,4},{4,5},{5,6},{6,7},{7,8},{8,9},{9,10... | collective-permute-start | bytes 3176 | tf_op jit(solution)/shard_map/ppermute | solution.py:15
  149.0 0.6 copy-start.30
  153.4 6.6 %copy-start.13 = (f32[44,268]{1,0:T(8,128)}, f32[44,268]{1,0:T(8,128)S(1)}, u32[]{:S(2)}) copy-start(f32[44,268]{1,0:T(8,128)S(1)} %get-tuple-element.114) | copy-start | bytes 141508
  153.8 5.4 %copy-start.17 = (f32[44,268]{1,0:T(8,128)}, f32[44,268]{1,0:T(8,128)S(1)}, u32[]{:S(2)}) copy-start(f32[44,268]{1,0:T(8,128)S(1)} %get-tuple-element.118) | copy-start | bytes 141508
  154.3 5.7 %copy-start.22 = (f32[44,268]{1,0:T(8,128)}, f32[44,268]{1,0:T(8,128)S(1)}, u32[]{:S(2)}) copy-start(f32[44,268]{1,0:T(8,128)S(1)} %get-tuple-element.107) | copy-start | bytes 141508
  154.5 2.4 copy-start.23
  154.9 5.0 %copy-start.15 = (f32[44,268]{1,0:T(8,128)}, f32[44,268]{1,0:T(8,128)S(1)}, u32[]{:S(2)}) copy-start(f32[44,268]{1,0:T(8,128)S(1)} %get-tuple-element.102) | copy-start | bytes 141508
  155.4 5.3 %copy-start.6 = (f32[44,268]{1,0:T(8,128)}, f32[44,268]{1,0:T(8,128)S(1)}, u32[]{:S(2)}) copy-start(f32[44,268]{1,0:T(8,128)S(1)} %get-tuple-element.111) | copy-start | bytes 141508
  155.8 5.0 %copy-start.20 = (f32[44,268]{1,0:T(8,128)}, f32[44,268]{1,0:T(8,128)S(1)}, u32[]{:S(2)}) copy-start(f32[44,268]{1,0:T(8,128)S(1)} %get-tuple-element.109) | copy-start | bytes 141508
  219.2 16.3 %all-to-all-start.1 = ((f32[128,1,128]{2,1,0:T(1,128)}), f32[128,1,128]{2,1,0:T(1,128)}, u32[]{:S(2)}, u32[]{:S(2)}) async-start(f32[128,1,128]{2,1,0:T(1,128)} %broadcast_in_dim.100), calls=%async_computation.1 | async-start | bytes 131072 | tf_op jit(solution)/shard_map/all_to_all | solution.py:183
  225.9 76.8 %copy-start.7 = (f32[44,268]{1,0:T(8,128)S(1)}, f32[44,268]{1,0:T(8,128)}, u32[]{:S(2)}) copy-start(f32[44,268]{1,0:T(8,128)} %copy-done.6) | copy-start | bytes 141508
  226.0 76.8 %copy-start.16 = (f32[44,268]{1,0:T(8,128)S(1)}, f32[44,268]{1,0:T(8,128)}, u32[]{:S(2)}) copy-start(f32[44,268]{1,0:T(8,128)} %copy-done.15) | copy-start | bytes 141508
  226.0 76.8 %copy-start.18 = (f32[44,268]{1,0:T(8,128)S(1)}, f32[44,268]{1,0:T(8,128)}, u32[]{:S(2)}) copy-start(f32[44,268]{1,0:T(8,128)} %copy-done.17) | copy-start | bytes 141508
  226.0 76.8 %copy-start.21 = (f32[44,268]{1,0:T(8,128)S(1)}, f32[44,268]{1,0:T(8,128)}, u32[]{:S(2)}) copy-start(f32[44,268]{1,0:T(8,128)} %copy-done.20) | copy-start | bytes 141508
  226.0 76.9 %copy-start.14 = (f32[44,268]{1,0:T(8,128)S(1)}, f32[44,268]{1,0:T(8,128)}, u32[]{:S(2)}) copy-start(f32[44,268]{1,0:T(8,128)} %copy-done.13) | copy-start | bytes 141508
  226.0 78.1 %copy-start.10 = (f32[36,260]{1,0:T(8,128)S(1)}, f32[36,260]{1,0:T(8,128)}, u32[]{:S(2)}) copy-start(f32[36,260]{1,0:T(8,128)} %fusion.74) | copy-start | bytes 112324
  226.0 78.1 %copy-start.31 = (f32[16]{0:T(128)S(1)}, f32[16]{0:T(128)}, u32[]{:S(2)}) copy-start(f32[16]{0:T(128)} %param.27) | copy-start | bytes 196
  302.7 3.5 %copy-start = (f32[112,36,260]{2,0,1:T(8,128)S(1)}, f32[112,36,260]{2,0,1:T(8,128)}, u32[]{:S(2)}) copy-start(f32[112,36,260]{2,0,1:T(8,128)} %pad_maximum_fusion) | copy-start | bytes 12579844
  308.2 1.2 copy-start.5

commit v2 on v1

v2 whole, which is shorter than its diff:
```python
import functools

import jax
import jax.numpy as jnp
from jax import lax
from jax.experimental import pallas as pl
from jax.experimental.pallas import tpu as pltpu
from jax.sharding import PartitionSpec as P

AXES = ("ty", "tx")
SHIFT_0 = 1.6
SHIFT_1 = 35.0
SCALE_0 = 1.0 / 32.0
SCALE_1 = 1.0 / 16.0
LANES = 128
VMEM = pl.BlockSpec(memory_space=pltpu.VMEM)
F32 = jnp.float32
BF16 = jnp.bfloat16
PARAMS = pltpu.CompilerParams(vmem_limit_bytes=40 * 1024 * 1024)


def iota(shape, axis):
    return lax.broadcasted_iota(jnp.int32, shape, axis)


def split(x):
    hi = x.astype(BF16)
    return hi, (x - hi.astype(F32)).astype(BF16)


def pack_kernel(capacity, sla_ref, weight_ref, tile_ref, start_ref, count_ref, out_ref, data_ref):
    blocks = tile_ref.shape[0]
    devices = LANES
    chunk = 2 * capacity + 1
    square = (LANES, LANES)
    sub, lane = iota(square, 0), iota(square, 1)
    prefix = jnp.concatenate([(sub < lane).astype(BF16), jnp.ones(square, BF16)], axis=1)
    tile, start, count = tile_ref[...], start_ref[...], count_ref[...]
    col_t = jnp.transpose((start & (LANES - 1)).astype(F32)).astype(jnp.int32)
    count_t = jnp.transpose(count.astype(F32)).astype(jnp.int32)
    carry = jnp.zeros(square, F32)
    places, hits, firsts, lasts = [], [], [], []
    for k in range(blocks):
        target = tile[k : k + 1]
        hit = sub == target
        hits.append(hit.astype(F32).astype(BF16))
        both = jnp.dot(hits[-1], prefix, preferred_element_type=F32)
        slot = jnp.sum(jnp.where(hit, both[:, :LANES] + carry, 0.0), axis=0, keepdims=True)
        carry = carry + both[:, LANES:]
        slot = slot.astype(jnp.int32)
        places.append(target * capacity + slot)
        begin = start[k : k + 1]
        block_of = jnp.where(sub == slot, begin // LANES, 0)
        lane_of = jnp.where(sub == slot + 64, begin & (LANES - 1), 0)
        firsts.append((block_of + lane_of).astype(F32).astype(BF16))
        rows = slice(k * LANES, (k + 1) * LANES)
        weight = jnp.where(lane < count_t[:, k : k + 1], weight_ref[rows, :], 0.0)
        value = weight * sla_ref[rows, :]
        index = (lane - col_t[:, k : k + 1]) & (LANES - 1)
        weight = jnp.take_along_axis(weight, index, axis=1)
        value = jnp.take_along_axis(value, index, axis=1)
        data_ref[rows, :] = jnp.concatenate([*split(weight), *split(value)], axis=1)
    place = jnp.concatenate(places, axis=1)
    meta = lax.dot_general(
        jnp.concatenate(hits, axis=1),
        jnp.concatenate(firsts, axis=1),
        (((1,), (1,)), ((), ())),
        preferred_element_type=F32,
    )
    out_ref[pl.ds(2 * capacity, devices, stride=chunk), :] = meta
    group = 16
    height = group * capacity
    slots = iota((height, blocks * LANES), 0)
    for g in range(devices // group):
        pick = (slots == place - g * height).astype(F32).astype(BF16)
        moved = jnp.dot(pick, data_ref[...], preferred_element_type=F32)
        weight = moved[:, :LANES] + moved[:, LANES : 2 * LANES]
        value = moved[:, 2 * LANES : 3 * LANES] + moved[:, 3 * LANES :]
        for t in range(group):
            base = (g * group + t) * chunk
            rows = slice(t * capacity, (t + 1) * capacity)
            out_ref[base : base + capacity, :] = weight[rows]
            out_ref[base + capacity : base + 2 * capacity, :] = value[rows]


def pack(obs_sla, obs_weight, obs_tile, obs_start, obs_count, capacity):
    blocks = obs_sla.shape[0] // LANES
    chunk = 2 * capacity + 1
    return pl.pallas_call(
        functools.partial(pack_kernel, capacity),
        out_shape=jax.ShapeDtypeStruct((LANES * chunk, LANES), F32),
        in_specs=[VMEM] * 5,
        out_specs=VMEM,
        scratch_shapes=[pltpu.VMEM((blocks * LANES, 4 * LANES), BF16)],
        compiler_params=PARAMS,
        name="pack_segments",
    )(
        obs_sla,
        obs_weight,
        obs_tile.reshape(blocks, LANES),
        obs_start.reshape(blocks, LANES),
        obs_count.reshape(blocks, LANES),
    )


def unpack_kernel(capacity, got_ref, eta_ref, lam_ref, land_ref, q_ref, sum_ref):
    chunk = 2 * capacity + 1
    square = (LANES, LANES)
    lane = iota(square, 1)
    meta = got_ref[pl.ds(2 * capacity, LANES, stride=chunk), :]
    meta_t = jnp.transpose(meta)
    rows, cols = q_ref.shape
    cells = rows * cols // LANES
    blocks = iota((cells, LANES), 0).astype(F32)
    lane_f = lane.astype(F32)
    acc = jnp.zeros((cells, 4 * LANES), F32)
    for j in range(capacity):
        weight = got_ref[pl.ds(j, LANES, stride=chunk), :]
        value = got_ref[pl.ds(capacity + j, LANES, stride=chunk), :]
        here = lane_f >= meta[:, 64 + j : 65 + j]
        hit = (blocks == meta_t[j : j + 1]).astype(F32).astype(BF16)
        his, los = [], []
        for x in (weight, value):
            hi = x.astype(BF16).astype(F32)
            lo = x - hi
            for keep in (here, ~here):
                his.append(jnp.where(keep, hi, 0.0).astype(BF16))
                los.append(jnp.where(keep, lo, 0.0).astype(BF16))
        data = jnp.concatenate(
            [jnp.concatenate(his, axis=1), jnp.concatenate(los, axis=1)], axis=0
        )
        acc = acc + jnp.dot(
            jnp.concatenate([hit, hit], axis=1), data, preferred_element_type=F32
        )
    for i in range(2):
        here, after = acc[:, 2 * i * LANES : (2 * i + 1) * LANES], acc[:, (2 * i + 1) * LANES : (2 * i + 2) * LANES]
        sum_ref[i, :, :] = here + pltpu.roll(after, 1, 0)
    for half in range(2):
        at = slice(half * LANES, (half + 1) * LANES)
        weight = sum_ref[0, pl.ds(half, rows, stride=2), :]
        value = sum_ref[1, pl.ds(half, rows, stride=2), :]
        mu = lam_ref[:, at] + (weight * eta_ref[:, at] - value)
        q_ref[:, at] = land_ref[:, at].astype(F32) * mu


def unpack(got, eta, lam, land, capacity):
    return pl.pallas_call(
        functools.partial(unpack_kernel, capacity),
        out_shape=jax.ShapeDtypeStruct(eta.shape, F32),
        in_specs=[VMEM] * 4,
        out_specs=VMEM,
        scratch_shapes=[pltpu.VMEM((2, eta.size // LANES, LANES), F32)],
        compiler_params=PARAMS,
        name="forcing",
    )(got, eta, lam, land)


def two_sum(a, b):
    s = a + b
    t = s - a
    return s, (a - (s - t)) + (b - t)


def pair_sum(x, y):
    s, e = two_sum(x[0], y[0])
    e = e + (x[1] + y[1])
    return s, e


def tree(parts):
    while len(parts) > 1:
        odd = parts[len(parts) // 2 * 2 :]
        parts = [pair_sum(parts[i], parts[i + 1]) for i in range(0, len(parts) - 1, 2)] + odd
    return parts[0]


def rows_sum(hi):
    zero = jnp.zeros((8, LANES), F32)
    total = tree([(hi[8 * i : 8 * i + 8], zero) for i in range(16)])
    for step in (4, 2, 1):
        total = pair_sum(total, (pltpu.roll(total[0], step, 0), pltpu.roll(total[1], step, 0)))
    return total


def krylov(apply, start):
    first = apply(start)
    one = SCALE_0 * (first - SHIFT_0 * start)
    second = apply(one)
    two = SCALE_1 * (second - SHIFT_1 * one)
    return (start, one, two), (first, second, apply(two))


def sums_kernel(q_ref, north_ref, south_ref, east_ref, west_ref, face_ref, row_ref, field_ref, part_ref):
    rows, cols = q_ref.shape
    high, wide = rows + 16, cols + LANES
    side = jnp.where(iota((high, LANES), 1) < LANES // 2, east_ref[...], west_ref[...])
    q = jnp.concatenate(
        [jnp.concatenate([q_ref[...], north_ref[...], south_ref[...]], axis=0), side], axis=1
    )

    def apply(v):
        return (
            face_ref[0] * v
            - face_ref[1] * pltpu.roll(v, wide - 1, 1)
            - face_ref[2] * pltpu.roll(v, 1, 1)
            - face_ref[3] * pltpu.roll(v, high - 1, 0)
            - face_ref[4] * pltpu.roll(v, 1, 0)
        )

    def inner(at, a, b):
        p = a[:rows, :cols] * b[:rows, :cols]
        p = (p[0:8] + p[8:16]) + (p[16:24] + p[24:32])
        part_ref[8 * at : 8 * at + 8, :] = p[:, :LANES] + p[:, LANES:]

    w, aw = krylov(apply, q)
    y, ay = zip(*[krylov(apply, face_ref[5] * v) for v in w])
    for i in range(3):
        field_ref[i] = w[i]
        field_ref[3 + 2 * i] = y[i][1]
        field_ref[4 + 2 * i] = y[i][2]
    orders = [(k, l) for k in range(3) for l in range(k + 1)]
    at = 0
    for i in range(3):
        for j in range(3):
            for k, l in orders:
                inner(at, y[i][k], ay[j][l])
                at += 1
            for k in range(3):
                inner(at, y[i][k], y[j][0])
                at += 1
    for k, l in orders:
        inner(at, w[k], aw[l])
        at += 1
    for k in range(3):
        inner(at, w[k], q)
        at += 1
    part_ref[8 * at :, :] = jnp.zeros((8 * (LANES - at), LANES), F32)
    zero = jnp.zeros((LANES, LANES), F32)
    pieces = [(part_ref[pl.ds(s, LANES, stride=8), :], zero) for s in range(8)]
    hi, lo = tree(pieces)
    hi, lo = jnp.transpose(hi), jnp.transpose(lo)
    total = rows_sum(hi)
    row = total[0] + (total[1] + rows_sum(lo)[0])
    row_ref[...] = jnp.broadcast_to(row[0:1], row_ref.shape)


def sums(q, north, south, east, west, faces):
    rows, cols = q.shape
    high, wide = rows + 16, cols + LANES
    return pl.pallas_call(
        sums_kernel,
        out_shape=(
            jax.ShapeDtypeStruct((LANES, LANES), F32),
            jax.ShapeDtypeStruct((9, high, wide), F32),
        ),
        in_specs=[VMEM] * 6,
        out_specs=(VMEM, VMEM),
        scratch_shapes=[pltpu.VMEM((8 * LANES, LANES), F32)],
        compiler_params=PARAMS,
        name="krylov_sums",
    )(q, north, south, east, west, faces)


def two_prod(a, b):
    p = a * b
    t = 4097.0 * a
    ah = t - (t - a)
    al = a - ah
    t = 4097.0 * b
    bh = t - (t - b)
    bl = b - bh
    return p, ((ah * bh - p) + (ah * bl + al * bh)) + al * bl


def quick(s, e):
    t = s + e
    return t, e - (t - s)


def pair_add(x, y):
    s, e = two_sum(x[0], y[0])
    return quick(s, e + (x[1] + y[1]))


def pair_neg(x):
    return -x[0], -x[1]


def pair_mul(x, y):
    p, e = two_prod(x[0], y[0])
    return quick(p, e + (x[0] * y[1] + x[1] * y[0]))


def pair_div(x, y):
    first = x[0] / y[0]
    p, e = two_prod(first, y[0])
    rest = ((x[0] - p) - e) + (x[1] - first * y[1])
    return quick(first, rest / y[0])


def pair_where(ok, x):
    return jnp.where(ok, x[0], 0.0), jnp.where(ok, x[1], 0.0)


def small_solve(g, b):
    sub = lambda x, y: pair_add(x, pair_neg(y))
    l1 = pair_div(g[1], g[0])
    l2 = pair_div(g[3], g[0])
    d1 = sub(g[2], pair_mul(l1, g[1]))
    t = sub(g[4], pair_mul(l1, g[3]))
    ok1 = d1[0] > 1e-10 * g[2][0]
    m2 = pair_where(ok1, pair_div(t, d1))
    d2 = sub(sub(g[5], pair_mul(l2, g[3])), pair_mul(m2, t))
    y1 = sub(b[1], pair_mul(l1, b[0]))
    y2 = sub(sub(b[2], pair_mul(l2, b[0])), pair_mul(m2, y1))
    x2 = pair_where(d2[0] > 1e-10 * g[5][0], pair_div(y2, d2))
    x1 = sub(pair_where(ok1, pair_div(y1, d1)), pair_mul(m2, x2))
    x0 = sub(sub(pair_div(b[0], g[0]), pair_mul(l1, x1)), pair_mul(l2, x2))
    return x0, x1, x2


def coefficients(every_ref):
    total = rows_sum(every_ref[...])
    total = quick(*total)
    lane = iota((8, LANES), 1)

    def pick(x, at):
        return tuple(jnp.sum(jnp.where(lane == at, v, 0.0), axis=1, keepdims=True) for v in x)

    wide = lambda x: tuple(jnp.broadcast_to(v, (8, LANES)) for v in x)
    first = [wide(pick(total, 81 + m)) for m in range(9)]
    c = small_solve(first[:6], first[6:])
    system = None
    for i in range(3):
        for j in range(3):
            shift = (LANES - 9 * (3 * i + j)) % LANES
            row = tuple(pltpu.roll(v, shift, 1) if shift else v for v in total)
            term = pair_mul(row, pair_mul(c[i], c[j]))
            system = term if system is None else pair_add(system, term)
    second = [wide(pick(system, m)) for m in range(9)]
    e = small_solve(second[:6], second[6:])
    return [v[0] for v in c], [v[0] for v in e]


def tracer_kernel(steric_ref, every_ref, field_ref, ocean_ref, lam_ref, one_ref, zero_ref, mu_ref, rho_ref, scratch_ref):
    rows, cols = rho_ref.shape
    high, wide = rows + 8, cols + LANES
    level = pl.program_id(0)

    def trim(v):
        edge = jnp.where(iota((8, wide), 0) < 4, v[rows : rows + 8], v[rows + 8 :])
        return jnp.concatenate([v[:rows], edge], axis=0)

    @pl.when(level == 0)
    def _():
        c, e = coefficients(every_ref)
        c, e = [v[0:1, 0:1] for v in c], [v[0:1, 0:1] for v in e]
        w = [field_ref[i] for i in range(3)]
        rho_1 = c[0] * w[0] + c[1] * w[1] + c[2] * w[2]
        rho_0 = e[0] * (ocean_ref[...] * rho_1)
        for k in (1, 2):
            v = c[0] * field_ref[2 + k] + c[1] * field_ref[4 + k] + c[2] * field_ref[6 + k]
            rho_0 = rho_0 + e[k] * v
        rho_ref[...] = rho_0[:rows, :cols]
        scratch_ref[0] = trim(rho_1)
        scratch_ref[1] = trim(rho_0)
        scratch_ref[2] = trim(ocean_ref[...])

    height = steric_ref[level]
    ocean = scratch_ref[2]

    def near(g):
        return (
            pltpu.roll(g, wide - 1, 1),
            pltpu.roll(g, 1, 1),
            pltpu.roll(g, high - 1, 0),
            pltpu.roll(g, 1, 0),
        )

    g = ocean * (lam_ref[0] + height * scratch_ref[0])
    e, w, n, s = near(g)
    mu = g - (
        one_ref[0, 0] * (g - e) + one_ref[1, 0] * (w - g) + one_ref[2, 0] * (g - n) + one_ref[3, 0] * (s - g)
    )
    g = ocean * (mu + height * scratch_ref[1])
    e, w, n, s = [v[:rows, :cols] for v in near(g)]
    g = g[:rows, :cols]
    mu_ref[0] = g - (
        zero_ref[0, 0] * (g - e) + zero_ref[1, 0] * (w - g) + zero_ref[2, 0] * (g - n) + zero_ref[3, 0] * (s - g)
    )


def tracers(steric, every, fields, ocean, lam, one, zero):
    levels, high, wide = lam.shape
    rows, cols = high - 8, wide - LANES
    whole = lambda shape: pl.BlockSpec(shape, lambda k: (0,) * len(shape))
    return pl.pallas_call(
        tracer_kernel,
        grid=(levels,),
        out_shape=(
            jax.ShapeDtypeStruct((levels, rows, cols), F32),
            jax.ShapeDtypeStruct((rows, cols), F32),
        ),
        in_specs=[
            pl.BlockSpec(memory_space=pltpu.SMEM),
            whole(every.shape),
            whole(fields.shape),
            whole(ocean.shape),
            pl.BlockSpec((1, high, wide), lambda k: (k, 0, 0)),
            pl.BlockSpec((4, 1, high, wide), lambda k: (0, k, 0, 0)),
            pl.BlockSpec((4, 1, rows, cols), lambda k: (0, k, 0, 0)),
        ],
        out_specs=(pl.BlockSpec((1, rows, cols), lambda k: (k, 0, 0)), whole((rows, cols))),
        scratch_shapes=[pltpu.VMEM((3, high, wide), F32)],
        compiler_params=PARAMS,
        name="tracer_steps",
    )(steric, every, fields, ocean, lam, one, zero)


def beside(cells, axis, step):
    count = lax.axis_size(axis)
    return lax.ppermute(cells, axis, [((i + step) % count, i) for i in range(count)])


def stretched(field, width, rows_to, cols_to):
    top, bottom = field[..., :width, :], field[..., -width:, :]
    north, south = beside(top, "ty", 1), beside(bottom, "ty", -1)
    gap = jnp.zeros(field.shape[:-2] + (rows_to - 2 * width, field.shape[-1]), F32)
    field = jnp.concatenate([field, north, gap, south], axis=-2)

    def strip(cells, step):
        flat = jnp.moveaxis(cells, -1, 0)
        sent = beside(flat.reshape(-1, LANES) if flat.size % LANES == 0 else flat.reshape(-1), "tx", step)
        return jnp.moveaxis(sent.reshape(flat.shape), 0, -1)

    east, west = strip(field[..., :width], 1), strip(field[..., -width:], -1)
    gap = jnp.zeros(field.shape[:-1] + (cols_to - 2 * width,), F32)
    return jnp.concatenate([field, east, gap, west], axis=-1)


def west_of(v):
    return jnp.roll(v, 1, axis=-1)


def south_of(v):
    return jnp.roll(v, 1, axis=-2)


def on_device(
    lam_tracer,
    lam_eta,
    land,
    zonal_flow,
    merid_flow,
    zonal_mixing,
    merid_mixing,
    surface_east,
    surface_north,
    surface_diag,
    steric,
    eta_saved,
    obs_sla,
    obs_weight,
    obs_tile,
    obs_start,
    obs_count,
):
    levels, rows, cols = lam_tracer.shape
    n_rows = lax.axis_size("ty")
    devices = n_rows * lax.axis_size("tx")
    capacity = 2 * obs_sla.shape[0] // devices
    row_ids = lax.broadcasted_iota(jnp.int32, (rows, 1), 0) + lax.axis_index("ty") * rows
    open_rows = (row_ids < rows * n_rows - 1).astype(jnp.float32)

    sent = pack(obs_sla, obs_weight, obs_tile, obs_start, obs_count, capacity)
    got = lax.all_to_all(
        sent.reshape(devices, 1, -1), AXES, split_axis=0, concat_axis=0, tiled=True
    ).reshape(sent.shape)

    merid_flow = merid_flow * open_rows
    merid_mixing = merid_mixing * open_rows
    surface_north = surface_north * open_rows
    ocean = land.astype(jnp.float32)
    faces = stretched(jnp.stack([surface_diag, surface_east, surface_north, ocean]), 6, 16, LANES)
    diag, f_east, f_north, ocean_6 = faces[0], faces[1], faces[2], faces[3]
    f_west, f_south = west_of(f_east), south_of(f_north)
    centre = (1.0 + diag) + f_east + f_west + f_north + f_south
    faces = jnp.stack([centre, f_east, f_west, f_north, f_south, ocean_6])

    half_x, half_y = 0.5 * zonal_flow, 0.5 * merid_flow
    fields = stretched(
        jnp.concatenate(
            [
                lam_tracer,
                half_x[1] + zonal_mixing,
                half_x[1] - zonal_mixing,
                half_y[1] + merid_mixing,
                half_y[1] - merid_mixing,
                half_x[0] - zonal_mixing,
                half_y[0] - merid_mixing,
            ]
        ),
        2,
        8,
        LANES,
    ).reshape(7, levels, rows + 8, cols + LANES)
    lam = fields[0]
    one = jnp.stack([fields[1], west_of(fields[2]), fields[3], south_of(fields[4])])
    zero = jnp.stack(
        [
            half_x[0] + zonal_mixing,
            west_of(fields[5])[:, :rows, :cols],
            half_y[0] + merid_mixing,
            south_of(fields[6])[:, :rows, :cols],
        ]
    )

    rhs = unpack(got, eta_saved, lam_eta, land, capacity)
    north, south = beside(rhs[:8], "ty", 1), beside(rhs[-8:], "ty", -1)
    tall = jnp.concatenate([rhs, north, south], axis=0)
    east, west = beside(tall[:, :LANES], "tx", 1), beside(tall[:, -LANES:], "tx", -1)
    mine, krylov_fields = sums(rhs, north, south, east, west, faces)
    every = lax.all_to_all(
        mine.reshape(devices, 1, LANES), AXES, split_axis=0, concat_axis=0, tiled=True
    ).reshape(devices, LANES)
    return tracers(steric, every, krylov_fields, ocean_6, lam, one, zero)


def solution(mesh):
    in_specs = (
        P(None, "ty", "tx"),
        P("ty", "tx"),
        P("ty", "tx"),
        P(None, None, "ty", "tx"),
        P(None, None, "ty", "tx"),
        P(None, "ty", "tx"),
        P(None, "ty", "tx"),
        P("ty", "tx"),
        P("ty", "tx"),
        P("ty", "tx"),
        P(),
        P("ty", "tx"),
        P(AXES, None),
        P(AXES, None),
        P(AXES, None),
        P(AXES),
        P(AXES),
    )
    out_specs = (P(None, "ty", "tx"), P("ty", "tx"))
    return jax.shard_map(
        on_device, mesh=mesh, in_specs=in_specs, out_specs=out_specs, check_vma=False
    )
```

time: 315 us -> 136 us (0.43); the launches traced: 311 us -> 136 us
  local copies, waits for them, and re-layouts: 114 us -> 36.1 us
  between operations: 64.8 us -> 1.07 us
  starting transfers between devices: 62.6 us -> 36.7 us
  other arithmetic: 43.5 us -> 27.7 us
  Pallas kernels: 0 us -> 14.6 us
  matrix products: 11.3 us -> 0 us
  waiting for transfers between devices: 15.6 us -> 19.4 us
    another operation x1, local copies, waits for them, and re-layouts: 57.8 us -> 0.01 us  [on_device(): faces = jnp.stack([centre, f_east, f_west, f_north, f_south, ocean_6])]
    pallas_call x0 -> x4, Pallas kernels: none -> 14.6 us  [the longest x1 8.26 us: tracers(): pl.pallas_call(tracer_kernel, grid=(levels,), out_shape=(jax.ShapeDtypeSt...]
    ppermute x12, starting transfers between devices: 32.9 us -> 19.5 us  [beside(): lax.ppermute(cells, axis, [((i + step) % count, i) for i in range(count)])]
    all_to_all x2, starting transfers between devices: 29.7 us -> 17.1 us  [the longest x1 11 us: on_device(): lax.all_to_all(sent.reshape(devices, 1, -1), AXES, split_axis=0, concat_a...]
    slice x91 -> x12, local copies, waits for them, and re-layouts: 20.6 us -> 8.27 us  [the longest x4 3.25 us: west_of(): return jnp.roll(v, 1, axis=-1)]
    select_n x8 -> x0, other arithmetic: 12.2 us -> none  [the longest x7 12.2 us: unpack(): pair = jnp.where(flag, jnp.roll(pair, 1 << bit, axis=2), pair)]
    dot_general x3 -> x0, matrix products: 11.3 us -> none  [the longest x1 5.33 us: pack(): jnp.dot(placed.astype(jnp.float32), stacked, precision=lax.Precision.HIGH...]
    another operation x0 -> x6, other arithmetic: none -> 11.3 us  [the longest x2 6.12 us: on_device(): jnp.stack([fields[1], west_of(fields[2]), fields[3], south_of(fields[4])])]
  transfers between devices with their start and end apart: 14 -> 14, of which waited for: 5 -> 3; matrix products, arithmetic and copies ran while one was open for 7% -> 40% of each run, Pallas kernels for 0% -> 3%
where the time goes in v2:
time: 136 us
  starting transfers between devices  36.7 us (27%)
  local copies, waits for them, and re-layouts  36.1 us (27%)
  other arithmetic  27.7 us (20%)
  waiting for transfers between devices  19.4 us (14%)
  Pallas kernels  14.6 us (11%)
    ppermute x12, starting transfers between devices, beside(): lax.ppermute(cells, axis, [((i + step) % count, i) for i in range(count)])  19.5 us
    ppermute x12, waiting for transfers between devices, beside(): lax.ppermute(cells, axis, [((i + step) % count, i) for i in range(count)])  11.4 us
    all_to_all x1, starting transfers between devices, on_device(): lax.all_to_all(sent.reshape(devices, 1, -1), AXES, split_axis=0, concat_a...  11 us
    transpose x6, local copies, waits for them, and re-layouts, strip(): flat = jnp.moveaxis(cells, -1, 0)  9.35 us
    reshape x8, local copies, waits for them, and re-layouts, strip(): return jnp.moveaxis(sent.reshape(flat.shape), 0, -1)  8.93 us
    pallas_call x1, Pallas kernels, tracers(): pl.pallas_call(tracer_kernel, grid=(levels,), out_shape=(jax.ShapeDtypeSt...  8.26 us
    all_to_all x1, waiting for transfers between devices, on_device(): lax.all_to_all(mine.reshape(devices, 1, LANES), AXES, split_axis=0, conca...  8.05 us
    unnamed x52, local copies, waits for them, and re-layouts  7.08 us
  transfers between devices with their start and end apart: 14, of which 3 were waited for; matrix products, arithmetic and copies ran while one was open for 40% of the time, Pallas kernels for 3%

profile of v2, /device:TPU:1, one launch (start us, length us, event | category | flops | bytes accessed | tf_op | source)
XLA Modules:
  0.0 135.5 jit_solution(12583895445987038000)
XLA Ops:
  0.7 0.8 convert_bitcast_fusion
  1.5 0.8 multiply_bitcast_fusion
  2.3 0.8 pad_maximum_fusion.12
  3.1 1.4 %collective-permute-start.4 = (f32[4,6,256]{2,1,0:T(8,128)S(1)}, f32[4,6,256]{2,1,0:T(8,128)S(1)}, u32[]{:S(2)}, u32[]{:S(2)}) collective-permute-start(f32[4,6,256]{2,1,0:T(8,128)S(1)} %get-tuple-element.33), channel_id=1, source_target_pairs={{16,0},{32,16},{48,32},{64,48},{80,64},{96,80},{112,96},{0,112},{1... | collective-permute-start | bytes 73736 | tf_op jit(solution)/shard_map/ppermute | solution.py:422
  4.5 1.6 %collective-permute-start.5 = (f32[4,6,256]{2,1,0:T(8,128)S(1)}, f32[4,6,256]{2,1,0:T(8,128)S(1)}, u32[]{:S(2)}, u32[]{:S(2)}) collective-permute-start(f32[4,6,256]{2,1,0:T(8,128)S(1)} %get-tuple-element.34), channel_id=1, source_target_pairs={{112,0},{0,16},{16,32},{32,48},{48,64},{64,80},{80,96},{96,112},{1... | collective-permute-start | bytes 73736 | tf_op jit(solution)/shard_map/ppermute | solution.py:422
  6.1 1.4 %multiply_multiply_fusion = f32[2,16,32,256]{3,2,1,0:T(8,128)S(1)} fusion(f32[2,16,32,256]{3,2,1,0:T(8,128)} %param.21, f32[32]{0:T(128)S(1)} %compare_convert_fusion), kind=kLoop, calls=%fused_computation.6 | loop fusion | flops 524288 | bytes 2097280 | tf_op jit(solution)/shard_map/mul | solution.py:490
  7.6 1.4 %broadcast_multiply_fusion = f32[2,16,32,256]{3,2,1,0:T(8,128)S(1)} fusion(f32[2,16,32,256]{3,2,1,0:T(8,128)} %param.20), kind=kLoop, calls=%fused_computation.27 | loop fusion | flops 262144 | bytes 2097152 | tf_op jit(solution)/shard_map/mul | solution.py:490
  8.9 0.8 constant_dynamic-update-slice_fusion
  9.8 0.9 add_dynamic-update-slice_fusion.1
  10.7 1.1 add_bitcast_fusion.1
  11.8 0.9 add_dynamic-update-slice_fusion
  12.7 1.2 add_bitcast_fusion
  13.9 0.9 subtract_dynamic-update-slice_fusion.1
  14.8 1.0 subtract_dynamic-update-slice_fusion
  15.8 0.1 slice_bitcast_fusion.9
  15.9 0.1 copy.30
  16.0 0.1 reshape.96
  16.1 5.0 %collective-permute-start.6 = (f32[9,128]{1,0:T(8,128)S(1)}, f32[9,128]{1,0:T(8,128)S(1)}, u32[]{:S(2)}, u32[]{:S(2)}) collective-permute-start(f32[9,128]{1,0:T(8,128)S(1)} %reshape.96), channel_id=1, source_target_pairs={{1,0},{2,1},{3,2},{4,3},{5,4},{6,5},{7,6},{8,7},{9,8},{10,9},{11,1... | collective-permute-start | bytes 13832 | tf_op jit(solution)/shard_map/ppermute | solution.py:422
  21.1 0.1 reshape.98
  21.2 2.4 %fusion.12 = (f32[112,2,256]{2,1,0:T(2,128)}, f32[112,2,256]{2,1,0:T(2,128)}) fusion(f32[112,32,256]{2,1,0:T(8,128)} %subtract_dynamic-update-slice_fusion), kind=kLoop, calls=%fused_computation.63 | loop fusion | bytes 917504 | tf_op jit(solution)/shard_map/slice | solution.py:426
  23.6 2.2 %collective-permute-start.8 = (f32[112,2,256]{2,1,0:T(2,128)}, f32[112,2,256]{2,1,0:T(2,128)S(1)}, u32[]{:S(2)}, u32[]{:S(2)}) collective-permute-start(f32[112,2,256]{2,1,0:T(2,128)} %get-tuple-element.17), channel_id=1, source_target_pairs={{16,0},{32,16},{48,32},{64,48},{80,64},{96,80},{112,96},{0,112},{1... | collective-permute-start | bytes 688136 | tf_op jit(solution)/shard_map/ppermute | solution.py:422
  25.9 3.5 %pack_segments.1 = f32[4224,128]{1,0:T(8,128)S(1)} custom-call(f32[1024,128]{1,0:T(8,128)S(1)} %copy-done.6, f32[1024,128]{1,0:T(8,128)S(1)} %copy-done.7, s32[8,128]{1,0:T(8,128)S(1)} %bitcast.90, s32[8,128]{1,0:T(8,128)S(1)} %bitcast.91, s32[8,128]{1,0:T(8,128)S(1)} %bitcast.92), custom_call_target="tpu_custom_call" | custom-call | tf_op jit(solution)/shard_map/pack_segments/pallas_call | solution.py:89
  29.4 1.4 %copy-done.1 = f32[4224,128]{1,0:T(8,128)} copy-done((f32[4224,128]{1,0:T(8,128)}, f32[4224,128]{1,0:T(8,128)S(1)}, u32[]{:S(2)}) %copy-start.1) | copy-done | bytes 2162712
  30.8 11.0 %all-to-all-start = ((f32[128,1,4224]{2,1,0:T(1,128)}), f32[128,1,4224]{2,1,0:T(1,128)S(1)}, u32[]{:S(2)}, u32[]{:S(2)}) async-start(f32[128,1,4224]{2,1,0:T(1,128)} %bitcast.88), calls=%async_computation | async-start | bytes 4325376 | tf_op jit(solution)/shard_map/all_to_all | solution.py:476
  42.0 0.1 copy.31
  42.2 0.1 copy.33
  42.4 0.1 pad_maximum_fusion.6
  42.6 0.1 fusion.6
  42.9 0.7 copy-done.20
  43.6 2.9 %pad_maximum_fusion.1 = f32[112,40,256]{2,1,0:T(8,128)S(1)} fusion(f32[112,2,256]{2,1,0:T(2,128)} %collective-permute-done.9, f32[112,4,256]{2,1,0:T(4,128)S(1)} %broadcast_in_dim.16, f32[112,2,256]{2,1,0:T(2,128)} %copy-done.20, f32[112,32,256]{2,1,0:T(8,128)} %subtract_dynamic-update-slice_fusion), kind=kLoop, calls=%fused_computation.1 | loop fusion | flops 3440640 | bytes 9175040 | tf_op jit(solution)/shard_map/concatenate | solution.py:429
  46.5 2.8 %slice_bitcast_fusion.1 = (f32[2,112,40]{0,2,1:T(8,128)}, f32[2,112,40]{0,2,1:T(8,128)}) fusion(f32[112,40,256]{2,1,0:T(8,128)S(1)} %pad_maximum_fusion.1), kind=kLoop, calls=%fused_computation.4 | loop fusion | bytes 143360 | tf_op jit(solution)/shard_map/transpose | solution.py:432
  49.4 3.1 %copy.38 = f32[2,112,40]{2,1,0:T(8,128)} copy(f32[2,112,40]{0,2,1:T(8,128)} %get-tuple-element.16) | data formatting | bytes 71680 | tf_op jit(solution)/shard_map/transpose | solution.py:432
  52.5 1.0 reshape.104
  53.5 1.5 %collective-permute-start.11 = (f32[70,128]{1,0:T(8,128)S(1)}, f32[70,128]{1,0:T(8,128)S(1)}, u32[]{:S(2)}, u32[]{:S(2)}) collective-permute-start(f32[70,128]{1,0:T(8,128)S(1)} %reshape.104), channel_id=1, source_target_pairs={{15,0},{0,1},{1,2},{2,3},{3,4},{4,5},{5,6},{6,7},{7,8},{8,9},{9,10... | collective-permute-start | bytes 107528 | tf_op jit(solution)/shard_map/ppermute | solution.py:422
  55.0 3.1 %copy.36 = f32[2,112,40]{2,1,0:T(8,128)} copy(f32[2,112,40]{0,2,1:T(8,128)} %get-tuple-element.15) | data formatting | bytes 71680 | tf_op jit(solution)/shard_map/transpose | solution.py:432
  58.1 1.0 reshape.102
  59.1 3.7 %collective-permute-start.10 = (f32[70,128]{1,0:T(8,128)S(1)}, f32[70,128]{1,0:T(8,128)}, u32[]{:S(2)}, u32[]{:S(2)}) collective-permute-start(f32[70,128]{1,0:T(8,128)S(1)} %reshape.102), channel_id=1, source_target_pairs={{1,0},{2,1},{3,2},{4,3},{5,4},{6,5},{7,6},{8,7},{9,8},{10,9},{11,1... | collective-permute-start | bytes 107528 | tf_op jit(solution)/shard_map/ppermute | solution.py:422
  62.8 7.5 %collective-permute-done.11 = f32[70,128]{1,0:T(8,128)S(1)} collective-permute-done((f32[70,128]{1,0:T(8,128)S(1)}, f32[70,128]{1,0:T(8,128)S(1)}, u32[]{:S(2)}, u32[]{:S(2)}) %collective-permute-start.11) | collective-permute-done | bytes 35872 | tf_op jit(solution)/shard_map/ppermute | solution.py:422
  70.3 0.8 reshape.105
  71.0 3.2 %copy.39 = f32[2,112,40]{0,2,1:T(8,128)} copy(f32[2,112,40]{2,1,0:T(8,128)} %reshape.105) | data formatting | bytes 71680 | tf_op jit(solution)/shard_map/reshape | solution.py:434
  74.2 1.5 %reshape.103 = f32[2,112,40]{2,1,0:T(8,128)} reshape(f32[70,128]{1,0:T(8,128)} %collective-permute-done.10) | data formatting | bytes 71680 | tf_op jit(solution)/shard_map/reshape | solution.py:434
  75.7 3.1 %copy.37 = f32[2,112,40]{0,2,1:T(8,128)} copy(f32[2,112,40]{2,1,0:T(8,128)} %reshape.103) | data formatting | bytes 71680 | tf_op jit(solution)/shard_map/reshape | solution.py:434
  78.8 4.4 %pad_maximum_fusion = f32[112,40,384]{2,1,0:T(8,128)S(1)} fusion(f32[112,40,2]{2,1,0:T(8,128)} %bitcast.93, f32[112,40,2]{2,1,0:T(8,128)} %bitcast.95, f32[112,2,256]{2,1,0:T(2,128)} %collective-permute-done.9, f32[112,4,256]{2,1,0:T(4,128)S(1)} %broadcast_in_dim.16, f32[112,2,256]{2,1,0:T(2,128)S(1)} %copy-done.21, ...), kind=kLoop, calls=%fused_computation | loop fusion | flops 10321920 | bytes 11542016 | tf_op jit(solution)/shard_map/concatenate | solution.py:438
  83.3 2.0 %fusion.13 = (f32[16,40,1]{2,1,0:T(8,128)}, f32[16,40,1]{2,1,0:T(8,128)S(1)}) fusion(f32[112,40,2]{2,1,0:T(8,128)} %bitcast.94), kind=kLoop, calls=%fused_computation.64 | loop fusion | bytes 10240 | tf_op jit(solution)/shard_map/jit(_roll_static)/slice | solution.py:442
  85.4 1.1 fusion.11
  86.4 1.1 fusion.9
  87.6 1.7 %maximum_bitcast_fusion = (f32[1,16,40,384]{3,2,1,0:T(8,128)}, f32[1,16,40,384]{3,2,1,0:T(8,128)}) fusion(f32[16,40,383]{2,1,0:T(8,128)S(1)} %get-tuple-element.7, f32[16,40,1]{2,1,0:T(8,128)S(1)} %get-tuple-element.20, f32[16,39,384]{2,1,0:T(8,128)S(1)} %get-tuple-element.11, f32[16,1,384]{2,1,0:T(1,128)S(1)} %get-tuple-element.9), kind=kLoop, calls=%fused_computation.9 | loop fusion | flops 491520 | bytes 3932160 | tf_op jit(solution)/shard_map/stack | solution.py:508
  89.3 1.5 %slice_bitcast_fusion.3 = (f32[1,16,40,384]{3,2,1,0:T(8,128)}, f32[1,16,40,384]{3,2,1,0:T(8,128)}, f32[16,40,384]{2,1,0:T(8,128)S(1)}) fusion(f32[112,40,384]{2,1,0:T(8,128)S(1)} %pad_maximum_fusion), kind=kLoop, calls=%fused_computation.8 | loop fusion | bytes 5898240 | tf_op jit(solution)/shard_map/slice | solution.py:508
  90.8 1.0 forcing.1.q_ref
  91.8 1.2 collective-permute-start
  93.0 1.4 %collective-permute-start.1 = (f32[8,256]{1,0:T(8,128)S(1)}, f32[8,256]{1,0:T(8,128)S(1)}, u32[]{:S(2)}, u32[]{:S(2)}) collective-permute-start(f32[8,256]{1,0:T(8,128)S(1)} %get-tuple-element.41), channel_id=1, source_target_pairs={{112,0},{0,16},{16,32},{32,48},{48,64},{64,80},{80,96},{96,112},{1... | collective-permute-start | bytes 24584 | tf_op jit(solution)/shard_map/ppermute | solution.py:422
  94.4 4.4 %pad_maximum_fusion.2.one_ref = f32[4,16,40,384]{3,2,1,0:T(8,128)} fusion(f32[1,16,40,384]{3,2,1,0:T(8,128)} %get-tuple-element.44, f32[1,16,40,384]{3,2,1,0:T(8,128)} %get-tuple-element.13, f32[1,16,40,384]{3,2,1,0:T(8,128)} %get-tuple-element.43, f32[1,16,40,384]{3,2,1,0:T(8,128)} %get-tuple-element.12), kind=kLoop, calls=%fused_computation.2 | loop fusion | flops 2949120 | bytes 7864320 | tf_op jit(solution)/shard_map/stack | solution.py:508
  98.8 0.6 collective-permute-start.2
  99.5 0.9 collective-permute-start.3
  100.4 1.2 fusion
  101.6 3.9 %collective-permute-done.3.west_ref = f32[48,128]{1,0:T(8,128)S(1)} collective-permute-done((f32[48,128]{1,0:T(8,128)S(1)}, f32[48,128]{1,0:T(8,128)S(1)}, u32[]{:S(2)}, u32[]{:S(2)}) %collective-permute-start.3) | collective-permute-done | bytes 24608 | tf_op jit(solution)/shard_map/ppermute | solution.py:422
  105.5 1.8 %krylov_sums.1 = (f32[128,128]{1,0:T(8,128)}, f32[9,48,384]{2,1,0:T(8,128)S(1)}) custom-call(f32[32,256]{1,0:T(8,128)S(1)} %forcing.1.q_ref, f32[8,256]{1,0:T(8,128)S(1)} %collective-permute-done.north_ref, f32[8,256]{1,0:T(8,128)S(1)} %collective-permute-done.1.south_ref, f32[48,128]{1,0:T(8,128)S(1)} %collective-permute-done.2.east_ref, ...), custom_call_target="tpu_custom_call" | custom-call | tf_op jit(solution)/shard_map/krylov_sums/pallas_call | solution.py:250
  107.3 0.9 copy-done.2
  108.2 6.2 %all-to-all-start.1 = ((f32[128,1,128]{2,1,0:T(1,128)}), f32[128,1,128]{2,1,0:T(1,128)S(1)}, u32[]{:S(2)}, u32[]{:S(2)}) async-start(f32[128,1,128]{2,1,0:T(1,128)} %bitcast.21), calls=%async_computation.1 | async-start | bytes 131072 | tf_op jit(solution)/shard_map/all_to_all | solution.py:523
  114.4 1.7 %pad_maximum_fusion.3.zero_ref = f32[4,16,32,256]{3,2,1,0:T(8,128)S(1)} fusion(f32[1,16,32,256]{3,2,1,0:T(8,128)} %get-tuple-element.45, f32[1,16,32,256]{3,2,1,0:T(8,128)} %get-tuple-element.21, f32[1,16,32,256]{3,2,1,0:T(8,128)} %get-tuple-element.46, f32[1,16,32,256]{3,2,1,0:T(8,128)} %get-tuple-element.23), kind=kLoop, calls=%fused_computation.5 | loop fusion | flops 1572864 | bytes 4194304 | tf_op jit(solution)/shard_map/stack | solution.py:509
  116.0 8.1 %all-to-all-done.1 = f32[128,1,128]{2,1,0:T(1,128)S(1)} async-done(((f32[128,1,128]{2,1,0:T(1,128)}), f32[128,1,128]{2,1,0:T(1,128)S(1)}, u32[]{:S(2)}, u32[]{:S(2)}) %all-to-all-start.1) | async-done | bytes 65568 | tf_op jit(solution)/shard_map/all_to_all | solution.py:523
  124.1 2.1 %copy-done = f32[4,16,40,384]{3,2,1,0:T(8,128)S(1)} copy-done((f32[4,16,40,384]{3,2,1,0:T(8,128)S(1)}, f32[4,16,40,384]{3,2,1,0:T(8,128)}, u32[]{:S(2)}) %copy-start) | copy-done | bytes 3932184
  126.2 1.1 copy-done.3
  127.3 8.3 %tracer_steps.1 = (f32[16,32,256]{2,1,0:T(8,128)}, f32[32,256]{1,0:T(8,128)}) custom-call(f32[16]{0:T(128)S(1)} %copy-done.14, f32[128,128]{1,0:T(8,128)S(1)} %bitcast.89, f32[9,48,384]{2,1,0:T(8,128)S(1)} %copy-done.3, f32[48,384]{1,0:T(8,128)S(1)} %get-tuple-element.25.ocean_ref, f32[16,40,384]{2,1,0:T(8,128)S(1)} %get-tuple-element.14.lam_ref, ...), custom_call_target="tpu_custom_call" | custom-call | tf_op jit(solution)/shard_map/tracer_steps/pallas_call | solution.py:397
  (83 shorter events, 0.9 us)
Async XLA Ops:
  0.6 8.3 %copy-start.22 = (f32[16,32,256]{2,1,0:T(8,128)S(1)}, f32[16,32,256]{2,1,0:T(8,128)}, u32[]{:S(2)}) copy-start(f32[16,32,256]{2,1,0:T(8,128)} %param.17) | copy-start | bytes 1572868
  0.6 9.2 %copy-start.15 = (f32[16,32,256]{2,1,0:T(8,128)S(1)}, f32[16,32,256]{2,1,0:T(8,128)}, u32[]{:S(2)}) copy-start(f32[16,32,256]{2,1,0:T(8,128)} %param.22) | copy-start | bytes 1572868
  3.1 12.6 %collective-permute-start.4 = (f32[4,6,256]{2,1,0:T(8,128)S(1)}, f32[4,6,256]{2,1,0:T(8,128)S(1)}, u32[]{:S(2)}, u32[]{:S(2)}) collective-permute-start(f32[4,6,256]{2,1,0:T(8,128)S(1)} %get-tuple-element.33), channel_id=1, source_target_pairs={{16,0},{32,16},{48,32},{64,48},{80,64},{96,80},{112,96},{0,112},{1... | collective-permute-start | bytes 73736 | tf_op jit(solution)/shard_map/ppermute | solution.py:422
  4.5 11.2 %collective-permute-start.5 = (f32[4,6,256]{2,1,0:T(8,128)S(1)}, f32[4,6,256]{2,1,0:T(8,128)S(1)}, u32[]{:S(2)}, u32[]{:S(2)}) collective-permute-start(f32[4,6,256]{2,1,0:T(8,128)S(1)} %get-tuple-element.34), channel_id=1, source_target_pairs={{112,0},{0,16},{16,32},{32,48},{48,64},{64,80},{80,96},{96,112},{1... | collective-permute-start | bytes 73736 | tf_op jit(solution)/shard_map/ppermute | solution.py:422
  7.6 4.2 %copy-start.16 = (f32[16,32,256]{2,1,0:T(8,128)S(1)}, f32[16,32,256]{2,1,0:T(8,128)}, u32[]{:S(2)}) copy-start(f32[16,32,256]{2,1,0:T(8,128)} %param.23) | copy-start | bytes 1572868
  11.8 4.0 %copy-start.23 = (f32[32,256]{1,0:T(8,128)S(1)}, f32[32,256]{1,0:T(8,128)}, u32[]{:S(2)}) copy-start(f32[32,256]{1,0:T(8,128)} %param.24) | copy-start | bytes 98308
  11.8 4.0 %copy-start.24 = (f32[32,256]{1,0:T(8,128)S(1)}, f32[32,256]{1,0:T(8,128)}, u32[]{:S(2)}) copy-start(f32[32,256]{1,0:T(8,128)} %param.26) | copy-start | bytes 98308
  12.7 13.1 %copy-start.6 = (f32[1024,128]{1,0:T(8,128)S(1)}, f32[1024,128]{1,0:T(8,128)}, u32[]{:S(2)}) copy-start(f32[1024,128]{1,0:T(8,128)} %sla_ref.1) | copy-start | bytes 1572868
  12.7 13.1 %copy-start.7 = (f32[1024,128]{1,0:T(8,128)S(1)}, f32[1024,128]{1,0:T(8,128)}, u32[]{:S(2)}) copy-start(f32[1024,128]{1,0:T(8,128)} %weight_ref.1) | copy-start | bytes 1572868
  12.7 13.1 %copy-start.11 = (s32[1024,1]{0,1:T(1,128)S(1)}, s32[1024,1]{0,1:T(1,128)}, u32[]{:S(2)}) copy-start(s32[1024,1]{0,1:T(1,128)} %param.31) | copy-start | bytes 12292
  12.7 13.1 %copy-start.12 = (s32[1024]{0:T(1024)S(1)}, s32[1024]{0:T(1024)}, u32[]{:S(2)}) copy-start(s32[1024]{0:T(1024)} %param.32) | copy-start | bytes 12292
  12.7 13.1 %copy-start.13 = (s32[1024]{0:T(1024)S(1)}, s32[1024]{0:T(1024)}, u32[]{:S(2)}) copy-start(s32[1024]{0:T(1024)} %param.33) | copy-start | bytes 12292
  16.1 25.9 %collective-permute-start.6 = (f32[9,128]{1,0:T(8,128)S(1)}, f32[9,128]{1,0:T(8,128)S(1)}, u32[]{:S(2)}, u32[]{:S(2)}) collective-permute-start(f32[9,128]{1,0:T(8,128)S(1)} %reshape.96), channel_id=1, source_target_pairs={{1,0},{2,1},{3,2},{4,3},{5,4},{6,5},{7,6},{8,7},{9,8},{10,9},{11,1... | collective-permute-start | bytes 13832 | tf_op jit(solution)/shard_map/ppermute | solution.py:422
  21.2 21.0 %collective-permute-start.7 = (f32[9,128]{1,0:T(8,128)S(1)}, f32[9,128]{1,0:T(8,128)S(1)}, u32[]{:S(2)}, u32[]{:S(2)}) collective-permute-start(f32[9,128]{1,0:T(8,128)S(1)} %reshape.98), channel_id=1, source_target_pairs={{15,0},{0,1},{1,2},{2,3},{3,4},{4,5},{5,6},{6,7},{7,8},{8,9},{9,10... | collective-permute-start | bytes 13832 | tf_op jit(solution)/shard_map/ppermute | solution.py:422
  23.6 19.2 %collective-permute-start.8 = (f32[112,2,256]{2,1,0:T(2,128)}, f32[112,2,256]{2,1,0:T(2,128)S(1)}, u32[]{:S(2)}, u32[]{:S(2)}) collective-permute-start(f32[112,2,256]{2,1,0:T(2,128)} %get-tuple-element.17), channel_id=1, source_target_pairs={{16,0},{32,16},{48,32},{64,48},{80,64},{96,80},{112,96},{0,112},{1... | collective-permute-start | bytes 688136 | tf_op jit(solution)/shard_map/ppermute | solution.py:422
  25.8 17.7 %collective-permute-start.9 = (f32[112,2,256]{2,1,0:T(2,128)}, f32[112,2,256]{2,1,0:T(2,128)}, u32[]{:S(2)}, u32[]{:S(2)}) collective-permute-start(f32[112,2,256]{2,1,0:T(2,128)} %get-tuple-element.18), channel_id=1, source_target_pairs={{112,0},{0,16},{16,32},{32,48},{48,64},{64,80},{80,96},{96,112},{1... | collective-permute-start | bytes 688136 | tf_op jit(solution)/shard_map/ppermute | solution.py:422
  29.4 1.4 %copy-start.1 = (f32[4224,128]{1,0:T(8,128)}, f32[4224,128]{1,0:T(8,128)S(1)}, u32[]{:S(2)}) copy-start(f32[4224,128]{1,0:T(8,128)S(1)} %pack_segments.1) | copy-start | bytes 6488068
  30.8 60.0 %all-to-all-start = ((f32[128,1,4224]{2,1,0:T(1,128)}), f32[128,1,4224]{2,1,0:T(1,128)S(1)}, u32[]{:S(2)}, u32[]{:S(2)}) async-start(f32[128,1,4224]{2,1,0:T(1,128)} %bitcast.88), calls=%async_computation | async-start | bytes 4325376 | tf_op jit(solution)/shard_map/all_to_all | solution.py:476
  42.8 0.7 copy-start.20
  53.5 16.8 %collective-permute-start.11 = (f32[70,128]{1,0:T(8,128)S(1)}, f32[70,128]{1,0:T(8,128)S(1)}, u32[]{:S(2)}, u32[]{:S(2)}) collective-permute-start(f32[70,128]{1,0:T(8,128)S(1)} %reshape.104), channel_id=1, source_target_pairs={{15,0},{0,1},{1,2},{2,3},{3,4},{4,5},{5,6},{6,7},{7,8},{8,9},{9,10... | collective-permute-start | bytes 107528 | tf_op jit(solution)/shard_map/ppermute | solution.py:422
  59.1 15.1 %collective-permute-start.10 = (f32[70,128]{1,0:T(8,128)S(1)}, f32[70,128]{1,0:T(8,128)}, u32[]{:S(2)}, u32[]{:S(2)}) collective-permute-start(f32[70,128]{1,0:T(8,128)S(1)} %reshape.102), channel_id=1, source_target_pairs={{1,0},{2,1},{3,2},{4,3},{5,4},{6,5},{7,6},{8,7},{9,8},{10,9},{11,1... | collective-permute-start | bytes 107528 | tf_op jit(solution)/shard_map/ppermute | solution.py:422
  62.8 20.5 %copy-start.4 = (f32[6,48,384]{2,1,0:T(8,128)}, f32[6,48,384]{2,1,0:T(8,128)S(1)}, u32[]{:S(2)}) copy-start(f32[6,48,384]{2,1,0:T(8,128)S(1)} %slice_dynamic-update-slice_fusion.face_ref) | copy-start | bytes 1327108
  62.8 16.0 %copy-start.21 = (f32[112,2,256]{2,1,0:T(2,128)S(1)}, f32[112,2,256]{2,1,0:T(2,128)}, u32[]{:S(2)}) copy-start(f32[112,2,256]{2,1,0:T(2,128)} %copy-done.20) | copy-start | bytes 688132
  89.3 1.5 %copy-start.8 = (s32[32,256]{1,0:T(8,128)S(1)}, s32[32,256]{1,0:T(8,128)}, u32[]{:S(2)}) copy-start(s32[32,256]{1,0:T(8,128)} %land_ref.1) | copy-start | bytes 98308
  89.3 1.5 %copy-start.9 = (f32[32,256]{1,0:T(8,128)S(1)}, f32[32,256]{1,0:T(8,128)}, u32[]{:S(2)}) copy-start(f32[32,256]{1,0:T(8,128)} %eta_ref.1) | copy-start | bytes 98308
  89.3 1.5 %copy-start.10 = (f32[32,256]{1,0:T(8,128)S(1)}, f32[32,256]{1,0:T(8,128)}, u32[]{:S(2)}) copy-start(f32[32,256]{1,0:T(8,128)} %lam_ref.1) | copy-start | bytes 98308
  91.8 7.0 %collective-permute-start = (f32[8,256]{1,0:T(8,128)S(1)}, f32[8,256]{1,0:T(8,128)S(1)}, u32[]{:S(2)}, u32[]{:S(2)}) collective-permute-start(f32[8,256]{1,0:T(8,128)S(1)} %get-tuple-element.42), channel_id=1, source_target_pairs={{16,0},{32,16},{48,32},{64,48},{80,64},{96,80},{112,96},{0,112},{1... | collective-permute-start | bytes 24584 | tf_op jit(solution)/shard_map/ppermute | solution.py:422
  93.0 5.8 %collective-permute-start.1 = (f32[8,256]{1,0:T(8,128)S(1)}, f32[8,256]{1,0:T(8,128)S(1)}, u32[]{:S(2)}, u32[]{:S(2)}) collective-permute-start(f32[8,256]{1,0:T(8,128)S(1)} %get-tuple-element.41), channel_id=1, source_target_pairs={{112,0},{0,16},{16,32},{32,48},{48,64},{64,80},{80,96},{96,112},{1... | collective-permute-start | bytes 24584 | tf_op jit(solution)/shard_map/ppermute | solution.py:422
  94.4 6.0 %copy-start.17 = (f32[16,39,384]{2,1,0:T(8,128)S(1)}, f32[16,39,384]{2,1,0:T(8,128)}, u32[]{:S(2)}) copy-start(f32[16,39,384]{2,1,0:T(8,128)} %get-tuple-element.10) | copy-start | bytes 2875396
  94.4 6.0 %copy-start.18 = (f32[16,40,383]{2,1,0:T(8,128)S(1)}, f32[16,40,383]{2,1,0:T(8,128)}, u32[]{:S(2)}) copy-start(f32[16,40,383]{2,1,0:T(8,128)} %get-tuple-element.6) | copy-start | bytes 2941444
  94.4 6.0 %copy-start.19 = (f32[16,40,1]{2,1,0:T(8,128)S(1)}, f32[16,40,1]{2,1,0:T(8,128)}, u32[]{:S(2)}) copy-start(f32[16,40,1]{2,1,0:T(8,128)} %get-tuple-element.19) | copy-start | bytes 7684
  98.8 6.7 %copy-start.5 = (f32[6,48,384]{2,1,0:T(8,128)S(1)}, f32[6,48,384]{2,1,0:T(8,128)}, u32[]{:S(2)}) copy-start(f32[6,48,384]{2,1,0:T(8,128)} %copy-done.4) | copy-start | bytes 1327108
  98.8 2.8 %collective-permute-start.2 = (f32[48,128]{1,0:T(8,128)S(1)}, f32[48,128]{1,0:T(8,128)S(1)}, u32[]{:S(2)}, u32[]{:S(2)}) collective-permute-start(f32[48,128]{1,0:T(8,128)S(1)} %get-tuple-element.40), channel_id=1, source_target_pairs={{1,0},{2,1},{3,2},{4,3},{5,4},{6,5},{7,6},{8,7},{9,8},{10,9},{11,1... | collective-permute-start | bytes 73736 | tf_op jit(solution)/shard_map/ppermute | solution.py:422
  99.5 6.0 %collective-permute-start.3 = (f32[48,128]{1,0:T(8,128)S(1)}, f32[48,128]{1,0:T(8,128)S(1)}, u32[]{:S(2)}, u32[]{:S(2)}) collective-permute-start(f32[48,128]{1,0:T(8,128)S(1)} %get-tuple-element.39), channel_id=1, source_target_pairs={{15,0},{0,1},{1,2},{2,3},{3,4},{4,5},{5,6},{6,7},{7,8},{8,9},{9,10... | collective-permute-start | bytes 73736 | tf_op jit(solution)/shard_map/ppermute | solution.py:422
  100.4 23.7 %copy-start.14 = (f32[16]{0:T(128)S(1)}, f32[16]{0:T(128)}, u32[]{:S(2)}) copy-start(f32[16]{0:T(128)} %steric_ref.1) | copy-start | bytes 196
  107.3 0.9 copy-start.2
  108.2 15.9 %all-to-all-start.1 = ((f32[128,1,128]{2,1,0:T(1,128)}), f32[128,1,128]{2,1,0:T(1,128)S(1)}, u32[]{:S(2)}, u32[]{:S(2)}) async-start(f32[128,1,128]{2,1,0:T(1,128)} %bitcast.21), calls=%async_computation.1 | async-start | bytes 131072 | tf_op jit(solution)/shard_map/all_to_all | solution.py:523
  124.1 2.1 %copy-start = (f32[4,16,40,384]{3,2,1,0:T(8,128)S(1)}, f32[4,16,40,384]{3,2,1,0:T(8,128)}, u32[]{:S(2)}) copy-start(f32[4,16,40,384]{3,2,1,0:T(8,128)} %pad_maximum_fusion.2.one_ref) | copy-start | bytes 11796484
  126.2 1.1 copy-start.3

commit v3 on v2

v3 whole, which is shorter than its diff:
```python
import functools

import jax
import jax.numpy as jnp
from jax import lax
from jax.experimental import pallas as pl
from jax.experimental.pallas import tpu as pltpu
from jax.sharding import PartitionSpec as P

AXES = ("ty", "tx")
SHIFT_0 = 1.6
SHIFT_1 = 35.0
SCALE_0 = 1.0 / 32.0
SCALE_1 = 1.0 / 16.0
LANES = 128
VMEM = pl.BlockSpec(memory_space=pltpu.VMEM)
SCALAR = pl.BlockSpec(memory_space=pltpu.SMEM)
HBM = pl.BlockSpec(memory_space=pltpu.HBM)
F32 = jnp.float32
BF16 = jnp.bfloat16


def params(mib):
    return pltpu.CompilerParams(vmem_limit_bytes=mib * 1024 * 1024)


def iota(dims, axis):
    return lax.broadcasted_iota(jnp.int32, dims, axis)


def shape(*dims):
    return jax.ShapeDtypeStruct(dims, F32)


def far_shape(*dims):
    return pltpu.HBM(dims, F32)


def far(arrays):
    return tuple(pltpu.with_memory_space_constraint(x, pltpu.HBM) for x in arrays)


def split(x):
    hi = x.astype(BF16)
    return hi, (x - hi.astype(F32)).astype(BF16)


def rank_kernel(capacity, sla_ref, weight_ref, tile_ref, start_ref, count_ref, token_ref, data_ref, place_ref, meta_ref):
    blocks = tile_ref.shape[0]
    square = (LANES, LANES)
    sub, lane = iota(square, 0), iota(square, 1)
    prefix = jnp.concatenate([(sub < lane).astype(BF16), jnp.ones(square, BF16)], axis=1)
    tile, start, count = tile_ref[...], start_ref[...], count_ref[...]
    col_t = jnp.transpose((start & (LANES - 1)).astype(F32)).astype(jnp.int32)
    count_t = jnp.transpose(count.astype(F32)).astype(jnp.int32)
    carry = jnp.zeros(square, F32)
    hits, firsts = [], []
    for k in range(blocks):
        target = tile[k : k + 1]
        hit = sub == target
        hits.append(hit.astype(F32).astype(BF16))
        both = jnp.dot(hits[-1], prefix, preferred_element_type=F32)
        slot = jnp.sum(jnp.where(hit, both[:, :LANES] + carry, 0.0), axis=0, keepdims=True)
        carry = carry + both[:, LANES:]
        slot = slot.astype(jnp.int32)
        place_ref[k : k + 1, :] = target * capacity + slot
        begin = start[k : k + 1]
        block_of = jnp.where(sub == slot, begin // LANES, 0)
        lane_of = jnp.where(sub == slot + 64, begin & (LANES - 1), 0)
        firsts.append((block_of + lane_of).astype(F32).astype(BF16))
        rows = slice(k * LANES, (k + 1) * LANES)
        weight = jnp.where(lane < count_t[:, k : k + 1], weight_ref[rows, :], 0.0)
        value = weight * sla_ref[rows, :]
        index = (lane - col_t[:, k : k + 1]) & (LANES - 1)
        weight = jnp.take_along_axis(weight, index, axis=1)
        value = jnp.take_along_axis(value, index, axis=1)
        data_ref[rows, :] = jnp.concatenate([*split(weight), *split(value)], axis=1)
    meta_ref[...] = lax.dot_general(
        jnp.concatenate(hits, axis=1),
        jnp.concatenate(firsts, axis=1),
        (((1,), (1,)), ((), ())),
        preferred_element_type=F32,
    )


def place_kernel(capacity, data_ref, place_ref, meta_ref, token_ref, north_ref, south_ref, out_ref, next_ref, made_ref, sems):
    next_ref[...] = token_ref[...]
    blocks = place_ref.shape[0]
    devices = LANES
    chunk = 2 * capacity + 1
    made_ref[pl.ds(2 * capacity, devices, stride=chunk), :] = meta_ref[...]
    place = jnp.concatenate([place_ref[k : k + 1, :] for k in range(blocks)], axis=1)
    group = 16
    height = group * capacity
    slots = iota((height, blocks * LANES), 0)
    copies = []
    for g in range(devices // group):
        pick = (slots == place - g * height).astype(F32).astype(BF16)
        moved = jnp.dot(pick, data_ref[...], preferred_element_type=F32)
        weight = moved[:, :LANES] + moved[:, LANES : 2 * LANES]
        value = moved[:, 2 * LANES : 3 * LANES] + moved[:, 3 * LANES :]
        for t in range(group):
            base = (g * group + t) * chunk
            rows = slice(t * capacity, (t + 1) * capacity)
            made_ref[base : base + capacity, :] = weight[rows]
            made_ref[base + capacity : base + 2 * capacity, :] = value[rows]
        ready = pl.ds(g * group * chunk, group * chunk)
        copies.append(pltpu.make_async_copy(made_ref.at[ready, :], out_ref.at[ready, :], sems.at[g]))
        copies[-1].start()
    for copy in copies:
        copy.wait()


def pack(obs_sla, obs_weight, obs_tile, obs_start, obs_count, token, capacity):
    blocks = obs_sla.shape[0] // LANES
    return pl.pallas_call(
        functools.partial(rank_kernel, capacity),
        out_shape=(
            jax.ShapeDtypeStruct((blocks * LANES, 4 * LANES), BF16),
            jax.ShapeDtypeStruct((blocks, LANES), jnp.int32),
            shape(LANES, LANES),
        ),
        in_specs=[VMEM] * 6,
        out_specs=(VMEM,) * 3,
        compiler_params=params(8),
        name="rank_segments",
    )(
        obs_sla,
        obs_weight,
        obs_tile.reshape(blocks, LANES),
        obs_start.reshape(blocks, LANES),
        obs_count.reshape(blocks, LANES),
        token,
    )


def placed(data, place, meta, token, around, capacity):
    chunk = 2 * capacity + 1
    return pl.pallas_call(
        functools.partial(place_kernel, capacity),
        out_shape=(far_shape(LANES * chunk, LANES), shape(*token.shape)),
        in_specs=[VMEM] * 4 + [pl.BlockSpec(memory_space=pl.ANY)] * 2,
        out_specs=(HBM, VMEM),
        scratch_shapes=[
            pltpu.VMEM((LANES * chunk, LANES), F32),
            pltpu.SemaphoreType.DMA((LANES // 16,)),
        ],
        compiler_params=params(12),
        name="place_segments",
    )(data, place, meta, token, *around)


def unpack_kernel(capacity, got_ref, height_ref, face_ref, token_ref, q_ref, next_ref, sum_ref):
    next_ref[...] = token_ref[...]
    chunk = 2 * capacity + 1
    square = (LANES, LANES)
    lane = iota(square, 1)
    meta = got_ref[pl.ds(2 * capacity, LANES, stride=chunk), :]
    meta_t = jnp.transpose(meta)
    rows, cols = q_ref.shape
    cells = rows * cols // LANES
    blocks = iota((cells, LANES), 0).astype(F32)
    lane_f = lane.astype(F32)
    acc = jnp.zeros((cells, 4 * LANES), F32)
    for j in range(capacity):
        weight = got_ref[pl.ds(j, LANES, stride=chunk), :]
        value = got_ref[pl.ds(capacity + j, LANES, stride=chunk), :]
        here = lane_f >= meta[:, 64 + j : 65 + j]
        hit = (blocks == meta_t[j : j + 1]).astype(F32).astype(BF16)
        his, los = [], []
        for x in (weight, value):
            hi = x.astype(BF16).astype(F32)
            lo = x - hi
            for keep in (here, ~here):
                his.append(jnp.where(keep, hi, 0.0).astype(BF16))
                los.append(jnp.where(keep, lo, 0.0).astype(BF16))
        data = jnp.concatenate(
            [jnp.concatenate(his, axis=1), jnp.concatenate(los, axis=1)], axis=0
        )
        acc = acc + jnp.dot(
            jnp.concatenate([hit, hit], axis=1), data, preferred_element_type=F32
        )
    for i in range(2):
        here, after = acc[:, 2 * i * LANES : (2 * i + 1) * LANES], acc[:, (2 * i + 1) * LANES : (2 * i + 2) * LANES]
        sum_ref[i, :, :] = here + pltpu.roll(after, 1, 0)
    for half in range(2):
        at = slice(half * LANES, (half + 1) * LANES)
        weight = sum_ref[0, pl.ds(half, rows, stride=2), :]
        value = sum_ref[1, pl.ds(half, rows, stride=2), :]
        mu = height_ref[0, :, at] + (weight * height_ref[1, :, at] - value)
        q_ref[:, at] = face_ref[3, 0:rows, at] * mu


def unpack(got, heights, faces, token, capacity):
    rows, cols = heights.shape[1:]
    return pl.pallas_call(
        functools.partial(unpack_kernel, capacity),
        out_shape=(shape(rows, cols), shape(*token.shape)),
        in_specs=[VMEM] * 4,
        out_specs=(VMEM, VMEM),
        scratch_shapes=[pltpu.VMEM((2, rows * cols // LANES, LANES), F32)],
        compiler_params=params(10),
        name="forcing",
    )(got, heights, faces, token)


def two_sum(a, b):
    s = a + b
    t = s - a
    return s, (a - (s - t)) + (b - t)


def pair_sum(x, y):
    s, e = two_sum(x[0], y[0])
    e = e + (x[1] + y[1])
    return s, e


def tree(parts):
    while len(parts) > 1:
        odd = parts[len(parts) // 2 * 2 :]
        parts = [pair_sum(parts[i], parts[i + 1]) for i in range(0, len(parts) - 1, 2)] + odd
    return parts[0]


def rows_sum(hi):
    zero = jnp.zeros((8, LANES), F32)
    total = tree([(hi[8 * i : 8 * i + 8], zero) for i in range(16)])
    for step in (4, 2, 1):
        total = pair_sum(total, (pltpu.roll(total[0], step, 0), pltpu.roll(total[1], step, 0)))
    return total


def krylov(apply, start):
    first = apply(start)
    one = SCALE_0 * (first - SHIFT_0 * start)
    second = apply(one)
    two = SCALE_1 * (second - SHIFT_1 * one)
    return (start, one, two), (first, second, apply(two))


def sums_kernel(q_ref, north_ref, south_ref, east_ref, west_ref, face_ref, token_ref, row_ref, field_ref, next_ref, part_ref):
    next_ref[...] = token_ref[...]
    rows, cols = q_ref.shape
    high, wide = rows + 16, cols + LANES
    side = jnp.where(iota((high, LANES), 1) < LANES // 2, east_ref[...], west_ref[...])
    q = jnp.concatenate(
        [jnp.concatenate([q_ref[...], north_ref[...], south_ref[...]], axis=0), side], axis=1
    )

    def apply(v):
        return (
            face_ref[0] * v
            - face_ref[1] * pltpu.roll(v, wide - 1, 1)
            - face_ref[2] * pltpu.roll(v, 1, 1)
            - face_ref[3] * pltpu.roll(v, high - 1, 0)
            - face_ref[4] * pltpu.roll(v, 1, 0)
        )

    def inner(at, a, b):
        p = a[:rows, :cols] * b[:rows, :cols]
        p = (p[0:8] + p[8:16]) + (p[16:24] + p[24:32])
        part_ref[8 * at : 8 * at + 8, :] = p[:, :LANES] + p[:, LANES:]

    w, aw = krylov(apply, q)
    y, ay = zip(*[krylov(apply, face_ref[5] * v) for v in w])
    for i in range(3):
        field_ref[i] = w[i]
        field_ref[3 + 2 * i] = y[i][1]
        field_ref[4 + 2 * i] = y[i][2]
    orders = [(k, l) for k in range(3) for l in range(k + 1)]
    at = 0
    for i in range(3):
        for j in range(3):
            for k, l in orders:
                inner(at, y[i][k], ay[j][l])
                at += 1
            for k in range(3):
                inner(at, y[i][k], y[j][0])
                at += 1
    for k, l in orders:
        inner(at, w[k], aw[l])
        at += 1
    for k in range(3):
        inner(at, w[k], q)
        at += 1
    part_ref[8 * at :, :] = jnp.zeros((8 * (LANES - at), LANES), F32)
    zero = jnp.zeros((LANES, LANES), F32)
    pieces = [(part_ref[pl.ds(s, LANES, stride=8), :], zero) for s in range(8)]
    hi, lo = tree(pieces)
    hi, lo = jnp.transpose(hi), jnp.transpose(lo)
    total = rows_sum(hi)
    row = total[0] + (total[1] + rows_sum(lo)[0])
    row_ref[...] = jnp.broadcast_to(row[0:1], row_ref.shape)


def sums(q, north, south, east, west, faces, token):
    rows, cols = q.shape
    return pl.pallas_call(
        sums_kernel,
        out_shape=(shape(LANES, LANES), shape(9, rows + 16, cols + LANES), shape(*token.shape)),
        in_specs=[VMEM] * 7,
        out_specs=(VMEM,) * 3,
        scratch_shapes=[pltpu.VMEM((8 * LANES, LANES), F32)],
        compiler_params=params(8),
        name="krylov_sums",
    )(q, north, south, east, west, faces, token)


def two_prod(a, b):
    p = a * b
    t = 4097.0 * a
    ah = t - (t - a)
    al = a - ah
    t = 4097.0 * b
    bh = t - (t - b)
    bl = b - bh
    return p, ((ah * bh - p) + (ah * bl + al * bh)) + al * bl


def quick(s, e):
    t = s + e
    return t, e - (t - s)


def pair_add(x, y):
    s, e = two_sum(x[0], y[0])
    return quick(s, e + (x[1] + y[1]))


def pair_neg(x):
    return -x[0], -x[1]


def pair_mul(x, y):
    p, e = two_prod(x[0], y[0])
    return quick(p, e + (x[0] * y[1] + x[1] * y[0]))


def pair_div(x, y):
    first = x[0] / y[0]
    p, e = two_prod(first, y[0])
    rest = ((x[0] - p) - e) + (x[1] - first * y[1])
    return quick(first, rest / y[0])


def minor(a, b, c, d):
    return pair_add(pair_mul(a, b), pair_neg(pair_mul(c, d)))


def pair_sum3(a, b, c):
    return pair_add(pair_add(a, b), c)


def small_solve(g, b):
    g00, g10, g11, g20, g21, g22 = g
    c00, c01, c02 = minor(g11, g22, g21, g21), minor(g20, g21, g10, g22), minor(g10, g21, g20, g11)
    c11, c12, c22 = minor(g00, g22, g20, g20), minor(g10, g20, g00, g21), minor(g00, g11, g10, g10)
    det = pair_sum3(pair_mul(g00, c00), pair_mul(g10, c01), pair_mul(g20, c02))
    three = det[0] > 1e-8 * (c22[0] * g22[0])
    two = c22[0] > 1e-8 * (g00[0] * g11[0])
    three = three & two
    rows = ((c00, c01, c02), (c01, c11, c12), (c02, c12, c22))
    full = [pair_div(pair_sum3(*[pair_mul(m, v) for m, v in zip(row, b)]), det)[0] for row in rows]
    half = [
        pair_div(minor(g11, b[0], g10, b[1]), c22)[0],
        pair_div(minor(g00, b[1], g10, b[0]), c22)[0],
        jnp.zeros_like(det[0]),
    ]
    alone = [b[0][0] / g00[0], half[2], half[2]]
    return [jnp.where(three, x, jnp.where(two, y, z)) for x, y, z in zip(full, half, alone)]


def coefficients(every_ref):
    total = quick(*rows_sum(every_ref[...]))

    def pick(x, at):
        return tuple(jnp.broadcast_to(v[:, at : at + 1], (8, LANES)) for v in x)

    def scaled(x, at):
        by = 1.0 / jnp.broadcast_to(x[0][:, at : at + 1], (8, LANES))
        p, e = two_prod(x[0], by)
        return quick(p, e + x[1] * by)

    first = scaled(total, 81)
    first = [pick(first, 81 + m) for m in range(9)]
    c = small_solve(first[:6], first[6:])
    terms = []
    for i in range(3):
        for j in range(3):
            shift = (LANES - 9 * (3 * i + j)) % LANES
            row = tuple(pltpu.roll(v, shift, 1) if shift else v for v in total)
            terms.append(pair_mul(row, two_prod(c[i], c[j])))
    while len(terms) > 1:
        odd = terms[len(terms) // 2 * 2 :]
        terms = [pair_add(terms[i], terms[i + 1]) for i in range(0, len(terms) - 1, 2)] + odd
    second = scaled(terms[0], 0)
    second = [pick(second, m) for m in range(9)]
    return c, small_solve(second[:6], second[6:])


def tracer_kernel(steric_ref, every_ref, field_ref, face_ref, far_ref, side_ref, mu_ref, rho_ref, tall_ref, sems):
    levels, rows, cols = mu_ref.shape

    def copy(level):
        return pltpu.make_async_copy(far_ref.at[level], tall_ref.at[level], sems.at[level])

    for level in range(levels):
        copy(level).start()
    high, wide = rows + 8, cols + LANES

    def trim(v):
        edge = jnp.where(iota((8, wide), 0) < 4, v[rows : rows + 8], v[rows + 8 :])
        return jnp.concatenate([v[:rows], edge], axis=0)

    c, e = coefficients(every_ref)
    c, e = [[jnp.broadcast_to(v[0:1, 0:1], (1, 1)) for v in part] for part in (c, e)]
    w = [trim(field_ref[i]) for i in range(3)]
    ocean = trim(face_ref[5])
    rho_1 = c[0] * w[0] + c[1] * w[1] + c[2] * w[2]
    rho_0 = e[0] * (ocean * rho_1)
    for k in (1, 2):
        v = [trim(field_ref[2 + k + 2 * i]) for i in range(3)]
        rho_0 = rho_0 + e[k] * (c[0] * v[0] + c[1] * v[1] + c[2] * v[2])
    rho_ref[...] = rho_0[:rows, :cols]

    def one_level(level, carry):
        copy(level).wait()
        height = steric_ref[level]
        full = lambda at: jnp.concatenate([tall_ref[level, at], side_ref[at, level]], axis=1)
        g = ocean * (full(0) + height * rho_1)
        dx = g - pltpu.roll(g, wide - 1, 1)
        dy = g - pltpu.roll(g, high - 1, 0)
        mu = g - (
            full(1) * dx + pltpu.roll(full(2) * dx, 1, 1) + full(3) * dy + pltpu.roll(full(4) * dy, 1, 0)
        )
        g = ocean * (mu + height * rho_0)
        dx = (g - pltpu.roll(g, wide - 1, 1))[:rows]
        dy = (g - pltpu.roll(g, high - 1, 0))[:, :cols]
        back_x = pltpu.roll(full(5)[:rows] * dx, 1, 1)[:, :cols]
        back_y = pltpu.roll(tall_ref[level, 6] * dy, 1, 0)[:rows]
        mu_ref[level] = g[:rows, :cols] - (
            tall_ref[level, 7, 0:rows, :] * dx[:, :cols] + back_x + tall_ref[level, 8, 0:rows, :] * dy[:rows] + back_y
        )
        return carry

    lax.fori_loop(0, levels, one_level, 0)


def tracers(steric, every, fields, faces, tall, side):
    levels, count, high, cols = tall.shape
    rows = high - 8
    return pl.pallas_call(
        tracer_kernel,
        out_shape=(shape(levels, rows, cols), shape(rows, cols)),
        in_specs=[SCALAR] + [VMEM] * 3 + [HBM, VMEM],
        out_specs=(VMEM, VMEM),
        scratch_shapes=[pltpu.VMEM((levels, count, high, cols), F32), pltpu.SemaphoreType.DMA((levels,))],
        compiler_params=params(20),
        name="tracer_steps",
    )(steric, every, fields, faces, *far((tall,)), side)


def beside(cells, axis, step):
    count = lax.axis_size(axis)
    return lax.ppermute(cells, axis, [((i + step) % count, i) for i in range(count)])


def tracer_fields(keep, lam, zonal_1, merid_1, zonal_0, merid_0, mix_x, mix_y):
    flow_x, flow_y = 0.5 * zonal_1, 0.5 * merid_1
    past_x, past_y = 0.5 * zonal_0, 0.5 * merid_0
    return (
        lam,
        flow_x + mix_x,
        flow_x - mix_x,
        keep * (flow_y + mix_y),
        keep * (flow_y - mix_y),
        past_x - mix_x,
        keep * (past_y - mix_y),
        past_x + mix_x,
        keep * (past_y + mix_y),
    )


def surface_fields(keep, diag_ref, east_ref, north_ref, land_ref, rows):
    return diag_ref[rows], east_ref[rows], keep * north_ref[rows], land_ref[rows].astype(F32)


UP = (0, 1, 2, 3)
DOWN = (0, 1, 2, 3, 4, 6)
SIDE = (0, 1, 2, 3, 4, 5)


def kept(token_ref, first, count, rows, cols):
    last = jnp.concatenate([token_ref[0:1, :]] * (cols // LANES), axis=1)
    return jnp.where((iota((count, cols), 0) + first == rows - 1) & (last == 1.0), 0.0, 1.0)


def rows_kernel(token_ref, lam_ref, zonal_ref, merid_ref, mix_x_ref, mix_y_ref, *refs):
    surface_refs, (up_ref, down_ref, next_ref, held_ref, sems) = refs[:4], refs[4:]
    levels, rows, cols = lam_ref.shape
    next_ref[...] = token_ref[...]
    copies = []
    for first in (0, rows - 8):
        block = pl.ds(first, 8)
        for source in (
            lam_ref.at[:, block, :],
            zonal_ref.at[1, :, block, :],
            merid_ref.at[1, :, block, :],
            mix_x_ref.at[:, block, :],
            mix_y_ref.at[:, block, :],
            merid_ref.at[0, :, block, :],
        ):
            at = len(copies)
            copies.append(pltpu.make_async_copy(source, held_ref.at[at], sems.at[at]))
            copies[-1].start()
    for part, (out_ref, picks, first, take) in enumerate(((up_ref, UP, 0, 0), (down_ref, DOWN, rows - 8, 6))):
        keep = kept(token_ref, first, 8, rows, cols)
        base = 2 * len(picks) * levels
        for at, field in enumerate(surface_fields(keep, *surface_refs, slice(first, first + 8))):
            out_ref[base + 8 * at : base + 8 * at + 8, :] = field
        for copy in copies[6 * part : 6 * part + 6]:
            copy.wait()
        for level in range(levels):
            lam, zonal_1, merid_1, mix_x, mix_y, merid_0 = [held_ref[6 * part + i, level] for i in range(6)]
            fields = tracer_fields(keep, lam, zonal_1, merid_1, zonal_1, merid_0, mix_x, mix_y)
            for at, pick in enumerate(picks):
                base = 2 * (at * levels + level)
                out_ref[base : base + 2, :] = fields[pick][take : take + 2]


def edge_rows(n_ref, s_ref, pick, levels, level, cols):
    zero = lambda count: jnp.zeros((count, cols), F32)
    north = zero(2)
    if pick in UP:
        base = 2 * (UP.index(pick) * levels + level)
        north = n_ref[base : base + 2, :]
    south = zero(2)
    if pick in DOWN:
        base = 2 * (DOWN.index(pick) * levels + level)
        south = s_ref[base : base + 2, :]
    return jnp.concatenate([north, zero(4), south], axis=0)


def halves(tall):
    lane = iota((tall.shape[0], LANES), 1)
    return jnp.where(lane < LANES // 2, tall[:, :LANES], tall[:, -LANES:])


GROUP = 4


def cols_kernel(token_ref, lam_ref, zonal_ref, merid_ref, mix_x_ref, mix_y_ref, *refs):
    surface_refs, height_refs, (n_ref, s_ref) = refs[:4], refs[4:6], refs[6:8]
    out_ref, far_ref, face_ref, height_ref, held_ref, flat_ref, tall_ref, sems, far_sems = refs[8:]
    levels, rows, cols = lam_ref.shape
    copies = []
    for group in range(levels // GROUP):
        block = pl.ds(group * GROUP, GROUP)
        for i, source in enumerate(
            (
                lam_ref.at[block],
                zonal_ref.at[1, block],
                merid_ref.at[1, block],
                zonal_ref.at[0, block],
                merid_ref.at[0, block],
                mix_x_ref.at[block],
                mix_y_ref.at[block],
            )
        ):
            copies.append(pltpu.make_async_copy(source, held_ref.at[i, block], sems.at[len(copies)]))
            copies[-1].start()
    keep = kept(token_ref, 0, rows, rows, cols)
    high = rows + 8
    used = 8 * len(SIDE)
    blocks = levels * high // LANES
    base = blocks * used
    up, down = 2 * len(UP) * levels, 2 * len(DOWN) * levels
    for at, field in enumerate(surface_fields(keep, *surface_refs, slice(0, rows))):
        tall = jnp.concatenate(
            [field, n_ref[up + 8 * at : up + 8 * at + 8, :], s_ref[down + 8 * at : down + 8 * at + 8, :]], axis=0
        )
        face_ref[at] = tall
        out_ref[base : base + rows + 16, :] = halves(tall)
        base += rows + 16
    for at, ref in enumerate(height_refs):
        height_ref[at] = ref[...]
    lane = iota((high, LANES), 1)
    far = []
    for level in range(levels):
        if level % GROUP == 0:
            for copy in copies[7 * (level // GROUP) : 7 * (level // GROUP) + 7]:
                copy.wait()
        fields = tracer_fields(keep, *[held_ref[i, level] for i in range(7)])
        mixed = jnp.zeros((high, LANES), F32)
        for pick, field in enumerate(fields):
            tall_ref[level, pick, 0:rows, :] = field
            edge = edge_rows(n_ref, s_ref, pick, levels, level, cols)
            tall_ref[level, pick, rows:high, :] = edge
            if pick in SIDE:
                at = SIDE.index(pick)
                tall = jnp.concatenate([field, edge], axis=0)
                mixed = jnp.where(lane // 8 == at, pltpu.roll(halves(tall), 4 + 8 * at, 1), mixed)
        flat_ref[level * high : (level + 1) * high, :] = mixed
        far.append(pltpu.make_async_copy(tall_ref.at[level], far_ref.at[level], far_sems.at[level]))
        far[-1].start()
    for b in range(blocks):
        turned = jnp.transpose(flat_ref[b * LANES : (b + 1) * LANES, :])
        out_ref[b * used : (b + 1) * used, :] = turned[:used]
    for copy in far:
        copy.wait()


def side_kernel(e_ref, w_ref, token_ref, side_ref, flat_ref):
    levels, high = side_ref.shape[1:3]
    used = 8 * len(SIDE)
    blocks = levels * high // LANES
    western = iota((used, LANES), 0) % 8 < 4
    for b in range(blocks):
        at = slice(b * used, (b + 1) * used)
        both = jnp.where(western, w_ref[at, :], e_ref[at, :])
        both = jnp.concatenate([both, jnp.zeros((LANES - used, LANES), F32)], axis=0)
        flat_ref[b * LANES : (b + 1) * LANES, :] = jnp.transpose(both)
    for level in range(levels):
        mixed = flat_ref[level * high : (level + 1) * high, :]
        for at in range(len(SIDE)):
            side_ref[at, level] = pltpu.roll(mixed, LANES - 4 - 8 * at, 1)


def face_halo_kernel(base, token_ref, tall_ref, e_ref, w_ref, face_ref):
    high = tall_ref.shape[1]
    eastern = iota((high, LANES), 1) < LANES // 2
    full = []
    for at in range(4):
        here = slice(base + at * high, base + (at + 1) * high)
        full.append(jnp.concatenate([tall_ref[at], jnp.where(eastern, e_ref[here, :], w_ref[here, :])], axis=1))
    diag, east, north, ocean = full
    west, south = pltpu.roll(east, 1, 1), pltpu.roll(north, 1, 0)
    face_ref[0] = (1.0 + diag) + east + west + north + south
    for at, field in enumerate((east, west, north, south, ocean)):
        face_ref[1 + at] = field


def edges_to_ty(token, tracer, surface):
    levels, rows, cols = tracer[0].shape
    up, down = 2 * len(UP) * levels + 32, 2 * len(DOWN) * levels + 32
    to_south, to_north, token = pl.pallas_call(
        rows_kernel,
        out_shape=(shape(up, cols), shape(down, cols), shape(*token.shape)),
        in_specs=[VMEM] + [HBM] * 5 + [VMEM] * 4,
        out_specs=(VMEM,) * 3,
        scratch_shapes=[pltpu.VMEM((12, levels, 8, cols), F32), pltpu.SemaphoreType.DMA((12,))],
        compiler_params=params(8),
        name="edge_rows",
    )(token, *far(tracer), *far(surface))
    return (beside(to_south, "ty", 1), beside(to_north, "ty", -1)), token


def edges_to_tx(token, tracer, surface, heights, north, south):
    levels, rows, cols = tracer[0].shape
    high = rows + 8
    side_rows = 8 * len(SIDE) * levels * high // LANES + 4 * (rows + 16)
    sides, tall, faces, heights = pl.pallas_call(
        cols_kernel,
        out_shape=(
            shape(side_rows, LANES),
            far_shape(levels, 9, high, cols),
            shape(4, rows + 16, cols),
            shape(2, rows, cols),
        ),
        in_specs=[VMEM] + [HBM] * 5 + [VMEM] * 8,
        out_specs=(VMEM, HBM, VMEM, VMEM),
        scratch_shapes=[
            pltpu.VMEM((7, levels, rows, cols), F32),
            pltpu.VMEM((levels * high, LANES), F32),
            pltpu.VMEM((levels, 9, high, cols), F32),
            pltpu.SemaphoreType.DMA((7 * levels // GROUP,)),
            pltpu.SemaphoreType.DMA((levels,)),
        ],
        compiler_params=params(24),
        name="edge_columns",
    )(token, *far(tracer), *far(surface), *far(heights), north, south)
    return (beside(sides, "tx", 1), beside(sides, "tx", -1)), tall, faces, heights


def faces_with_halo(token, tall, east, west):
    count, high, cols = tall.shape
    return pl.pallas_call(
        functools.partial(face_halo_kernel, east.shape[0] - count * high),
        out_shape=shape(6, high, cols + LANES),
        in_specs=[VMEM] * 4,
        out_specs=VMEM,
        compiler_params=params(6),
        name="surface_halos",
    )(token, tall, east, west)


def tracer_sides(token, levels, rows, east, west):
    high = rows + 8
    return pl.pallas_call(
        side_kernel,
        out_shape=shape(len(SIDE), levels, high, LANES),
        in_specs=[VMEM] * 3,
        out_specs=VMEM,
        scratch_shapes=[pltpu.VMEM((levels * high, LANES), F32)],
        compiler_params=params(8),
        name="tracer_halos",
    )(east, west, token)


def on_device(
    lam_tracer,
    lam_eta,
    land,
    zonal_flow,
    merid_flow,
    zonal_mixing,
    merid_mixing,
    surface_east,
    surface_north,
    surface_diag,
    steric,
    eta_saved,
    obs_sla,
    obs_weight,
    obs_tile,
    obs_start,
    obs_count,
):
    levels, rows, cols = lam_tracer.shape
    n_rows = lax.axis_size("ty")
    devices = n_rows * lax.axis_size("tx")
    capacity = 2 * obs_sla.shape[0] // devices
    token = jnp.full((8, LANES), lax.axis_index("ty") == n_rows - 1, F32)
    tracer = (lam_tracer, zonal_flow, merid_flow, zonal_mixing, merid_mixing)
    surface = (surface_diag, surface_east, surface_north, land)
    around_ty, token = edges_to_ty(token, tracer, surface)
    ranked = pack(obs_sla, obs_weight, obs_tile, obs_start, obs_count, token, capacity)
    sent, token = placed(*ranked, token, around_ty, capacity)
    got = lax.all_to_all(
        sent.reshape(devices, 1, -1), AXES, split_axis=0, concat_axis=0, tiled=True
    ).reshape(sent.shape)
    around_tx, tall, faces, heights = edges_to_tx(token, tracer, surface, (lam_eta, eta_saved), *around_ty)
    rhs, token = unpack(got, heights, faces, token, capacity)
    faces = faces_with_halo(token, faces, *around_tx)
    north, south = beside(rhs[:8], "ty", 1), beside(rhs[-8:], "ty", -1)
    side = halves(jnp.concatenate([rhs, north, south], axis=0))
    east, west = beside(side, "tx", 1), beside(side, "tx", -1)
    mine, krylov_fields, token = sums(rhs, north, south, east, west, faces, token)
    every = lax.all_to_all(
        mine.reshape(devices, 1, LANES), AXES, split_axis=0, concat_axis=0, tiled=True
    ).reshape(devices, LANES)
    sides = tracer_sides(token, levels, rows, *around_tx)
    return tracers(steric, every, krylov_fields, faces, tall, sides)


def solution(mesh):
    in_specs = (
        P(None, "ty", "tx"),
        P("ty", "tx"),
        P("ty", "tx"),
        P(None, None, "ty", "tx"),
        P(None, None, "ty", "tx"),
        P(None, "ty", "tx"),
        P(None, "ty", "tx"),
        P("ty", "tx"),
        P("ty", "tx"),
        P("ty", "tx"),
        P(),
        P("ty", "tx"),
        P(AXES, None),
        P(AXES, None),
        P(AXES, None),
        P(AXES),
        P(AXES),
    )
    out_specs = (P(None, "ty", "tx"), P("ty", "tx"))
    return jax.shard_map(
        on_device, mesh=mesh, in_specs=in_specs, out_specs=out_specs, check_vma=False
    )
```

time: 136 us -> 94.6 us (0.70)
  local copies, waits for them, and re-layouts: 36.1 us -> 0.04 us
  other arithmetic: 27.7 us -> 0.01 us
  waiting for transfers between devices: 19.4 us -> 35.4 us
  Pallas kernels: 14.6 us -> 24 us
  starting transfers between devices: 36.7 us -> 33.9 us
    all_to_all x1, waiting for transfers between devices: 0.01 us -> 20.8 us  [on_device(): lax.all_to_all(sent.reshape(devices, 1, -1), AXES, split_axis=0, concat_a...]
    another operation x8 -> x0, other arithmetic: 12.9 us -> none  [the longest x2 6.12 us: on_device(): jnp.stack([fields[1], west_of(fields[2]), fields[3], south_of(fields[4])])]
    reshape x12 -> x0, local copies, waits for them, and re-layouts: 11.1 us -> none  [the longest x8 8.93 us: strip(): return jnp.moveaxis(sent.reshape(flat.shape), 0, -1)]
    pallas_call x4 -> x9, Pallas kernels: 14.6 us -> 24 us  [the longest x1 8 us: tracers(): pl.pallas_call(tracer_kernel, out_shape=(shape(levels, rows, cols), shape...]
    transpose x6 -> x0, local copies, waits for them, and re-layouts: 9.35 us -> none  [strip(): flat = jnp.moveaxis(cells, -1, 0)]
    concatenate x6 -> x0, other arithmetic: 8.42 us -> none  [the longest x2 4.52 us: stretched(): return jnp.concatenate([field, east, gap, west], axis=-1)]
    slice x11 -> x0, local copies, waits for them, and re-layouts: 8.26 us -> none  [the longest x4 3.25 us: west_of(): return jnp.roll(v, 1, axis=-1)]
    unnamed x52 -> x14, local copies, waits for them, and re-layouts: 7.08 us -> 0.03 us
  transfers between devices with their start and end apart: 14 -> 10, of which waited for: 3 -> 5; matrix products, arithmetic and copies ran while one was open for 40% -> 0% of each run, Pallas kernels for 3% -> 9%
where the time goes in v3:
time: 94.6 us; the launch traced here: 94.2 us
  waiting for transfers between devices  35.4 us (37%)
  starting transfers between devices  33.9 us (36%)
  Pallas kernels  24 us (25%)
    all_to_all x1, waiting for transfers between devices, on_device(): lax.all_to_all(sent.reshape(devices, 1, -1), AXES, split_axis=0, concat_a...  20.8 us
    ppermute x8, starting transfers between devices, beside(): lax.ppermute(cells, axis, [((i + step) % count, i) for i in range(count)])  14.6 us
    all_to_all x1, starting transfers between devices, on_device(): lax.all_to_all(mine.reshape(devices, 1, LANES), AXES, split_axis=0, conca...  9.95 us
    all_to_all x1, starting transfers between devices, on_device(): lax.all_to_all(sent.reshape(devices, 1, -1), AXES, split_axis=0, concat_a...  9.36 us
    all_to_all x1, waiting for transfers between devices, on_device(): lax.all_to_all(mine.reshape(devices, 1, LANES), AXES, split_axis=0, conca...  8.87 us
    pallas_call x1, Pallas kernels, tracers(): pl.pallas_call(tracer_kernel, out_shape=(shape(levels, rows, cols), shape...  8 us
    ppermute x8, waiting for transfers between devices, beside(): lax.ppermute(cells, axis, [((i + step) % count, i) for i in range(count)])  5.78 us
    pallas_call x1, Pallas kernels, edges_to_tx(): pl.pallas_call(cols_kernel, out_shape=(shape(side_rows, LANES), far_shape...  5.15 us
  transfers between devices with their start and end apart: 10, of which 5 were waited for; matrix products, arithmetic and copies ran while one was open for 0% of the time, Pallas kernels for 9%

profile of v3, /device:TPU:1, one launch (start us, length us, event | category | flops | bytes accessed | tf_op | source)
XLA Modules:
  0.0 94.2 jit_solution(14155127600195075077)
XLA Ops:
  0.6 0.0 copy-start.4
  0.6 0.0 copy-start.3
  0.7 0.0 copy-start.2
  0.7 0.0 copy-start.1
  0.7 0.0 copy-start
  0.7 2.5 %edge_rows.1 = (f32[160,256]{1,0:T(8,128)S(1)}, f32[224,256]{1,0:T(8,128)S(1)}, f32[8,128]{1,0:T(8,128)S(1)}) custom-call(f32[8,128]{1,0:T(8,128)S(1)} %broadcast_in_dim.3.token_ref, f32[16,32,256]{2,1,0:T(8,128)} %lam_ref.3, f32[2,16,32,256]{3,2,1,0:T(8,128)} %zonal_ref.3, f32[2,16,32,256]{3,2,1,0:T(8,128)} %merid_ref.3, f32[16,32,256]{2,1,0:T(8,128)} %mix_x_ref.3, ...), custom_call_target="tpu_custom_call" | custom-call | tf_op jit(solution)/shard_map/edge_rows/pallas_call | solution.py:647
  3.2 3.0 %collective-permute-start.1 = (f32[224,256]{1,0:T(8,128)S(1)}, f32[224,256]{1,0:T(8,128)S(1)}, u32[]{:S(2)}, u32[]{:S(2)}) collective-permute-start(f32[224,256]{1,0:T(8,128)S(1)} %get-tuple-element.24), channel_id=1, source_target_pairs={{112,0},{0,16},{16,32},{32,48},{48,64},{64,80},{80,96},{96,112},{1... | collective-permute-start | bytes 688136 | tf_op jit(solution)/shard_map/ppermute | solution.py:466
  6.3 0.0 collective-permute-start
  6.3 0.0 copy-done.4
  6.3 0.0 copy-done.3
  6.3 0.0 copy-done.2
  6.3 0.0 copy-done.1
  6.3 0.0 copy-done
  6.3 1.7 %rank_segments.1 = (bf16[1024,512]{1,0:T(8,128)(2,1)S(1)}, s32[8,128]{1,0:T(8,128)S(1)}, f32[128,128]{1,0:T(8,128)S(1)}) custom-call(f32[1024,128]{1,0:T(8,128)S(1)} %copy-done, f32[1024,128]{1,0:T(8,128)S(1)} %copy-done.1, s32[8,128]{1,0:T(8,128)S(1)} %bitcast.10, s32[8,128]{1,0:T(8,128)S(1)} %bitcast.11, s32[8,128]{1,0:T(8,128)S(1)} %bitcast.12, ...), custom_call_target="tpu_custom_call" | custom-call | tf_op jit(solution)/shard_map/rank_segments/pallas_call | solution.py:116
  8.0 3.3 %collective-permute-done.north_ref.refs_6_ = f32[160,256]{1,0:T(8,128)S(1)} collective-permute-done((f32[160,256]{1,0:T(8,128)S(1)}, f32[160,256]{1,0:T(8,128)S(1)}, u32[]{:S(2)}, u32[]{:S(2)}) %collective-permute-start) | collective-permute-done | bytes 163872 | tf_op jit(solution)/shard_map/ppermute | solution.py:466
  11.3 0.0 collective-permute-done.1.south_ref.refs_7_
  11.3 3.2 %place_segments.1 = (f32[4224,128]{1,0:T(8,128)}, f32[8,128]{1,0:T(8,128)S(1)}) custom-call(bf16[1024,512]{1,0:T(8,128)(2,1)S(1)} %get-tuple-element.20.data_ref, s32[8,128]{1,0:T(8,128)S(1)} %get-tuple-element.21.place_ref, f32[128,128]{1,0:T(8,128)S(1)} %get-tuple-element.22.meta_ref, f32[8,128]{1,0:T(8,128)S(1)} %get-tuple-element.19.token_ref, ...), custom_call_target="tpu_custom_call" | custom-call | tf_op jit(solution)/shard_map/place_segments/pallas_call | solution.py:139
  14.5 9.4 %all-to-all-start = ((f32[128,1,4224]{2,1,0:T(1,128)}), f32[128,1,4224]{2,1,0:T(1,128)S(1)}, u32[]{:S(2)}, u32[]{:S(2)}) async-start(f32[128,1,4224]{2,1,0:T(1,128)} %bitcast.13), calls=%async_computation | async-start | bytes 4325376 | tf_op jit(solution)/shard_map/all_to_all | solution.py:740
  23.9 5.1 %edge_columns.1 = (f32[432,128]{1,0:T(8,128)S(1)}, f32[16,9,40,256]{3,2,1,0:T(8,128)}, f32[4,48,256]{2,1,0:T(8,128)S(1)}, f32[2,32,256]{2,1,0:T(8,128)S(1)}) custom-call(f32[8,128]{1,0:T(8,128)S(1)} %get-tuple-element.26.token_ref, f32[16,32,256]{2,1,0:T(8,128)} %lam_ref.3, f32[2,16,32,256]{3,2,1,0:T(8,128)} %zonal_ref.3, f32[2,16,32,256]{3,2,1,0:T(8,128)} %merid_ref.3, ...), custom_call_target="tpu_custom_call" | custom-call | tf_op jit(solution)/shard_map/edge_columns/pallas_call | solution.py:663
  29.0 1.5 %collective-permute-start.7 = (f32[432,128]{1,0:T(8,128)S(1)}, f32[432,128]{1,0:T(8,128)S(1)}, u32[]{:S(2)}, u32[]{:S(2)}) collective-permute-start(f32[432,128]{1,0:T(8,128)S(1)} %get-tuple-element.31), channel_id=1, source_target_pairs={{15,0},{0,1},{1,2},{2,3},{3,4},{4,5},{5,6},{6,7},{7,8},{8,9},{9,10... | collective-permute-start | bytes 663560 | tf_op jit(solution)/shard_map/ppermute | solution.py:466
  30.5 3.5 %collective-permute-start.6 = (f32[432,128]{1,0:T(8,128)S(1)}, f32[432,128]{1,0:T(8,128)S(1)}, u32[]{:S(2)}, u32[]{:S(2)}) collective-permute-start(f32[432,128]{1,0:T(8,128)S(1)} %get-tuple-element.31), channel_id=1, source_target_pairs={{1,0},{2,1},{3,2},{4,3},{5,4},{6,5},{7,6},{8,7},{9,8},{10,9},{11,1... | collective-permute-start | bytes 663560 | tf_op jit(solution)/shard_map/ppermute | solution.py:466
  34.0 20.8 %all-to-all-done = f32[128,1,4224]{2,1,0:T(1,128)S(1)} async-done(((f32[128,1,4224]{2,1,0:T(1,128)}), f32[128,1,4224]{2,1,0:T(1,128)S(1)}, u32[]{:S(2)}, u32[]{:S(2)}) %all-to-all-start) | async-done | bytes 2162720 | tf_op jit(solution)/shard_map/all_to_all | solution.py:740
  54.7 1.0 %forcing.1 = (f32[32,256]{1,0:T(8,128)S(1)}, f32[8,128]{1,0:T(8,128)S(1)}) custom-call(f32[4224,128]{1,0:T(8,128)S(1)} %bitcast.9, f32[2,32,256]{2,1,0:T(8,128)S(1)} %get-tuple-element.27.height_ref, f32[4,48,256]{2,1,0:T(8,128)S(1)} %get-tuple-element.28.face_ref.tall_ref, f32[8,128]{1,0:T(8,128)S(1)} %get-tuple-element.26.token_ref), custom_call_target="tpu_custom_call" | custom-call | tf_op jit(solution)/shard_map/forcing/pallas_call | solution.py:196
  55.7 0.6 collective-permute-start.2
  56.3 0.0 copy-start.5
  56.3 1.1 %collective-permute-start.3 = (f32[8,256]{1,0:T(8,128)S(1)}, f32[8,256]{1,0:T(8,128)S(1)}, u32[]{:S(2)}, u32[]{:S(2)}) collective-permute-start(f32[8,256]{1,0:T(8,128)S(1)} %get-tuple-element.36), channel_id=1, source_target_pairs={{112,0},{0,16},{16,32},{32,48},{48,64},{64,80},{80,96},{96,112},{1... | collective-permute-start | bytes 24584 | tf_op jit(solution)/shard_map/ppermute | solution.py:466
  57.5 1.3 %collective-permute-done.2.north_ref = f32[8,256]{1,0:T(8,128)S(1)} collective-permute-done((f32[8,256]{1,0:T(8,128)S(1)}, f32[8,256]{1,0:T(8,128)S(1)}, u32[]{:S(2)}, u32[]{:S(2)}) %collective-permute-start.2) | collective-permute-done | bytes 8224 | tf_op jit(solution)/shard_map/ppermute | solution.py:466
  58.8 0.0 collective-permute-done.3.south_ref
  58.8 0.7 collective-permute-start.5
  59.5 4.1 %collective-permute-start.4 = (f32[48,128]{1,0:T(8,128)S(1)}, f32[48,128]{1,0:T(8,128)S(1)}, u32[]{:S(2)}, u32[]{:S(2)}) collective-permute-start(f32[48,128]{1,0:T(8,128)S(1)} %slice_select_fusion), channel_id=1, source_target_pairs={{1,0},{2,1},{3,2},{4,3},{5,4},{6,5},{7,6},{8,7},{9,8},{10,9},{11,1... | collective-permute-start | bytes 73736 | tf_op jit(solution)/shard_map/ppermute | solution.py:466
  63.7 0.0 collective-permute-done.7.w_ref
  63.7 0.0 collective-permute-done.6.e_ref
  63.7 0.1 surface_halos.1.face_ref
  63.8 1.1 %collective-permute-done.5.west_ref = f32[48,128]{1,0:T(8,128)S(1)} collective-permute-done((f32[48,128]{1,0:T(8,128)S(1)}, f32[48,128]{1,0:T(8,128)S(1)}, u32[]{:S(2)}, u32[]{:S(2)}) %collective-permute-start.5) | collective-permute-done | bytes 24608 | tf_op jit(solution)/shard_map/ppermute | solution.py:466
  64.9 0.0 collective-permute-done.4.east_ref
  64.9 1.8 %krylov_sums.1 = (f32[128,128]{1,0:T(8,128)}, f32[9,48,384]{2,1,0:T(8,128)S(1)}, f32[8,128]{1,0:T(8,128)S(1)}) custom-call(f32[32,256]{1,0:T(8,128)S(1)} %get-tuple-element.29.q_ref, f32[8,256]{1,0:T(8,128)S(1)} %collective-permute-done.2.north_ref, f32[8,256]{1,0:T(8,128)S(1)} %collective-permute-done.3.south_ref, ...), custom_call_target="tpu_custom_call" | custom-call | tf_op jit(solution)/shard_map/krylov_sums/pallas_call | solution.py:299
  66.7 9.9 %all-to-all-start.1 = ((f32[128,1,128]{2,1,0:T(1,128)}), f32[128,1,128]{2,1,0:T(1,128)}, u32[]{:S(2)}, u32[]{:S(2)}) async-start(f32[128,1,128]{2,1,0:T(1,128)} %bitcast.6), calls=%async_computation.1 | async-start | bytes 131072 | tf_op jit(solution)/shard_map/all_to_all | solution.py:750
  76.6 0.7 tracer_halos.1.side_ref
  77.3 8.9 %all-to-all-done.1 = f32[128,1,128]{2,1,0:T(1,128)} async-done(((f32[128,1,128]{2,1,0:T(1,128)}), f32[128,1,128]{2,1,0:T(1,128)}, u32[]{:S(2)}, u32[]{:S(2)}) %all-to-all-start.1) | async-done | bytes 65568 | tf_op jit(solution)/shard_map/all_to_all | solution.py:750
  86.2 0.0 copy-done.5
  86.2 8.0 %tracer_steps.1 = (f32[16,32,256]{2,1,0:T(8,128)}, f32[32,256]{1,0:T(8,128)}) custom-call(f32[16]{0:T(128)S(1)} %copy-done.5, f32[128,128]{1,0:T(8,128)} %bitcast.7.every_ref, f32[9,48,384]{2,1,0:T(8,128)S(1)} %get-tuple-element.33.field_ref, f32[6,48,384]{2,1,0:T(8,128)S(1)} %surface_halos.1.face_ref, f32[16,9,40,256]{3,2,1,0:T(8,128)} %get-tuple-element.34.far_ref, ...), custom_call_target="tpu_custom_call" | custom-call | tf_op jit(solution)/shard_map/tracer_steps/pallas_call | solution.py:453
  (7 shorter events, 0.0 us)
Async XLA Ops:
  0.6 5.6 %copy-start.4 = (s32[1024]{0:T(1024)S(1)}, s32[1024]{0:T(1024)}, u32[]{:S(2)}) copy-start(s32[1024]{0:T(1024)} %param.33) | copy-start | bytes 12292
  0.6 5.6 %copy-start.3 = (s32[1024]{0:T(1024)S(1)}, s32[1024]{0:T(1024)}, u32[]{:S(2)}) copy-start(s32[1024]{0:T(1024)} %param.32) | copy-start | bytes 12292
  0.7 5.6 %copy-start.2 = (s32[1024,1]{0,1:T(1,128)S(1)}, s32[1024,1]{0,1:T(1,128)}, u32[]{:S(2)}) copy-start(s32[1024,1]{0,1:T(1,128)} %param.31) | copy-start | bytes 12292
  0.7 5.6 %copy-start.1 = (f32[1024,128]{1,0:T(8,128)S(1)}, f32[1024,128]{1,0:T(8,128)}, u32[]{:S(2)}) copy-start(f32[1024,128]{1,0:T(8,128)} %weight_ref.1) | copy-start | bytes 1572868
  0.7 5.6 %copy-start = (f32[1024,128]{1,0:T(8,128)S(1)}, f32[1024,128]{1,0:T(8,128)}, u32[]{:S(2)}) copy-start(f32[1024,128]{1,0:T(8,128)} %sla_ref.1) | copy-start | bytes 1572868
  3.2 8.1 %collective-permute-start.1 = (f32[224,256]{1,0:T(8,128)S(1)}, f32[224,256]{1,0:T(8,128)S(1)}, u32[]{:S(2)}, u32[]{:S(2)}) collective-permute-start(f32[224,256]{1,0:T(8,128)S(1)} %get-tuple-element.24), channel_id=1, source_target_pairs={{112,0},{0,16},{16,32},{32,48},{48,64},{64,80},{80,96},{96,112},{1... | collective-permute-start | bytes 688136 | tf_op jit(solution)/shard_map/ppermute | solution.py:466
  6.3 5.0 %collective-permute-start = (f32[160,256]{1,0:T(8,128)S(1)}, f32[160,256]{1,0:T(8,128)S(1)}, u32[]{:S(2)}, u32[]{:S(2)}) collective-permute-start(f32[160,256]{1,0:T(8,128)S(1)} %get-tuple-element.23), channel_id=1, source_target_pairs={{16,0},{32,16},{48,32},{64,48},{80,64},{96,80},{112,96},{0,112},{1... | collective-permute-start | bytes 491528 | tf_op jit(solution)/shard_map/ppermute | solution.py:466
  14.5 40.3 %all-to-all-start = ((f32[128,1,4224]{2,1,0:T(1,128)}), f32[128,1,4224]{2,1,0:T(1,128)S(1)}, u32[]{:S(2)}, u32[]{:S(2)}) async-start(f32[128,1,4224]{2,1,0:T(1,128)} %bitcast.13), calls=%async_computation | async-start | bytes 4325376 | tf_op jit(solution)/shard_map/all_to_all | solution.py:740
  29.0 34.7 %collective-permute-start.7 = (f32[432,128]{1,0:T(8,128)S(1)}, f32[432,128]{1,0:T(8,128)S(1)}, u32[]{:S(2)}, u32[]{:S(2)}) collective-permute-start(f32[432,128]{1,0:T(8,128)S(1)} %get-tuple-element.31), channel_id=1, source_target_pairs={{15,0},{0,1},{1,2},{2,3},{3,4},{4,5},{5,6},{6,7},{7,8},{8,9},{9,10... | collective-permute-start | bytes 663560 | tf_op jit(solution)/shard_map/ppermute | solution.py:466
  30.5 33.2 %collective-permute-start.6 = (f32[432,128]{1,0:T(8,128)S(1)}, f32[432,128]{1,0:T(8,128)S(1)}, u32[]{:S(2)}, u32[]{:S(2)}) collective-permute-start(f32[432,128]{1,0:T(8,128)S(1)} %get-tuple-element.31), channel_id=1, source_target_pairs={{1,0},{2,1},{3,2},{4,3},{5,4},{6,5},{7,6},{8,7},{9,8},{10,9},{11,1... | collective-permute-start | bytes 663560 | tf_op jit(solution)/shard_map/ppermute | solution.py:466
  55.7 3.1 %collective-permute-start.2 = (f32[8,256]{1,0:T(8,128)S(1)}, f32[8,256]{1,0:T(8,128)S(1)}, u32[]{:S(2)}, u32[]{:S(2)}) collective-permute-start(f32[8,256]{1,0:T(8,128)S(1)} %get-tuple-element.37), channel_id=1, source_target_pairs={{16,0},{32,16},{48,32},{64,48},{80,64},{96,80},{112,96},{0,112},{1... | collective-permute-start | bytes 24584 | tf_op jit(solution)/shard_map/ppermute | solution.py:466
  56.3 29.9 %copy-start.5 = (f32[16]{0:T(128)S(1)}, f32[16]{0:T(128)}, u32[]{:S(2)}) copy-start(f32[16]{0:T(128)} %steric_ref.1) | copy-start | bytes 196
  56.3 2.5 %collective-permute-start.3 = (f32[8,256]{1,0:T(8,128)S(1)}, f32[8,256]{1,0:T(8,128)S(1)}, u32[]{:S(2)}, u32[]{:S(2)}) collective-permute-start(f32[8,256]{1,0:T(8,128)S(1)} %get-tuple-element.36), channel_id=1, source_target_pairs={{112,0},{0,16},{16,32},{32,48},{48,64},{64,80},{80,96},{96,112},{1... | collective-permute-start | bytes 24584 | tf_op jit(solution)/shard_map/ppermute | solution.py:466
  58.8 6.1 %collective-permute-start.5 = (f32[48,128]{1,0:T(8,128)S(1)}, f32[48,128]{1,0:T(8,128)S(1)}, u32[]{:S(2)}, u32[]{:S(2)}) collective-permute-start(f32[48,128]{1,0:T(8,128)S(1)} %slice_select_fusion), channel_id=1, source_target_pairs={{15,0},{0,1},{1,2},{2,3},{3,4},{4,5},{5,6},{6,7},{7,8},{8,9},{9,10... | collective-permute-start | bytes 73736 | tf_op jit(solution)/shard_map/ppermute | solution.py:466
  59.5 5.4 %collective-permute-start.4 = (f32[48,128]{1,0:T(8,128)S(1)}, f32[48,128]{1,0:T(8,128)S(1)}, u32[]{:S(2)}, u32[]{:S(2)}) collective-permute-start(f32[48,128]{1,0:T(8,128)S(1)} %slice_select_fusion), channel_id=1, source_target_pairs={{1,0},{2,1},{3,2},{4,3},{5,4},{6,5},{7,6},{8,7},{9,8},{10,9},{11,1... | collective-permute-start | bytes 73736 | tf_op jit(solution)/shard_map/ppermute | solution.py:466
  66.7 19.5 %all-to-all-start.1 = ((f32[128,1,128]{2,1,0:T(1,128)}), f32[128,1,128]{2,1,0:T(1,128)}, u32[]{:S(2)}, u32[]{:S(2)}) async-start(f32[128,1,128]{2,1,0:T(1,128)} %bitcast.6), calls=%async_computation.1 | async-start | bytes 131072 | tf_op jit(solution)/shard_map/all_to_all | solution.py:750

commit v4 on v3

--- a/solution.py
+++ b/solution.py
@@ -45,14 +45,11 @@
     return hi, (x - hi.astype(F32)).astype(BF16)
 
 
-def rank_kernel(capacity, sla_ref, weight_ref, tile_ref, start_ref, count_ref, token_ref, data_ref, place_ref, meta_ref):
-    blocks = tile_ref.shape[0]
+def ranks(capacity, tile, start, count, place_ref, meta_ref):
+    blocks = tile.shape[0]
     square = (LANES, LANES)
     sub, lane = iota(square, 0), iota(square, 1)
     prefix = jnp.concatenate([(sub < lane).astype(BF16), jnp.ones(square, BF16)], axis=1)
-    tile, start, count = tile_ref[...], start_ref[...], count_ref[...]
-    col_t = jnp.transpose((start & (LANES - 1)).astype(F32)).astype(jnp.int32)
-    count_t = jnp.transpose(count.astype(F32)).astype(jnp.int32)
     carry = jnp.zeros(square, F32)
     hits, firsts = [], []
     for k in range(blocks):
@@ -68,22 +65,27 @@
         block_of = jnp.where(sub == slot, begin // LANES, 0)
         lane_of = jnp.where(sub == slot + 64, begin & (LANES - 1), 0)
         firsts.append((block_of + lane_of).astype(F32).astype(BF16))
-        rows = slice(k * LANES, (k + 1) * LANES)
-        weight = jnp.where(lane < count_t[:, k : k + 1], weight_ref[rows, :], 0.0)
-        value = weight * sla_ref[rows, :]
-        index = (lane - col_t[:, k : k + 1]) & (LANES - 1)
-        weight = jnp.take_along_axis(weight, index, axis=1)
-        value = jnp.take_along_axis(value, index, axis=1)
-        data_ref[rows, :] = jnp.concatenate([*split(weight), *split(value)], axis=1)
     meta_ref[...] = lax.dot_general(
         jnp.concatenate(hits, axis=1),
         jnp.concatenate(firsts, axis=1),
         (((1,), (1,)), ((), ())),
         preferred_element_type=F32,
     )
-
-
-def place_kernel(capacity, data_ref, place_ref, meta_ref, token_ref, north_ref, south_ref, out_ref, next_ref, made_ref, sems):
+    col_t = jnp.transpose((start & (LANES - 1)).astype(F32)).astype(jnp.int32)
+    return col_t, jnp.transpose(count.astype(F32)).astype(jnp.int32)
+
+
+def turned_rows(data_ref, k, weight, sla, col, count):
+    lane = iota((LANES, LANES), 1)
+    weight = jnp.where(lane < count, weight, 0.0)
+    value = weight * sla
+    index = (lane - col) & (LANES - 1)
+    weight = jnp.take_along_axis(weight, index, axis=1)
+    value = jnp.take_along_axis(value, index, axis=1)
+    data_ref[k * LANES : (k + 1) * LANES, :] = jnp.concatenate([*split(weight), *split(value)], axis=1)
+
+
+def place_kernel(capacity, data_ref, place_ref, meta_ref, token_ref, out_ref, next_ref, made_ref, sems):
     next_ref[...] = token_ref[...]
     blocks = place_ref.shape[0]
     devices = LANES
@@ -111,35 +113,12 @@
         copy.wait()
 
 
-def pack(obs_sla, obs_weight, obs_tile, obs_start, obs_count, token, capacity):
-    blocks = obs_sla.shape[0] // LANES
-    return pl.pallas_call(
-        functools.partial(rank_kernel, capacity),
-        out_shape=(
-            jax.ShapeDtypeStruct((blocks * LANES, 4 * LANES), BF16),
-            jax.ShapeDtypeStruct((blocks, LANES), jnp.int32),
-            shape(LANES, LANES),
-        ),
-        in_specs=[VMEM] * 6,
-        out_specs=(VMEM,) * 3,
-        compiler_params=params(8),
-        name="rank_segments",
-    )(
-        obs_sla,
-        obs_weight,
-        obs_tile.reshape(blocks, LANES),
-        obs_start.reshape(blocks, LANES),
-        obs_count.reshape(blocks, LANES),
-        token,
-    )
-
-
-def placed(data, place, meta, token, around, capacity):
+def placed(data, place, meta, token, capacity):
     chunk = 2 * capacity + 1
     return pl.pallas_call(
         functools.partial(place_kernel, capacity),
         out_shape=(far_shape(LANES * chunk, LANES), shape(*token.shape)),
-        in_specs=[VMEM] * 4 + [pl.BlockSpec(memory_space=pl.ANY)] * 2,
+        in_specs=[VMEM] * 4,
         out_specs=(HBM, VMEM),
         scratch_shapes=[
             pltpu.VMEM((LANES * chunk, LANES), F32),
@@ -147,7 +126,7 @@
         ],
         compiler_params=params(12),
         name="place_segments",
-    )(data, place, meta, token, *around)
+    )(data, place, meta, token)
 
 
 def unpack_kernel(capacity, got_ref, height_ref, face_ref, token_ref, q_ref, next_ref, sum_ref):
@@ -424,8 +403,7 @@
         rho_0 = rho_0 + e[k] * (c[0] * v[0] + c[1] * v[1] + c[2] * v[2])
     rho_ref[...] = rho_0[:rows, :cols]
 
-    def one_level(level, carry):
-        copy(level).wait()
+    def one_level(level):
         height = steric_ref[level]
         full = lambda at: jnp.concatenate([tall_ref[level, at], side_ref[at, level]], axis=1)
         g = ocean * (full(0) + height * rho_1)
@@ -442,9 +420,15 @@
         mu_ref[level] = g[:rows, :cols] - (
             tall_ref[level, 7, 0:rows, :] * dx[:, :cols] + back_x + tall_ref[level, 8, 0:rows, :] * dy[:rows] + back_y
         )
+
+    def some_levels(group, carry):
+        for i in range(GROUP):
+            copy(group * GROUP + i).wait()
+        for i in range(GROUP):
+            one_level(group * GROUP + i)
         return carry
 
-    lax.fori_loop(0, levels, one_level, 0)
+    lax.fori_loop(0, levels // GROUP, some_levels, 0)
 
 
 def tracers(steric, every, fields, faces, tall, side):
@@ -496,12 +480,26 @@
     return jnp.where((iota((count, cols), 0) + first == rows - 1) & (last == 1.0), 0.0, 1.0)
 
 
-def rows_kernel(token_ref, lam_ref, zonal_ref, merid_ref, mix_x_ref, mix_y_ref, *refs):
-    surface_refs, (up_ref, down_ref, next_ref, held_ref, sems) = refs[:4], refs[4:]
+def opening_kernel(capacity, token_ref, lam_ref, zonal_ref, merid_ref, mix_x_ref, mix_y_ref, *refs):
+    surface_refs, (sla_ref, weight_ref), marks = refs[:4], refs[4:6], refs[6:9]
+    up_ref, down_ref, next_ref, data_ref, place_ref, meta_ref = refs[9:15]
+    held_ref, flat_ref, land_ref, segment_ref, mark_ref, sems, flat_sems, segment_sems, mark_sems = refs[15:]
     levels, rows, cols = lam_ref.shape
-    next_ref[...] = token_ref[...]
-    copies = []
-    for first in (0, rows - 8):
+    blocks = mark_ref.shape[1]
+
+    def started(source, target, sem):
+        copy = pltpu.make_async_copy(source, target, sem)
+        copy.start()
+        return copy
+
+    mark_copies = [started(ref, mark_ref.at[i], mark_sems.at[i]) for i, ref in enumerate(marks)]
+    segment_copies = []
+    for k in range(2):
+        block = pl.ds(k * blocks * LANES // 2, blocks * LANES // 2)
+        for i, ref in enumerate((sla_ref, weight_ref)):
+            segment_copies.append(started(ref.at[block, :], segment_ref.at[i, block, :], segment_sems.at[2 * k + i]))
+    copies, flat_copies = [], []
+    for part, first in enumerate((0, rows - 8)):
         block = pl.ds(first, 8)
         for source in (
             lam_ref.at[:, block, :],
@@ -511,22 +509,38 @@
             mix_y_ref.at[:, block, :],
             merid_ref.at[0, :, block, :],
         ):
-            at = len(copies)
-            copies.append(pltpu.make_async_copy(source, held_ref.at[at], sems.at[at]))
-            copies[-1].start()
+            copies.append(started(source, held_ref.at[len(copies)], sems.at[len(copies)]))
+        for i, ref in enumerate(surface_refs[:3]):
+            flat_copies.append(started(ref.at[block, :], flat_ref.at[part, i], flat_sems.at[len(flat_copies)]))
+        ref = surface_refs[3]
+        flat_copies.append(started(ref.at[block, :], land_ref.at[part], flat_sems.at[len(flat_copies)]))
+    next_ref[...] = token_ref[...]
+
+    for copy in mark_copies:
+        copy.wait()
+    col_t, count_t = ranks(capacity, mark_ref[0], mark_ref[1], mark_ref[2], place_ref, meta_ref)
+    for copy in copies + flat_copies:
+        copy.wait()
     for part, (out_ref, picks, first, take) in enumerate(((up_ref, UP, 0, 0), (down_ref, DOWN, rows - 8, 6))):
         keep = kept(token_ref, first, 8, rows, cols)
         base = 2 * len(picks) * levels
-        for at, field in enumerate(surface_fields(keep, *surface_refs, slice(first, first + 8))):
+        diag, east, north = [flat_ref[part, i] for i in range(3)]
+        ocean = land_ref[part].astype(F32)
+        for at, field in enumerate((diag, east, keep * north, ocean)):
             out_ref[base + 8 * at : base + 8 * at + 8, :] = field
-        for copy in copies[6 * part : 6 * part + 6]:
-            copy.wait()
         for level in range(levels):
             lam, zonal_1, merid_1, mix_x, mix_y, merid_0 = [held_ref[6 * part + i, level] for i in range(6)]
             fields = tracer_fields(keep, lam, zonal_1, merid_1, zonal_1, merid_0, mix_x, mix_y)
             for at, pick in enumerate(picks):
                 base = 2 * (at * levels + level)
                 out_ref[base : base + 2, :] = fields[pick][take : take + 2]
+    for copy in segment_copies:
+        copy.wait()
+    for k in range(blocks):
+        here = slice(k * LANES, (k + 1) * LANES)
+        turned_rows(
+            data_ref, k, segment_ref[1, here, :], segment_ref[0, here, :], col_t[:, k : k + 1], count_t[:, k : k + 1]
+        )
 
 
 def edge_rows(n_ref, s_ref, pick, levels, level, cols):
@@ -545,6 +559,22 @@
 def halves(tall):
     lane = iota((tall.shape[0], LANES), 1)
     return jnp.where(lane < LANES // 2, tall[:, :LANES], tall[:, -LANES:])
+
+
+def gathered(talls, width):
+    lane = iota((talls[0].shape[0], LANES), 1)
+    mixed = jnp.zeros((talls[0].shape[0], LANES), F32)
+    for at, tall in enumerate(talls):
+        mixed = jnp.where(lane // (2 * width) == at, pltpu.roll(halves(tall), width + 2 * width * at, 1), mixed)
+    return mixed
+
+
+def scattered(mixed, at, width):
+    return pltpu.roll(mixed, LANES - width - 2 * width * at, 1)
+
+
+TRACER_WIDTH = 2
+FACE_WIDTH = 8
 
 
 GROUP = 4
@@ -572,36 +602,34 @@
             copies[-1].start()
     keep = kept(token_ref, 0, rows, rows, cols)
     high = rows + 8
-    used = 8 * len(SIDE)
+    used = 2 * TRACER_WIDTH * len(SIDE)
     blocks = levels * high // LANES
     base = blocks * used
     up, down = 2 * len(UP) * levels, 2 * len(DOWN) * levels
+    talls = []
     for at, field in enumerate(surface_fields(keep, *surface_refs, slice(0, rows))):
         tall = jnp.concatenate(
             [field, n_ref[up + 8 * at : up + 8 * at + 8, :], s_ref[down + 8 * at : down + 8 * at + 8, :]], axis=0
         )
         face_ref[at] = tall
-        out_ref[base : base + rows + 16, :] = halves(tall)
-        base += rows + 16
+        talls.append(tall)
+    out_ref[base : base + rows + 16, :] = gathered(talls, FACE_WIDTH)
     for at, ref in enumerate(height_refs):
         height_ref[at] = ref[...]
-    lane = iota((high, LANES), 1)
     far = []
     for level in range(levels):
         if level % GROUP == 0:
             for copy in copies[7 * (level // GROUP) : 7 * (level // GROUP) + 7]:
                 copy.wait()
         fields = tracer_fields(keep, *[held_ref[i, level] for i in range(7)])
-        mixed = jnp.zeros((high, LANES), F32)
+        talls = []
         for pick, field in enumerate(fields):
             tall_ref[level, pick, 0:rows, :] = field
             edge = edge_rows(n_ref, s_ref, pick, levels, level, cols)
             tall_ref[level, pick, rows:high, :] = edge
             if pick in SIDE:
-                at = SIDE.index(pick)
-                tall = jnp.concatenate([field, edge], axis=0)
-                mixed = jnp.where(lane // 8 == at, pltpu.roll(halves(tall), 4 + 8 * at, 1), mixed)
-        flat_ref[level * high : (level + 1) * high, :] = mixed
+                talls.append(jnp.concatenate([field, edge], axis=0))
+        flat_ref[level * high : (level + 1) * high, :] = gathered(talls, TRACER_WIDTH)
         far.append(pltpu.make_async_copy(tall_ref.at[level], far_ref.at[level], far_sems.at[level]))
         far[-1].start()
     for b in range(blocks):
@@ -613,9 +641,9 @@
 
 def side_kernel(e_ref, w_ref, token_ref, side_ref, flat_ref):
     levels, high = side_ref.shape[1:3]
-    used = 8 * len(SIDE)
+    used = 2 * TRACER_WIDTH * len(SIDE)
     blocks = levels * high // LANES
-    western = iota((used, LANES), 0) % 8 < 4
+    western = iota((used, LANES), 0) % (2 * TRACER_WIDTH) < TRACER_WIDTH
     for b in range(blocks):
         at = slice(b * used, (b + 1) * used)
         both = jnp.where(western, w_ref[at, :], e_ref[at, :])
@@ -624,16 +652,15 @@
     for level in range(levels):
         mixed = flat_ref[level * high : (level + 1) * high, :]
         for at in range(len(SIDE)):
-            side_ref[at, level] = pltpu.roll(mixed, LANES - 4 - 8 * at, 1)
+            side_ref[at, level] = scattered(mixed, at, TRACER_WIDTH)
 
 
 def face_halo_kernel(base, token_ref, tall_ref, e_ref, w_ref, face_ref):
     high = tall_ref.shape[1]
-    eastern = iota((high, LANES), 1) < LANES // 2
-    full = []
-    for at in range(4):
-        here = slice(base + at * high, base + (at + 1) * high)
-        full.append(jnp.concatenate([tall_ref[at], jnp.where(eastern, e_ref[here, :], w_ref[here, :])], axis=1))
+    western = iota((high, LANES), 1) % (2 * FACE_WIDTH) < FACE_WIDTH
+    here = slice(base, base + high)
+    mixed = jnp.where(western, w_ref[here, :], e_ref[here, :])
+    full = [jnp.concatenate([tall_ref[at], scattered(mixed, at, FACE_WIDTH)], axis=1) for at in range(4)]
     diag, east, north, ocean = full
     west, south = pltpu.roll(east, 1, 1), pltpu.roll(north, 1, 0)
     face_ref[0] = (1.0 + diag) + east + west + north + south
@@ -641,25 +668,43 @@
         face_ref[1 + at] = field
 
 
-def edges_to_ty(token, tracer, surface):
+def opening(token, tracer, surface, segments, marks, capacity):
     levels, rows, cols = tracer[0].shape
     up, down = 2 * len(UP) * levels + 32, 2 * len(DOWN) * levels + 32
-    to_south, to_north, token = pl.pallas_call(
-        rows_kernel,
-        out_shape=(shape(up, cols), shape(down, cols), shape(*token.shape)),
-        in_specs=[VMEM] + [HBM] * 5 + [VMEM] * 4,
-        out_specs=(VMEM,) * 3,
-        scratch_shapes=[pltpu.VMEM((12, levels, 8, cols), F32), pltpu.SemaphoreType.DMA((12,))],
-        compiler_params=params(8),
-        name="edge_rows",
-    )(token, *far(tracer), *far(surface))
-    return (beside(to_south, "ty", 1), beside(to_north, "ty", -1)), token
+    blocks = segments[0].shape[0] // LANES
+    marks = tuple(mark.reshape(blocks, LANES) for mark in marks)
+    return pl.pallas_call(
+        functools.partial(opening_kernel, capacity),
+        out_shape=(
+            shape(up, cols),
+            shape(down, cols),
+            shape(*token.shape),
+            jax.ShapeDtypeStruct((blocks * LANES, 4 * LANES), BF16),
+            jax.ShapeDtypeStruct((blocks, LANES), jnp.int32),
+            shape(LANES, LANES),
+        ),
+        in_specs=[VMEM] + [HBM] * 14,
+        out_specs=(VMEM,) * 6,
+        scratch_shapes=[
+            pltpu.VMEM((12, levels, 8, cols), F32),
+            pltpu.VMEM((2, 3, 8, cols), F32),
+            pltpu.VMEM((2, 8, cols), jnp.int32),
+            pltpu.VMEM((2, blocks * LANES, LANES), F32),
+            pltpu.VMEM((3, blocks, LANES), jnp.int32),
+            pltpu.SemaphoreType.DMA((12,)),
+            pltpu.SemaphoreType.DMA((8,)),
+            pltpu.SemaphoreType.DMA((4,)),
+            pltpu.SemaphoreType.DMA((3,)),
+        ],
+        compiler_params=params(12),
+        name="opening",
+    )(token, *far(tracer), *far(surface), *far(segments), *far(marks))
 
 
 def edges_to_tx(token, tracer, surface, heights, north, south):
     levels, rows, cols = tracer[0].shape
     high = rows + 8
-    side_rows = 8 * len(SIDE) * levels * high // LANES + 4 * (rows + 16)
+    side_rows = 2 * TRACER_WIDTH * len(SIDE) * levels * high // LANES + rows + 16
     sides, tall, faces, heights = pl.pallas_call(
         cols_kernel,
         out_shape=(
@@ -686,7 +731,7 @@
 def faces_with_halo(token, tall, east, west):
     count, high, cols = tall.shape
     return pl.pallas_call(
-        functools.partial(face_halo_kernel, east.shape[0] - count * high),
+        functools.partial(face_halo_kernel, east.shape[0] - high),
         out_shape=shape(6, high, cols + LANES),
         in_specs=[VMEM] * 4,
         out_specs=VMEM,
@@ -734,9 +779,12 @@
     token = jnp.full((8, LANES), lax.axis_index("ty") == n_rows - 1, F32)
     tracer = (lam_tracer, zonal_flow, merid_flow, zonal_mixing, merid_mixing)
     surface = (surface_diag, surface_east, surface_north, land)
-    around_ty, token = edges_to_ty(token, tracer, surface)
-    ranked = pack(obs_sla, obs_weight, obs_tile, obs_start, obs_count, token, capacity)
-    sent, token = placed(*ranked, token, around_ty, capacity)
+    to_south, to_north, token, *ranked = opening(
+        token, tracer, surface, (obs_sla, obs_weight), (obs_tile, obs_start, obs_count), capacity
+    )
+    around_ty = beside(to_south, "ty", 1), beside(to_north, "ty", -1)
+    sent, token = placed(*ranked, token, capacity)
+    sent, *around_ty = lax.optimization_barrier((sent, *around_ty))
     got = lax.all_to_all(
         sent.reshape(devices, 1, -1), AXES, split_axis=0, concat_axis=0, tiled=True
     ).reshape(sent.shape)

time: 94.6 us -> 89.1 us (0.942)
  Pallas kernels: 24 us -> 20.7 us
  waiting for transfers between devices: 35.4 us -> 33.9 us
    pallas_call x1, Pallas kernels: 8 us -> 4.61 us  [tracers(): pl.pallas_call(tracer_kernel, out_shape=(shape(levels, rows, cols), shape...]
    ppermute x8, waiting for transfers between devices: 5.78 us -> 4.28 us  [beside(): lax.ppermute(cells, axis, [((i + step) % count, i) for i in range(count)])]
    pallas_call x3 -> x2, Pallas kernels: 4.27 us -> 4.32 us  [the longest x1 4.17 us: opening(): pl.pallas_call(functools.partial(opening_kernel, capacity), out_shape=(sh...]
  transfers between devices with their start and end apart: 10 -> 10, of which waited for: 5 -> 5; matrix products, arithmetic and copies ran while one was open for 0% -> 0% of each run, Pallas kernels for 9% -> 11%
where the time goes in v4:
time: 89.1 us; the launch traced here: 88.8 us
  waiting for transfers between devices  33.9 us (38%)
  starting transfers between devices  33.5 us (38%)
  Pallas kernels  20.7 us (23%)
    all_to_all x1, waiting for transfers between devices, on_device(): lax.all_to_all(sent.reshape(devices, 1, -1), AXES, split_axis=0, concat_a...  20.8 us
    ppermute x8, starting transfers between devices, beside(): lax.ppermute(cells, axis, [((i + step) % count, i) for i in range(count)])  14.6 us
    all_to_all x1, starting transfers between devices, on_device(): lax.all_to_all(mine.reshape(devices, 1, LANES), AXES, split_axis=0, conca...  9.5 us
    all_to_all x1, starting transfers between devices, on_device(): lax.all_to_all(sent.reshape(devices, 1, -1), AXES, split_axis=0, concat_a...  9.36 us
    all_to_all x1, waiting for transfers between devices, on_device(): lax.all_to_all(mine.reshape(devices, 1, LANES), AXES, split_axis=0, conca...  8.84 us
    pallas_call x1, Pallas kernels, edges_to_tx(): pl.pallas_call(cols_kernel, out_shape=(shape(side_rows, LANES), far_shape...  5.15 us
    pallas_call x1, Pallas kernels, tracers(): pl.pallas_call(tracer_kernel, out_shape=(shape(levels, rows, cols), shape...  4.61 us
    ppermute x8, waiting for transfers between devices, beside(): lax.ppermute(cells, axis, [((i + step) % count, i) for i in range(count)])  4.28 us
  transfers between devices with their start and end apart: 10, of which 5 were waited for; matrix products, arithmetic and copies ran while one was open for 0% of the time, Pallas kernels for 11%

profile of v4, /device:TPU:1, one launch (start us, length us, event | category | flops | bytes accessed | tf_op | source)
XLA Modules:
  0.0 88.8 jit_solution(4168683613538537484)
XLA Ops:
  0.6 4.2 %opening.1 = (f32[160,256]{1,0:T(8,128)S(1)}, f32[224,256]{1,0:T(8,128)S(1)}, f32[8,128]{1,0:T(8,128)S(1)}, bf16[1024,512]{1,0:T(8,128)(2,1)S(1)}, s32[8,128]{1,0:T(8,128)S(1)}, /*index=5*/f32[128,128]{1,0:T(8,128)S(1)}) custom-call(f32[8,128]{1,0:T(8,128)S(1)} %broadcast_in_dim.3.token_ref, f32[16,32,256]{2,1,0:T(8,128)} %lam_ref.3, ...), custom_call_target="tpu_custom_call" | custom-call | tf_op jit(solution)/shard_map/opening/pallas_call | solution.py:676
  4.8 3.0 %collective-permute-start.1 = (f32[224,256]{1,0:T(8,128)S(1)}, f32[224,256]{1,0:T(8,128)S(1)}, u32[]{:S(2)}, u32[]{:S(2)}) collective-permute-start(f32[224,256]{1,0:T(8,128)S(1)} %get-tuple-element.28), channel_id=1, source_target_pairs={{112,0},{0,16},{16,32},{32,48},{48,64},{64,80},{80,96},{96,112},{1... | collective-permute-start | bytes 688136 | tf_op jit(solution)/shard_map/ppermute | solution.py:450
  7.9 0.0 collective-permute-start
  7.9 3.1 %place_segments.1 = (f32[4224,128]{1,0:T(8,128)}, f32[8,128]{1,0:T(8,128)S(1)}) custom-call(bf16[1024,512]{1,0:T(8,128)(2,1)S(1)} %get-tuple-element.22.data_ref, s32[8,128]{1,0:T(8,128)S(1)} %get-tuple-element.23.place_ref, f32[128,128]{1,0:T(8,128)S(1)} %get-tuple-element.24.meta_ref, f32[8,128]{1,0:T(8,128)S(1)} %get-tuple-element.25.token_ref), custom_call_target="tpu_custom_call" | custom-call | tf_op jit(solution)/shard_map/place_segments/pallas_call | solution.py:118
  11.0 1.9 %collective-permute-done.refs_6_ = f32[160,256]{1,0:T(8,128)S(1)} collective-permute-done((f32[160,256]{1,0:T(8,128)S(1)}, f32[160,256]{1,0:T(8,128)S(1)}, u32[]{:S(2)}, u32[]{:S(2)}) %collective-permute-start) | collective-permute-done | bytes 163872 | tf_op jit(solution)/shard_map/ppermute | solution.py:450
  12.9 0.0 collective-permute-done.1.refs_7_
  12.9 9.4 %all-to-all-start = ((f32[128,1,4224]{2,1,0:T(1,128)}), f32[128,1,4224]{2,1,0:T(1,128)S(1)}, u32[]{:S(2)}, u32[]{:S(2)}) async-start(f32[128,1,4224]{2,1,0:T(1,128)} %bitcast.11), calls=%async_computation | async-start | bytes 4325376 | tf_op jit(solution)/shard_map/all_to_all | solution.py:788
  22.3 5.2 %edge_columns.1 = (f32[168,128]{1,0:T(8,128)S(1)}, f32[16,9,40,256]{3,2,1,0:T(8,128)}, f32[4,48,256]{2,1,0:T(8,128)S(1)}, f32[2,32,256]{2,1,0:T(8,128)S(1)}) custom-call(f32[8,128]{1,0:T(8,128)S(1)} %get-tuple-element.30.token_ref, f32[16,32,256]{2,1,0:T(8,128)} %lam_ref.3, f32[2,16,32,256]{3,2,1,0:T(8,128)} %zonal_ref.3, f32[2,16,32,256]{3,2,1,0:T(8,128)} %merid_ref.3, ...), custom_call_target="tpu_custom_call" | custom-call | tf_op jit(solution)/shard_map/edge_columns/pallas_call | solution.py:708
  27.4 1.5 %collective-permute-start.7 = (f32[168,128]{1,0:T(8,128)S(1)}, f32[168,128]{1,0:T(8,128)S(1)}, u32[]{:S(2)}, u32[]{:S(2)}) collective-permute-start(f32[168,128]{1,0:T(8,128)S(1)} %get-tuple-element.37), channel_id=1, source_target_pairs={{15,0},{0,1},{1,2},{2,3},{3,4},{4,5},{5,6},{6,7},{7,8},{8,9},{9,10... | collective-permute-start | bytes 258056 | tf_op jit(solution)/shard_map/ppermute | solution.py:450
  28.9 3.5 %collective-permute-start.6 = (f32[168,128]{1,0:T(8,128)S(1)}, f32[168,128]{1,0:T(8,128)S(1)}, u32[]{:S(2)}, u32[]{:S(2)}) collective-permute-start(f32[168,128]{1,0:T(8,128)S(1)} %get-tuple-element.37), channel_id=1, source_target_pairs={{1,0},{2,1},{3,2},{4,3},{5,4},{6,5},{7,6},{8,7},{9,8},{10,9},{11,1... | collective-permute-start | bytes 258056 | tf_op jit(solution)/shard_map/ppermute | solution.py:450
  32.4 20.8 %all-to-all-done = f32[128,1,4224]{2,1,0:T(1,128)S(1)} async-done(((f32[128,1,4224]{2,1,0:T(1,128)}), f32[128,1,4224]{2,1,0:T(1,128)S(1)}, u32[]{:S(2)}, u32[]{:S(2)}) %all-to-all-start) | async-done | bytes 2162720 | tf_op jit(solution)/shard_map/all_to_all | solution.py:788
  53.2 1.0 %forcing.1 = (f32[32,256]{1,0:T(8,128)S(1)}, f32[8,128]{1,0:T(8,128)S(1)}) custom-call(f32[4224,128]{1,0:T(8,128)S(1)} %bitcast.9, f32[2,32,256]{2,1,0:T(8,128)S(1)} %get-tuple-element.33.height_ref, f32[4,48,256]{2,1,0:T(8,128)S(1)} %get-tuple-element.34.face_ref.tall_ref, f32[8,128]{1,0:T(8,128)S(1)} %get-tuple-element.30.token_ref), custom_call_target="tpu_custom_call" | custom-call | tf_op jit(solution)/shard_map/forcing/pallas_call | solution.py:175
  54.1 0.0 copy-start
  54.1 0.6 collective-permute-start.2
  54.8 1.1 %collective-permute-start.3 = (f32[8,256]{1,0:T(8,128)S(1)}, f32[8,256]{1,0:T(8,128)S(1)}, u32[]{:S(2)}, u32[]{:S(2)}) collective-permute-start(f32[8,256]{1,0:T(8,128)S(1)} %get-tuple-element.42), channel_id=1, source_target_pairs={{112,0},{0,16},{16,32},{32,48},{48,64},{64,80},{80,96},{96,112},{1... | collective-permute-start | bytes 24584 | tf_op jit(solution)/shard_map/ppermute | solution.py:450
  55.9 1.3 %collective-permute-done.2.north_ref = f32[8,256]{1,0:T(8,128)S(1)} collective-permute-done((f32[8,256]{1,0:T(8,128)S(1)}, f32[8,256]{1,0:T(8,128)S(1)}, u32[]{:S(2)}, u32[]{:S(2)}) %collective-permute-start.2) | collective-permute-done | bytes 8224 | tf_op jit(solution)/shard_map/ppermute | solution.py:450
  57.2 0.0 collective-permute-done.3.south_ref
  57.3 0.7 collective-permute-start.5
  58.0 4.1 %collective-permute-start.4 = (f32[48,128]{1,0:T(8,128)S(1)}, f32[48,128]{1,0:T(8,128)S(1)}, u32[]{:S(2)}, u32[]{:S(2)}) collective-permute-start(f32[48,128]{1,0:T(8,128)S(1)} %slice_select_fusion), channel_id=1, source_target_pairs={{1,0},{2,1},{3,2},{4,3},{5,4},{6,5},{7,6},{8,7},{9,8},{10,9},{11,1... | collective-permute-start | bytes 73736 | tf_op jit(solution)/shard_map/ppermute | solution.py:450
  62.1 0.0 collective-permute-done.7.w_ref
  62.1 0.0 collective-permute-done.6.e_ref
  62.1 0.1 surface_halos.1.face_ref
  62.3 1.0 %collective-permute-done.5.west_ref = f32[48,128]{1,0:T(8,128)S(1)} collective-permute-done((f32[48,128]{1,0:T(8,128)S(1)}, f32[48,128]{1,0:T(8,128)S(1)}, u32[]{:S(2)}, u32[]{:S(2)}) %collective-permute-start.5) | collective-permute-done | bytes 24608 | tf_op jit(solution)/shard_map/ppermute | solution.py:450
  63.3 0.0 collective-permute-done.4.east_ref
  63.3 1.8 %krylov_sums.1 = (f32[128,128]{1,0:T(8,128)}, f32[9,48,384]{2,1,0:T(8,128)S(1)}, f32[8,128]{1,0:T(8,128)S(1)}) custom-call(f32[32,256]{1,0:T(8,128)S(1)} %get-tuple-element.35.q_ref, f32[8,256]{1,0:T(8,128)S(1)} %collective-permute-done.2.north_ref, f32[8,256]{1,0:T(8,128)S(1)} %collective-permute-done.3.south_ref, ...), custom_call_target="tpu_custom_call" | custom-call | tf_op jit(solution)/shard_map/krylov_sums/pallas_call | solution.py:278
  65.2 9.5 %all-to-all-start.1 = ((f32[128,1,128]{2,1,0:T(1,128)}), f32[128,1,128]{2,1,0:T(1,128)S(1)}, u32[]{:S(2)}, u32[]{:S(2)}) async-start(f32[128,1,128]{2,1,0:T(1,128)} %bitcast.6), calls=%async_computation.1 | async-start | bytes 131072 | tf_op jit(solution)/shard_map/all_to_all | solution.py:798
  74.7 0.7 tracer_halos.1.side_ref
  75.3 8.8 %all-to-all-done.1 = f32[128,1,128]{2,1,0:T(1,128)S(1)} async-done(((f32[128,1,128]{2,1,0:T(1,128)}), f32[128,1,128]{2,1,0:T(1,128)S(1)}, u32[]{:S(2)}, u32[]{:S(2)}) %all-to-all-start.1) | async-done | bytes 65568 | tf_op jit(solution)/shard_map/all_to_all | solution.py:798
  84.2 0.0 copy-done
  84.2 4.6 %tracer_steps.1 = (f32[16,32,256]{2,1,0:T(8,128)}, f32[32,256]{1,0:T(8,128)}) custom-call(f32[16]{0:T(128)S(1)} %copy-done, f32[128,128]{1,0:T(8,128)S(1)} %bitcast.10, f32[9,48,384]{2,1,0:T(8,128)S(1)} %get-tuple-element.39.field_ref, f32[6,48,384]{2,1,0:T(8,128)S(1)} %surface_halos.1.face_ref, f32[16,9,40,256]{3,2,1,0:T(8,128)} %get-tuple-element.40.far_ref, ...), custom_call_target="tpu_custom_call" | custom-call | tf_op jit(solution)/shard_map/tracer_steps/pallas_call | solution.py:437
  (7 shorter events, 0.0 us)
Async XLA Ops:
  4.8 8.1 %collective-permute-start.1 = (f32[224,256]{1,0:T(8,128)S(1)}, f32[224,256]{1,0:T(8,128)S(1)}, u32[]{:S(2)}, u32[]{:S(2)}) collective-permute-start(f32[224,256]{1,0:T(8,128)S(1)} %get-tuple-element.28), channel_id=1, source_target_pairs={{112,0},{0,16},{16,32},{32,48},{48,64},{64,80},{80,96},{96,112},{1... | collective-permute-start | bytes 688136 | tf_op jit(solution)/shard_map/ppermute | solution.py:450
  7.9 5.0 %collective-permute-start = (f32[160,256]{1,0:T(8,128)S(1)}, f32[160,256]{1,0:T(8,128)S(1)}, u32[]{:S(2)}, u32[]{:S(2)}) collective-permute-start(f32[160,256]{1,0:T(8,128)S(1)} %get-tuple-element.27), channel_id=1, source_target_pairs={{16,0},{32,16},{48,32},{64,48},{80,64},{96,80},{112,96},{0,112},{1... | collective-permute-start | bytes 491528 | tf_op jit(solution)/shard_map/ppermute | solution.py:450
  12.9 40.3 %all-to-all-start = ((f32[128,1,4224]{2,1,0:T(1,128)}), f32[128,1,4224]{2,1,0:T(1,128)S(1)}, u32[]{:S(2)}, u32[]{:S(2)}) async-start(f32[128,1,4224]{2,1,0:T(1,128)} %bitcast.11), calls=%async_computation | async-start | bytes 4325376 | tf_op jit(solution)/shard_map/all_to_all | solution.py:788
  27.4 34.7 %collective-permute-start.7 = (f32[168,128]{1,0:T(8,128)S(1)}, f32[168,128]{1,0:T(8,128)S(1)}, u32[]{:S(2)}, u32[]{:S(2)}) collective-permute-start(f32[168,128]{1,0:T(8,128)S(1)} %get-tuple-element.37), channel_id=1, source_target_pairs={{15,0},{0,1},{1,2},{2,3},{3,4},{4,5},{5,6},{6,7},{7,8},{8,9},{9,10... | collective-permute-start | bytes 258056 | tf_op jit(solution)/shard_map/ppermute | solution.py:450
  28.9 33.2 %collective-permute-start.6 = (f32[168,128]{1,0:T(8,128)S(1)}, f32[168,128]{1,0:T(8,128)S(1)}, u32[]{:S(2)}, u32[]{:S(2)}) collective-permute-start(f32[168,128]{1,0:T(8,128)S(1)} %get-tuple-element.37), channel_id=1, source_target_pairs={{1,0},{2,1},{3,2},{4,3},{5,4},{6,5},{7,6},{8,7},{9,8},{10,9},{11,1... | collective-permute-start | bytes 258056 | tf_op jit(solution)/shard_map/ppermute | solution.py:450
  54.1 30.1 %copy-start = (f32[16]{0:T(128)S(1)}, f32[16]{0:T(128)}, u32[]{:S(2)}) copy-start(f32[16]{0:T(128)} %steric_ref.1) | copy-start | bytes 196
  54.1 3.1 %collective-permute-start.2 = (f32[8,256]{1,0:T(8,128)S(1)}, f32[8,256]{1,0:T(8,128)S(1)}, u32[]{:S(2)}, u32[]{:S(2)}) collective-permute-start(f32[8,256]{1,0:T(8,128)S(1)} %get-tuple-element.43), channel_id=1, source_target_pairs={{16,0},{32,16},{48,32},{64,48},{80,64},{96,80},{112,96},{0,112},{1... | collective-permute-start | bytes 24584 | tf_op jit(solution)/shard_map/ppermute | solution.py:450
  54.8 2.5 %collective-permute-start.3 = (f32[8,256]{1,0:T(8,128)S(1)}, f32[8,256]{1,0:T(8,128)S(1)}, u32[]{:S(2)}, u32[]{:S(2)}) collective-permute-start(f32[8,256]{1,0:T(8,128)S(1)} %get-tuple-element.42), channel_id=1, source_target_pairs={{112,0},{0,16},{16,32},{32,48},{48,64},{64,80},{80,96},{96,112},{1... | collective-permute-start | bytes 24584 | tf_op jit(solution)/shard_map/ppermute | solution.py:450
  57.3 6.1 %collective-permute-start.5 = (f32[48,128]{1,0:T(8,128)S(1)}, f32[48,128]{1,0:T(8,128)S(1)}, u32[]{:S(2)}, u32[]{:S(2)}) collective-permute-start(f32[48,128]{1,0:T(8,128)S(1)} %slice_select_fusion), channel_id=1, source_target_pairs={{15,0},{0,1},{1,2},{2,3},{3,4},{4,5},{5,6},{6,7},{7,8},{8,9},{9,10... | collective-permute-start | bytes 73736 | tf_op jit(solution)/shard_map/ppermute | solution.py:450
  58.0 5.4 %collective-permute-start.4 = (f32[48,128]{1,0:T(8,128)S(1)}, f32[48,128]{1,0:T(8,128)S(1)}, u32[]{:S(2)}, u32[]{:S(2)}) collective-permute-start(f32[48,128]{1,0:T(8,128)S(1)} %slice_select_fusion), channel_id=1, source_target_pairs={{1,0},{2,1},{3,2},{4,3},{5,4},{6,5},{7,6},{8,7},{9,8},{10,9},{11,1... | collective-permute-start | bytes 73736 | tf_op jit(solution)/shard_map/ppermute | solution.py:450
  65.2 19.0 %all-to-all-start.1 = ((f32[128,1,128]{2,1,0:T(1,128)}), f32[128,1,128]{2,1,0:T(1,128)S(1)}, u32[]{:S(2)}, u32[]{:S(2)}) async-start(f32[128,1,128]{2,1,0:T(1,128)} %bitcast.6), calls=%async_computation.1 | async-start | bytes 131072 | tf_op jit(solution)/shard_map/all_to_all | solution.py:798

commit v5 on v4

--- a/solution.py
+++ b/solution.py
@@ -85,44 +85,104 @@
     data_ref[k * LANES : (k + 1) * LANES, :] = jnp.concatenate([*split(weight), *split(value)], axis=1)
 
 
-def place_kernel(capacity, data_ref, place_ref, meta_ref, token_ref, out_ref, next_ref, made_ref, sems):
+EDGE = 5
+WIDE = 2 * EDGE
+FIRST_SLOTS = 12
+
+
+def edge_lanes(rows):
+    slot, lane = iota((rows, LANES), 0) % 16, iota((rows, LANES), 1)
+    rest = 16 - FIRST_SLOTS
+    late = slot - FIRST_SLOTS
+    is_first = (lane // WIDE == slot) & (late < 0)
+    is_late = ((lane // WIDE) % rest == late) & (lane < 2 * rest * WIDE)
+    first = (lane - WIDE * slot) & (LANES - 1)
+    second = (first + WIDE) & (LANES - 1)
+    third = jnp.where(lane < rest * WIDE, lane - WIDE * late, lane - WIDE * (late + rest - 1)) & (LANES - 1)
+    return (first, is_first), (second, is_first), (third, is_late)
+
+
+def folded(parts):
+    sub = iota((8, LANES), 0)
+    for step in (4, 2, 1):
+        low = (sub & step) == 0
+        half = len(parts) // 2
+        pairs = []
+        for a, b in zip(parts[:half], parts[half:]):
+            other = jnp.where(low, b, a)
+            moved = jnp.where(low, pltpu.roll(other, 8 - step, 0), pltpu.roll(other, step, 0))
+            pairs.append(jnp.where(low, a, b) + moved)
+        parts = pairs
+    return parts[0]
+
+
+def place_kernel(capacity, n_cols, data_ref, place_ref, meta_ref, token_ref, out_ref, next_ref, made_ref, sems):
     next_ref[...] = token_ref[...]
     blocks = place_ref.shape[0]
-    devices = LANES
-    chunk = 2 * capacity + 1
-    made_ref[pl.ds(2 * capacity, devices, stride=chunk), :] = meta_ref[...]
+    chunk = 2 * capacity + 4
     place = jnp.concatenate([place_ref[k : k + 1, :] for k in range(blocks)], axis=1)
-    group = 16
-    height = group * capacity
+    height = n_cols * capacity
     slots = iota((height, blocks * LANES), 0)
+    lane = iota((capacity, LANES), 1)
+    ends = jnp.where(lane < WIDE, lane % EDGE, LANES - EDGE + lane % EDGE)
+    in_value = (lane // EDGE) % 2 == 1
+    lanes = edge_lanes(capacity)
+    western = iota((n_cols, LANES), 1) < WIDE * (16 - FIRST_SLOTS)
+    east_of = lambda x: pltpu.roll(x, n_cols - 1, 0)
+    west_of = lambda x: pltpu.roll(x, 1, 0)
     copies = []
-    for g in range(devices // group):
+    for g in range(LANES // n_cols):
         pick = (slots == place - g * height).astype(F32).astype(BF16)
         moved = jnp.dot(pick, data_ref[...], preferred_element_type=F32)
         weight = moved[:, :LANES] + moved[:, LANES : 2 * LANES]
         value = moved[:, 2 * LANES : 3 * LANES] + moved[:, 3 * LANES :]
-        for t in range(group):
-            base = (g * group + t) * chunk
+        first = g * n_cols * chunk
+        parts = [[], [], []]
+        for t in range(n_cols):
+            base = first + t * chunk
             rows = slice(t * capacity, (t + 1) * capacity)
             made_ref[base : base + capacity, :] = weight[rows]
             made_ref[base + capacity : base + 2 * capacity, :] = value[rows]
-        ready = pl.ds(g * group * chunk, group * chunk)
+            both = jnp.where(
+                in_value,
+                jnp.take_along_axis(value[rows], ends, axis=1),
+                jnp.take_along_axis(weight[rows], ends, axis=1),
+            )
+            for part, (index, mine) in zip(parts, lanes):
+                spread = jnp.where(mine, jnp.take_along_axis(both, index, axis=1), 0.0)
+                part.append(spread[:8] + spread[8:])
+        edges = [
+            jnp.concatenate([folded(part[i : i + 8]) for i in range(0, n_cols, 8)], axis=0) for part in parts
+        ]
+        meta = meta_ref[g * n_cols : (g + 1) * n_cols, :]
+        meta = (
+            meta + pltpu.roll(east_of(meta), capacity, 1) + pltpu.roll(west_of(meta), 2 * capacity, 1)
+        )
+        extra = (
+            meta,
+            east_of(edges[0]),
+            west_of(edges[1]),
+            jnp.where(western, east_of(edges[2]), west_of(edges[2])),
+        )
+        for i, rows in enumerate(extra):
+            made_ref[pl.ds(first + 2 * capacity + i, n_cols, stride=chunk), :] = rows
+        ready = pl.ds(first, n_cols * chunk)
         copies.append(pltpu.make_async_copy(made_ref.at[ready, :], out_ref.at[ready, :], sems.at[g]))
         copies[-1].start()
     for copy in copies:
         copy.wait()
 
 
-def placed(data, place, meta, token, capacity):
-    chunk = 2 * capacity + 1
+def placed(data, place, meta, token, capacity, n_cols):
+    chunk = 2 * capacity + 4
     return pl.pallas_call(
-        functools.partial(place_kernel, capacity),
+        functools.partial(place_kernel, capacity, n_cols),
         out_shape=(far_shape(LANES * chunk, LANES), shape(*token.shape)),
         in_specs=[VMEM] * 4,
         out_specs=(HBM, VMEM),
         scratch_shapes=[
             pltpu.VMEM((LANES * chunk, LANES), F32),
-            pltpu.SemaphoreType.DMA((LANES // 16,)),
+            pltpu.SemaphoreType.DMA((LANES // n_cols,)),
         ],
         compiler_params=params(12),
         name="place_segments",
@@ -131,12 +191,12 @@
 
 def unpack_kernel(capacity, got_ref, height_ref, face_ref, token_ref, q_ref, next_ref, sum_ref):
     next_ref[...] = token_ref[...]
-    chunk = 2 * capacity + 1
+    chunk = 2 * capacity + 4
     square = (LANES, LANES)
     lane = iota(square, 1)
     meta = got_ref[pl.ds(2 * capacity, LANES, stride=chunk), :]
     meta_t = jnp.transpose(meta)
-    rows, cols = q_ref.shape
+    rows, cols = q_ref.shape[0], q_ref.shape[1] - LANES
     cells = rows * cols // LANES
     blocks = iota((cells, LANES), 0).astype(F32)
     lane_f = lane.astype(F32)
@@ -167,17 +227,76 @@
         weight = sum_ref[0, pl.ds(half, rows, stride=2), :]
         value = sum_ref[1, pl.ds(half, rows, stride=2), :]
         mu = height_ref[0, :, at] + (weight * height_ref[1, :, at] - value)
-        q_ref[:, at] = face_ref[3, 0:rows, at] * mu
+        q_ref[:, at] = face_ref[5, 0:rows, at] * mu
+
+    row_of = iota((rows, LANES), 0).astype(F32)
+    group = iota((rows, LANES), 1) // WIDE
+    rest = capacity - FIRST_SLOTS
+    at = lane % EDGE
+    first = capacity + jnp.minimum(lane // WIDE, FIRST_SLOTS - 1)
+    late = capacity + FIRST_SLOTS + (lane // WIDE) % rest
+    western = lane < rest * WIDE
+    edges = []
+    for i, (index, is_west) in enumerate(
+        ((first, True), (first + capacity, False), (jnp.where(western, late, late + capacity), western))
+    ):
+        block = jnp.take_along_axis(meta, index, axis=1)
+        start = jnp.take_along_axis(meta, index + 64, axis=1).astype(jnp.int32)
+        odd = block != 2.0 * jnp.floor(0.5 * block)
+        has_west = ~odd & (at >= start)
+        has_east = odd | (LANES - EDGE + at < start)
+        if is_west is True:
+            valid = has_west
+        elif is_west is False:
+            valid = has_east
+        else:
+            valid = (is_west & has_west) | (~is_west & has_east)
+        edge = got_ref[pl.ds(2 * capacity + 1 + i, LANES, stride=chunk), :]
+        edges.append(jnp.concatenate(split(jnp.where(valid, edge, 0.0)), axis=0))
+
+    def edge_sum(base, row, first_group):
+        hits = []
+        for j in range(capacity):
+            hits.append((row_of == jnp.floor(0.5 * meta_t[base + j : base + j + 1])).astype(F32).astype(BF16))
+
+        def spread(picks, edge):
+            hit = jnp.concatenate(picks, axis=0)
+            return jnp.dot(jnp.concatenate([hit, hit], axis=1), edges[edge], preferred_element_type=F32)
+
+        total = jnp.zeros((rows, LANES), F32)
+        full = spread(hits[:FIRST_SLOTS], row)
+        for j in range(FIRST_SLOTS):
+            total = jnp.where(group == j, full[j * rows : (j + 1) * rows], total)
+        tail = spread(hits[FIRST_SLOTS:], 2)
+        late = jnp.zeros((rows, LANES), F32)
+        for j in range(rest):
+            late = jnp.where(group == first_group + j, tail[j * rows : (j + 1) * rows], late)
+        if first_group:
+            late = pltpu.roll(late, LANES - WIDE * first_group, 1)
+        total = total + late
+        total = total + pltpu.roll(total, LANES - 6 * WIDE, 1)
+        total = total + pltpu.roll(total, LANES - 3 * WIDE, 1)
+        total = total + pltpu.roll(total, LANES - WIDE, 1) + pltpu.roll(total, LANES - 2 * WIDE, 1)
+        return total, pltpu.roll(total, LANES - EDGE, 1)
+
+    side = slice(cols, cols + LANES)
+    eastern = iota((rows, LANES), 1) < LANES // 2
+    weight, value = [
+        jnp.where(eastern, e, pltpu.roll(w, LANES - EDGE, 1))
+        for e, w in zip(edge_sum(capacity, 0, 0), edge_sum(2 * capacity, 1, rest))
+    ]
+    mu = height_ref[0, :, side] + (weight * height_ref[1, :, side] - value)
+    q_ref[:, side] = face_ref[5, 0:rows, side] * mu
 
 
 def unpack(got, heights, faces, token, capacity):
-    rows, cols = heights.shape[1:]
+    rows, wide = heights.shape[1:]
     return pl.pallas_call(
         functools.partial(unpack_kernel, capacity),
-        out_shape=(shape(rows, cols), shape(*token.shape)),
+        out_shape=(shape(rows, wide), shape(*token.shape)),
         in_specs=[VMEM] * 4,
         out_specs=(VMEM, VMEM),
-        scratch_shapes=[pltpu.VMEM((2, rows * cols // LANES, LANES), F32)],
+        scratch_shapes=[pltpu.VMEM((2, rows * (wide - LANES) // LANES, LANES), F32)],
         compiler_params=params(10),
         name="forcing",
     )(got, heights, faces, token)
@@ -218,14 +337,11 @@
     return (start, one, two), (first, second, apply(two))
 
 
-def sums_kernel(q_ref, north_ref, south_ref, east_ref, west_ref, face_ref, token_ref, row_ref, field_ref, next_ref, part_ref):
+def sums_kernel(q_ref, north_ref, south_ref, face_ref, token_ref, row_ref, field_ref, next_ref, part_ref):
     next_ref[...] = token_ref[...]
-    rows, cols = q_ref.shape
+    rows, cols = q_ref.shape[0], q_ref.shape[1] - LANES
     high, wide = rows + 16, cols + LANES
-    side = jnp.where(iota((high, LANES), 1) < LANES // 2, east_ref[...], west_ref[...])
-    q = jnp.concatenate(
-        [jnp.concatenate([q_ref[...], north_ref[...], south_ref[...]], axis=0), side], axis=1
-    )
+    q = jnp.concatenate([q_ref[...], north_ref[...], south_ref[...]], axis=0)
 
     def apply(v):
         return (
@@ -273,17 +389,17 @@
     row_ref[...] = jnp.broadcast_to(row[0:1], row_ref.shape)
 
 
-def sums(q, north, south, east, west, faces, token):
-    rows, cols = q.shape
+def sums(q, north, south, faces, token):
+    rows, wide = q.shape
     return pl.pallas_call(
         sums_kernel,
-        out_shape=(shape(LANES, LANES), shape(9, rows + 16, cols + LANES), shape(*token.shape)),
-        in_specs=[VMEM] * 7,
+        out_shape=(shape(LANES, LANES), shape(9, rows + 16, wide), shape(*token.shape)),
+        in_specs=[VMEM] * 5,
         out_specs=(VMEM,) * 3,
         scratch_shapes=[pltpu.VMEM((8 * LANES, LANES), F32)],
         compiler_params=params(8),
         name="krylov_sums",
-    )(q, north, south, east, west, faces, token)
+    )(q, north, south, faces, token)
 
 
 def two_prod(a, b):
@@ -613,9 +729,10 @@
         )
         face_ref[at] = tall
         talls.append(tall)
-    out_ref[base : base + rows + 16, :] = gathered(talls, FACE_WIDTH)
     for at, ref in enumerate(height_refs):
         height_ref[at] = ref[...]
+        talls.append(jnp.concatenate([ref[...], jnp.zeros((16, cols), F32)], axis=0))
+    out_ref[base : base + rows + 16, :] = gathered(talls, FACE_WIDTH)
     far = []
     for level in range(levels):
         if level % GROUP == 0:
@@ -655,11 +772,16 @@
             side_ref[at, level] = scattered(mixed, at, TRACER_WIDTH)
 
 
-def face_halo_kernel(base, token_ref, tall_ref, e_ref, w_ref, face_ref):
+def face_halo_kernel(base, token_ref, tall_ref, height_ref, e_ref, w_ref, face_ref, full_ref):
     high = tall_ref.shape[1]
+    rows = height_ref.shape[1]
+    for at in range(2):
+        full_ref[at, :, : -LANES] = height_ref[at]
     western = iota((high, LANES), 1) % (2 * FACE_WIDTH) < FACE_WIDTH
     here = slice(base, base + high)
     mixed = jnp.where(western, w_ref[here, :], e_ref[here, :])
+    for at in range(2):
+        full_ref[at, :, -LANES:] = scattered(mixed, 4 + at, FACE_WIDTH)[:rows]
     full = [jnp.concatenate([tall_ref[at], scattered(mixed, at, FACE_WIDTH)], axis=1) for at in range(4)]
     diag, east, north, ocean = full
     west, south = pltpu.roll(east, 1, 1), pltpu.roll(north, 1, 0)
@@ -728,16 +850,16 @@
     return (beside(sides, "tx", 1), beside(sides, "tx", -1)), tall, faces, heights
 
 
-def faces_with_halo(token, tall, east, west):
+def faces_with_halo(token, tall, heights, east, west):
     count, high, cols = tall.shape
     return pl.pallas_call(
         functools.partial(face_halo_kernel, east.shape[0] - high),
-        out_shape=shape(6, high, cols + LANES),
-        in_specs=[VMEM] * 4,
-        out_specs=VMEM,
+        out_shape=(shape(6, high, cols + LANES), shape(2, heights.shape[1], cols + LANES)),
+        in_specs=[VMEM] * 5,
+        out_specs=(VMEM,) * 2,
         compiler_params=params(6),
         name="surface_halos",
-    )(token, tall, east, west)
+    )(token, tall, heights, east, west)
 
 
 def tracer_sides(token, levels, rows, east, west):
@@ -783,18 +905,16 @@
         token, tracer, surface, (obs_sla, obs_weight), (obs_tile, obs_start, obs_count), capacity
     )
     around_ty = beside(to_south, "ty", 1), beside(to_north, "ty", -1)
-    sent, token = placed(*ranked, token, capacity)
+    sent, token = placed(*ranked, token, capacity, devices // n_rows)
     sent, *around_ty = lax.optimization_barrier((sent, *around_ty))
     got = lax.all_to_all(
         sent.reshape(devices, 1, -1), AXES, split_axis=0, concat_axis=0, tiled=True
     ).reshape(sent.shape)
     around_tx, tall, faces, heights = edges_to_tx(token, tracer, surface, (lam_eta, eta_saved), *around_ty)
+    faces, heights = faces_with_halo(token, faces, heights, *around_tx)
     rhs, token = unpack(got, heights, faces, token, capacity)
-    faces = faces_with_halo(token, faces, *around_tx)
     north, south = beside(rhs[:8], "ty", 1), beside(rhs[-8:], "ty", -1)
-    side = halves(jnp.concatenate([rhs, north, south], axis=0))
-    east, west = beside(side, "tx", 1), beside(side, "tx", -1)
-    mine, krylov_fields, token = sums(rhs, north, south, east, west, faces, token)
+    mine, krylov_fields, token = sums(rhs, north, south, faces, token)
     every = lax.all_to_all(
         mine.reshape(devices, 1, LANES), AXES, split_axis=0, concat_axis=0, tiled=True
     ).reshape(devices, LANES)

time: 89.1 us -> 84.8 us (0.952)
  starting transfers between devices: 33.5 us -> 25.7 us
  Pallas kernels: 20.7 us -> 22.6 us
  local copies, waits for them, and re-layouts: 0.02 us -> 1.53 us
    ppermute x8 -> x6, waiting for transfers between devices: 4.28 us -> 25.7 us  [beside(): lax.ppermute(cells, axis, [((i + step) % count, i) for i in range(count)])]
    all_to_all x1, waiting for transfers between devices: 20.8 us -> 0.16 us  [on_device(): lax.all_to_all(sent.reshape(devices, 1, -1), AXES, split_axis=0, concat_a...]
    ppermute x8 -> x6, starting transfers between devices: 14.6 us -> 10.1 us  [beside(): lax.ppermute(cells, axis, [((i + step) % count, i) for i in range(count)])]
    all_to_all x1, starting transfers between devices: 9.5 us -> 6.07 us  [on_device(): lax.all_to_all(mine.reshape(devices, 1, LANES), AXES, split_axis=0, conca...]
    unnamed x4 -> x6, local copies, waits for them, and re-layouts: 0.01 us -> 1.52 us
    pallas_call x1, Pallas kernels: 3.13 us -> 4.38 us  [placed(): pl.pallas_call(functools.partial(place_kernel, capacity, n_cols), out_sha...]
  transfers between devices with their start and end apart: 10 -> 8, of which waited for: 5 -> 6; matrix products, arithmetic and copies ran while one was open for 0% -> 0% of each run, Pallas kernels for 11% -> 12%
where the time goes in v5:
time: 84.8 us; the launch traced here: 84.4 us
  waiting for transfers between devices  33.8 us (40%)
  starting transfers between devices  25.7 us (30%)
  Pallas kernels  22.6 us (27%)
  local copies, waits for them, and re-layouts  1.53 us (2%)
    ppermute x6, waiting for transfers between devices, beside(): lax.ppermute(cells, axis, [((i + step) % count, i) for i in range(count)])  25.7 us
    ppermute x6, starting transfers between devices, beside(): lax.ppermute(cells, axis, [((i + step) % count, i) for i in range(count)])  10.1 us
    all_to_all x1, starting transfers between devices, on_device(): lax.all_to_all(sent.reshape(devices, 1, -1), AXES, split_axis=0, concat_a...  9.58 us
    all_to_all x1, waiting for transfers between devices, on_device(): lax.all_to_all(mine.reshape(devices, 1, LANES), AXES, split_axis=0, conca...  8 us
    all_to_all x1, starting transfers between devices, on_device(): lax.all_to_all(mine.reshape(devices, 1, LANES), AXES, split_axis=0, conca...  6.07 us
    pallas_call x1, Pallas kernels, edges_to_tx(): pl.pallas_call(cols_kernel, out_shape=(shape(side_rows, LANES), far_shape...  5.15 us
    pallas_call x1, Pallas kernels, tracers(): pl.pallas_call(tracer_kernel, out_shape=(shape(levels, rows, cols), shape...  4.61 us
    pallas_call x1, Pallas kernels, placed(): pl.pallas_call(functools.partial(place_kernel, capacity, n_cols), out_sha...  4.38 us
  transfers between devices with their start and end apart: 8, of which 6 were waited for; matrix products, arithmetic and copies ran while one was open for 0% of the time, Pallas kernels for 12%

profile of v5, /device:TPU:1, one launch (start us, length us, event | category | flops | bytes accessed | tf_op | source)
XLA Modules:
  0.0 84.4 jit_solution(11745985873181364158)
XLA Ops:
  0.6 4.2 %opening.1 = (f32[160,256]{1,0:T(8,128)S(1)}, f32[224,256]{1,0:T(8,128)S(1)}, f32[8,128]{1,0:T(8,128)S(1)}, bf16[1024,512]{1,0:T(8,128)(2,1)S(1)}, s32[8,128]{1,0:T(8,128)S(1)}, /*index=5*/f32[128,128]{1,0:T(8,128)S(1)}) custom-call(f32[8,128]{1,0:T(8,128)S(1)} %broadcast_in_dim.3.token_ref, f32[16,32,256]{2,1,0:T(8,128)} %lam_ref.3, ...), custom_call_target="tpu_custom_call" | custom-call | tf_op jit(solution)/shard_map/opening/pallas_call | solution.py:798
  4.8 3.0 %collective-permute-start.1 = (f32[224,256]{1,0:T(8,128)S(1)}, f32[224,256]{1,0:T(8,128)S(1)}, u32[]{:S(2)}, u32[]{:S(2)}) collective-permute-start(f32[224,256]{1,0:T(8,128)S(1)} %get-tuple-element.30), channel_id=1, source_target_pairs={{112,0},{0,16},{16,32},{32,48},{48,64},{64,80},{80,96},{96,112},{1... | collective-permute-start | bytes 688136 | tf_op jit(solution)/shard_map/ppermute | solution.py:566
  7.9 0.0 collective-permute-start
  7.9 4.4 %place_segments.1 = (f32[4608,128]{1,0:T(8,128)}, f32[8,128]{1,0:T(8,128)S(1)}) custom-call(bf16[1024,512]{1,0:T(8,128)(2,1)S(1)} %get-tuple-element.24.data_ref, s32[8,128]{1,0:T(8,128)S(1)} %get-tuple-element.25.place_ref, f32[128,128]{1,0:T(8,128)S(1)} %get-tuple-element.26.meta_ref, f32[8,128]{1,0:T(8,128)S(1)} %get-tuple-element.27.token_ref), custom_call_target="tpu_custom_call" | custom-call | tf_op jit(solution)/shard_map/place_segments/pallas_call | solution.py:178
  12.3 0.6 collective-permute-done.refs_6_
  12.9 0.0 collective-permute-done.1.refs_7_
  12.9 9.6 %all-to-all-start = ((f32[128,1,4608]{2,1,0:T(1,128)}), f32[128,1,4608]{2,1,0:T(1,128)S(1)}, u32[]{:S(2)}, u32[]{:S(2)}) async-start(f32[128,1,4608]{2,1,0:T(1,128)} %bitcast.11), calls=%async_computation | async-start | bytes 4718592 | tf_op jit(solution)/shard_map/all_to_all | solution.py:910
  22.5 5.2 %edge_columns.1 = (f32[168,128]{1,0:T(8,128)S(1)}, f32[16,9,40,256]{3,2,1,0:T(8,128)}, f32[4,48,256]{2,1,0:T(8,128)S(1)}, f32[2,32,256]{2,1,0:T(8,128)S(1)}) custom-call(f32[8,128]{1,0:T(8,128)S(1)} %get-tuple-element.32.token_ref, f32[16,32,256]{2,1,0:T(8,128)} %lam_ref.3, f32[2,16,32,256]{3,2,1,0:T(8,128)} %zonal_ref.3, f32[2,16,32,256]{3,2,1,0:T(8,128)} %merid_ref.3, ...), custom_call_target="tpu_custom_call" | custom-call | tf_op jit(solution)/shard_map/edge_columns/pallas_call | solution.py:830
  27.7 1.5 %collective-permute-start.3 = (f32[168,128]{1,0:T(8,128)S(1)}, f32[168,128]{1,0:T(8,128)S(1)}, u32[]{:S(2)}, u32[]{:S(2)}) collective-permute-start(f32[168,128]{1,0:T(8,128)S(1)} %get-tuple-element.37), channel_id=1, source_target_pairs={{15,0},{0,1},{1,2},{2,3},{3,4},{4,5},{5,6},{6,7},{7,8},{8,9},{9,10... | collective-permute-start | bytes 258056 | tf_op jit(solution)/shard_map/ppermute | solution.py:566
  29.1 3.5 %collective-permute-start.2 = (f32[168,128]{1,0:T(8,128)S(1)}, f32[168,128]{1,0:T(8,128)S(1)}, u32[]{:S(2)}, u32[]{:S(2)}) collective-permute-start(f32[168,128]{1,0:T(8,128)S(1)} %get-tuple-element.37), channel_id=1, source_target_pairs={{1,0},{2,1},{3,2},{4,3},{5,4},{6,5},{7,6},{8,7},{9,8},{10,9},{11,1... | collective-permute-start | bytes 258056 | tf_op jit(solution)/shard_map/ppermute | solution.py:566
  32.6 21.9 %collective-permute-done.3.w_ref = f32[168,128]{1,0:T(8,128)S(1)} collective-permute-done((f32[168,128]{1,0:T(8,128)S(1)}, f32[168,128]{1,0:T(8,128)S(1)}, u32[]{:S(2)}, u32[]{:S(2)}) %collective-permute-start.3) | collective-permute-done | bytes 86048 | tf_op jit(solution)/shard_map/ppermute | solution.py:566
  54.5 0.0 collective-permute-done.2.e_ref
  54.5 0.1 surface_halos.1
  54.7 0.0 copy-start
  54.7 0.6 copy-done
  55.3 0.2 all-to-all-done
  55.5 0.0 copy-start.2
  55.5 1.6 %forcing.1 = (f32[32,384]{1,0:T(8,128)S(1)}, f32[8,128]{1,0:T(8,128)S(1)}) custom-call(f32[4608,128]{1,0:T(8,128)S(1)} %bitcast.9, f32[2,32,384]{2,1,0:T(8,128)S(1)} %get-tuple-element.38.height_ref, f32[6,48,384]{2,1,0:T(8,128)S(1)} %get-tuple-element.39.face_ref, f32[8,128]{1,0:T(8,128)S(1)} %get-tuple-element.32.token_ref), custom_call_target="tpu_custom_call" | custom-call | tf_op jit(solution)/shard_map/forcing/pallas_call | solution.py:294
  57.1 2.1 %collective-permute-start.5 = (f32[8,384]{1,0:T(8,128)S(1)}, f32[8,384]{1,0:T(8,128)S(1)}, u32[]{:S(2)}, u32[]{:S(2)}) collective-permute-start(f32[8,384]{1,0:T(8,128)S(1)} %get-tuple-element.46), channel_id=1, source_target_pairs={{112,0},{0,16},{16,32},{32,48},{48,64},{64,80},{80,96},{96,112},{1... | collective-permute-start | bytes 36872 | tf_op jit(solution)/shard_map/ppermute | solution.py:566
  59.2 0.0 collective-permute-start.4
  59.2 0.8 collective-permute-done.5.south_ref
  60.0 2.3 %collective-permute-done.4.north_ref = f32[8,384]{1,0:T(8,128)S(1)} collective-permute-done((f32[8,384]{1,0:T(8,128)S(1)}, f32[8,384]{1,0:T(8,128)S(1)}, u32[]{:S(2)}, u32[]{:S(2)}) %collective-permute-start.4) | collective-permute-done | bytes 12320 | tf_op jit(solution)/shard_map/ppermute | solution.py:566
  62.3 1.9 %krylov_sums.1 = (f32[128,128]{1,0:T(8,128)}, f32[9,48,384]{2,1,0:T(8,128)S(1)}, f32[8,128]{1,0:T(8,128)S(1)}) custom-call(f32[32,384]{1,0:T(8,128)S(1)} %get-tuple-element.40.q_ref, f32[8,384]{1,0:T(8,128)S(1)} %collective-permute-done.4.north_ref, f32[8,384]{1,0:T(8,128)S(1)} %collective-permute-done.5.south_ref, ...), custom_call_target="tpu_custom_call" | custom-call | tf_op jit(solution)/shard_map/krylov_sums/pallas_call | solution.py:394
  64.1 6.1 %all-to-all-start.1 = ((f32[128,1,128]{2,1,0:T(1,128)}), f32[128,1,128]{2,1,0:T(1,128)S(1)}, u32[]{:S(2)}, u32[]{:S(2)}) async-start(f32[128,1,128]{2,1,0:T(1,128)} %bitcast.6), calls=%async_computation.1 | async-start | bytes 131072 | tf_op jit(solution)/shard_map/all_to_all | solution.py:918
  70.2 0.0 copy-start.1
  70.2 0.9 %copy-done.1 = f32[168,128]{1,0:T(8,128)S(1)} copy-done((f32[168,128]{1,0:T(8,128)S(1)}, f32[168,128]{1,0:T(8,128)}, u32[]{:S(2)}) %copy-start.1) | copy-done | bytes 86040
  71.1 0.7 tracer_halos.1.side_ref
  71.8 8.0 %all-to-all-done.1 = f32[128,1,128]{2,1,0:T(1,128)S(1)} async-done(((f32[128,1,128]{2,1,0:T(1,128)}), f32[128,1,128]{2,1,0:T(1,128)S(1)}, u32[]{:S(2)}, u32[]{:S(2)}) %all-to-all-start.1) | async-done | bytes 65568 | tf_op jit(solution)/shard_map/all_to_all | solution.py:918
  79.8 0.0 copy-done.2
  79.8 4.6 %tracer_steps.1 = (f32[16,32,256]{2,1,0:T(8,128)}, f32[32,256]{1,0:T(8,128)}) custom-call(f32[16]{0:T(128)S(1)} %copy-done.2, f32[128,128]{1,0:T(8,128)S(1)} %bitcast.10, f32[9,48,384]{2,1,0:T(8,128)S(1)} %get-tuple-element.43.field_ref, f32[6,48,384]{2,1,0:T(8,128)S(1)} %get-tuple-element.39.face_ref, f32[16,9,40,256]{3,2,1,0:T(8,128)} %get-tuple-element.44.far_ref, ...), custom_call_target="tpu_custom_call" | custom-call | tf_op jit(solution)/shard_map/tracer_steps/pallas_call | solution.py:553
  (2 shorter events, 0.0 us)
Async XLA Ops:
  4.8 8.1 %collective-permute-start.1 = (f32[224,256]{1,0:T(8,128)S(1)}, f32[224,256]{1,0:T(8,128)S(1)}, u32[]{:S(2)}, u32[]{:S(2)}) collective-permute-start(f32[224,256]{1,0:T(8,128)S(1)} %get-tuple-element.30), channel_id=1, source_target_pairs={{112,0},{0,16},{16,32},{32,48},{48,64},{64,80},{80,96},{96,112},{1... | collective-permute-start | bytes 688136 | tf_op jit(solution)/shard_map/ppermute | solution.py:566
  7.9 5.0 %collective-permute-start = (f32[160,256]{1,0:T(8,128)S(1)}, f32[160,256]{1,0:T(8,128)S(1)}, u32[]{:S(2)}, u32[]{:S(2)}) collective-permute-start(f32[160,256]{1,0:T(8,128)S(1)} %get-tuple-element.29), channel_id=1, source_target_pairs={{16,0},{32,16},{48,32},{64,48},{80,64},{96,80},{112,96},{0,112},{1... | collective-permute-start | bytes 491528 | tf_op jit(solution)/shard_map/ppermute | solution.py:566
  12.9 42.6 %all-to-all-start = ((f32[128,1,4608]{2,1,0:T(1,128)}), f32[128,1,4608]{2,1,0:T(1,128)S(1)}, u32[]{:S(2)}, u32[]{:S(2)}) async-start(f32[128,1,4608]{2,1,0:T(1,128)} %bitcast.11), calls=%async_computation | async-start | bytes 4718592 | tf_op jit(solution)/shard_map/all_to_all | solution.py:910
  27.7 26.9 %collective-permute-start.3 = (f32[168,128]{1,0:T(8,128)S(1)}, f32[168,128]{1,0:T(8,128)S(1)}, u32[]{:S(2)}, u32[]{:S(2)}) collective-permute-start(f32[168,128]{1,0:T(8,128)S(1)} %get-tuple-element.37), channel_id=1, source_target_pairs={{15,0},{0,1},{1,2},{2,3},{3,4},{4,5},{5,6},{6,7},{7,8},{8,9},{9,10... | collective-permute-start | bytes 258056 | tf_op jit(solution)/shard_map/ppermute | solution.py:566
  29.1 25.4 %collective-permute-start.2 = (f32[168,128]{1,0:T(8,128)S(1)}, f32[168,128]{1,0:T(8,128)S(1)}, u32[]{:S(2)}, u32[]{:S(2)}) collective-permute-start(f32[168,128]{1,0:T(8,128)S(1)} %get-tuple-element.37), channel_id=1, source_target_pairs={{1,0},{2,1},{3,2},{4,3},{5,4},{6,5},{7,6},{8,7},{9,8},{10,9},{11,1... | collective-permute-start | bytes 258056 | tf_op jit(solution)/shard_map/ppermute | solution.py:566
  54.7 0.6 copy-start
  55.5 24.3 %copy-start.2 = (f32[16]{0:T(128)S(1)}, f32[16]{0:T(128)}, u32[]{:S(2)}) copy-start(f32[16]{0:T(128)} %steric_ref.1) | copy-start | bytes 196
  57.1 2.9 %collective-permute-start.5 = (f32[8,384]{1,0:T(8,128)S(1)}, f32[8,384]{1,0:T(8,128)S(1)}, u32[]{:S(2)}, u32[]{:S(2)}) collective-permute-start(f32[8,384]{1,0:T(8,128)S(1)} %get-tuple-element.46), channel_id=1, source_target_pairs={{112,0},{0,16},{16,32},{32,48},{48,64},{64,80},{80,96},{96,112},{1... | collective-permute-start | bytes 36872 | tf_op jit(solution)/shard_map/ppermute | solution.py:566
  59.2 3.1 %collective-permute-start.4 = (f32[8,384]{1,0:T(8,128)S(1)}, f32[8,384]{1,0:T(8,128)S(1)}, u32[]{:S(2)}, u32[]{:S(2)}) collective-permute-start(f32[8,384]{1,0:T(8,128)S(1)} %get-tuple-element.47), channel_id=1, source_target_pairs={{16,0},{32,16},{48,32},{64,48},{80,64},{96,80},{112,96},{0,112},{1... | collective-permute-start | bytes 36872 | tf_op jit(solution)/shard_map/ppermute | solution.py:566
  64.1 15.6 %all-to-all-start.1 = ((f32[128,1,128]{2,1,0:T(1,128)}), f32[128,1,128]{2,1,0:T(1,128)S(1)}, u32[]{:S(2)}, u32[]{:S(2)}) async-start(f32[128,1,128]{2,1,0:T(1,128)} %bitcast.6), calls=%async_computation.1 | async-start | bytes 131072 | tf_op jit(solution)/shard_map/all_to_all | solution.py:918
  70.2 0.9 %copy-start.1 = (f32[168,128]{1,0:T(8,128)S(1)}, f32[168,128]{1,0:T(8,128)}, u32[]{:S(2)}) copy-start(f32[168,128]{1,0:T(8,128)} %copy-done) | copy-start | bytes 258052

commit v6 on v5

--- a/solution.py
+++ b/solution.py
@@ -615,8 +615,8 @@
         for i, ref in enumerate((sla_ref, weight_ref)):
             segment_copies.append(started(ref.at[block, :], segment_ref.at[i, block, :], segment_sems.at[2 * k + i]))
     copies, flat_copies = [], []
-    for part, first in enumerate((0, rows - 8)):
-        block = pl.ds(first, 8)
+    for part, (first, outer) in enumerate(((0, 0), (rows - 8, rows - 2))):
+        block = pl.ds(outer, 2)
         for source in (
             lam_ref.at[:, block, :],
             zonal_ref.at[1, :, block, :],
@@ -624,8 +624,9 @@
             mix_x_ref.at[:, block, :],
             mix_y_ref.at[:, block, :],
             merid_ref.at[0, :, block, :],
-        ):
+        )[: 5 + part]:
             copies.append(started(source, held_ref.at[len(copies)], sems.at[len(copies)]))
+        block = pl.ds(first, 8)
         for i, ref in enumerate(surface_refs[:3]):
             flat_copies.append(started(ref.at[block, :], flat_ref.at[part, i], flat_sems.at[len(flat_copies)]))
         ref = surface_refs[3]
@@ -645,11 +646,11 @@
         for at, field in enumerate((diag, east, keep * north, ocean)):
             out_ref[base + 8 * at : base + 8 * at + 8, :] = field
         for level in range(levels):
-            lam, zonal_1, merid_1, mix_x, mix_y, merid_0 = [held_ref[6 * part + i, level] for i in range(6)]
-            fields = tracer_fields(keep, lam, zonal_1, merid_1, zonal_1, merid_0, mix_x, mix_y)
+            lam, zonal_1, merid_1, mix_x, mix_y, merid_0 = [held_ref[5 * part + min(i, 4 + part), level] for i in range(6)]
+            fields = tracer_fields(keep[take : take + 2], lam, zonal_1, merid_1, zonal_1, merid_0, mix_x, mix_y)
             for at, pick in enumerate(picks):
                 base = 2 * (at * levels + level)
-                out_ref[base : base + 2, :] = fields[pick][take : take + 2]
+                out_ref[base : base + 2, :] = fields[pick]
     for copy in segment_copies:
         copy.wait()
     for k in range(blocks):
@@ -756,14 +757,12 @@
         copy.wait()
 
 
-def side_kernel(e_ref, w_ref, token_ref, side_ref, flat_ref):
+def side_kernel(strip_ref, token_ref, side_ref, flat_ref):
     levels, high = side_ref.shape[1:3]
     used = 2 * TRACER_WIDTH * len(SIDE)
     blocks = levels * high // LANES
-    western = iota((used, LANES), 0) % (2 * TRACER_WIDTH) < TRACER_WIDTH
     for b in range(blocks):
-        at = slice(b * used, (b + 1) * used)
-        both = jnp.where(western, w_ref[at, :], e_ref[at, :])
+        both = strip_ref[b * used : (b + 1) * used, :]
         both = jnp.concatenate([both, jnp.zeros((LANES - used, LANES), F32)], axis=0)
         flat_ref[b * LANES : (b + 1) * LANES, :] = jnp.transpose(both)
     for level in range(levels):
@@ -772,7 +771,9 @@
             side_ref[at, level] = scattered(mixed, at, TRACER_WIDTH)
 
 
-def face_halo_kernel(base, token_ref, tall_ref, height_ref, e_ref, w_ref, face_ref, full_ref):
+def face_halo_kernel(base, token_ref, tall_ref, height_ref, e_ref, w_ref, face_ref, full_ref, strip_ref):
+    from_west = iota((base, LANES), 0) % (2 * TRACER_WIDTH) < TRACER_WIDTH
+    strip_ref[...] = jnp.where(from_west, w_ref[0:base, :], e_ref[0:base, :])
     high = tall_ref.shape[1]
     rows = height_ref.shape[1]
     for at in range(2):
@@ -808,12 +809,12 @@
         in_specs=[VMEM] + [HBM] * 14,
         out_specs=(VMEM,) * 6,
         scratch_shapes=[
-            pltpu.VMEM((12, levels, 8, cols), F32),
+            pltpu.VMEM((11, levels, 2, cols), F32),
             pltpu.VMEM((2, 3, 8, cols), F32),
             pltpu.VMEM((2, 8, cols), jnp.int32),
             pltpu.VMEM((2, blocks * LANES, LANES), F32),
             pltpu.VMEM((3, blocks, LANES), jnp.int32),
-            pltpu.SemaphoreType.DMA((12,)),
+            pltpu.SemaphoreType.DMA((11,)),
             pltpu.SemaphoreType.DMA((8,)),
             pltpu.SemaphoreType.DMA((4,)),
             pltpu.SemaphoreType.DMA((3,)),
@@ -852,27 +853,28 @@
 
 def faces_with_halo(token, tall, heights, east, west):
     count, high, cols = tall.shape
+    base = east.shape[0] - high
     return pl.pallas_call(
-        functools.partial(face_halo_kernel, east.shape[0] - high),
-        out_shape=(shape(6, high, cols + LANES), shape(2, heights.shape[1], cols + LANES)),
+        functools.partial(face_halo_kernel, base),
+        out_shape=(shape(6, high, cols + LANES), shape(2, heights.shape[1], cols + LANES), shape(base, LANES)),
         in_specs=[VMEM] * 5,
-        out_specs=(VMEM,) * 2,
+        out_specs=(VMEM,) * 3,
         compiler_params=params(6),
         name="surface_halos",
     )(token, tall, heights, east, west)
 
 
-def tracer_sides(token, levels, rows, east, west):
+def tracer_sides(token, strips, levels, rows):
     high = rows + 8
     return pl.pallas_call(
         side_kernel,
         out_shape=shape(len(SIDE), levels, high, LANES),
-        in_specs=[VMEM] * 3,
+        in_specs=[VMEM] * 2,
         out_specs=VMEM,
         scratch_shapes=[pltpu.VMEM((levels * high, LANES), F32)],
         compiler_params=params(8),
         name="tracer_halos",
-    )(east, west, token)
+    )(strips, token)
 
 
 def on_device(
@@ -911,14 +913,14 @@
         sent.reshape(devices, 1, -1), AXES, split_axis=0, concat_axis=0, tiled=True
     ).reshape(sent.shape)
     around_tx, tall, faces, heights = edges_to_tx(token, tracer, surface, (lam_eta, eta_saved), *around_ty)
-    faces, heights = faces_with_halo(token, faces, heights, *around_tx)
+    faces, heights, strips = faces_with_halo(token, faces, heights, *around_tx)
     rhs, token = unpack(got, heights, faces, token, capacity)
     north, south = beside(rhs[:8], "ty", 1), beside(rhs[-8:], "ty", -1)
     mine, krylov_fields, token = sums(rhs, north, south, faces, token)
     every = lax.all_to_all(
         mine.reshape(devices, 1, LANES), AXES, split_axis=0, concat_axis=0, tiled=True
     ).reshape(devices, LANES)
-    sides = tracer_sides(token, levels, rows, *around_tx)
+    sides = tracer_sides(token, strips, levels, rows)
     return tracers(steric, every, krylov_fields, faces, tall, sides)
 
 

time: 84.8 us -> 84 us (level)
  local copies, waits for them, and re-layouts: 1.53 us -> 0.01 us
  waiting for transfers between devices: 33.8 us -> 35.3 us
    unnamed x6 -> x2, local copies, waits for them, and re-layouts: 1.52 us -> 0.01 us
where the time goes in v6:
time: 84 us; the launch traced here: 83.6 us
  waiting for transfers between devices  35.3 us (42%)
  starting transfers between devices  25.7 us (31%)
  Pallas kernels  21.9 us (26%)
    ppermute x6, waiting for transfers between devices, beside(): lax.ppermute(cells, axis, [((i + step) % count, i) for i in range(count)])  25.7 us
    all_to_all x1, starting transfers between devices, on_device(): lax.all_to_all(sent.reshape(devices, 1, -1), AXES, split_axis=0, concat_a...  9.59 us
    ppermute x6, starting transfers between devices, beside(): lax.ppermute(cells, axis, [((i + step) % count, i) for i in range(count)])  9.46 us
    all_to_all x1, waiting for transfers between devices, on_device(): lax.all_to_all(mine.reshape(devices, 1, LANES), AXES, split_axis=0, conca...  8.84 us
    all_to_all x1, starting transfers between devices, on_device(): lax.all_to_all(mine.reshape(devices, 1, LANES), AXES, split_axis=0, conca...  6.68 us
    pallas_call x1, Pallas kernels, edges_to_tx(): pl.pallas_call(cols_kernel, out_shape=(shape(side_rows, LANES), far_shape...  5.15 us
    pallas_call x1, Pallas kernels, tracers(): pl.pallas_call(tracer_kernel, out_shape=(shape(levels, rows, cols), shape...  4.61 us
    pallas_call x1, Pallas kernels, placed(): pl.pallas_call(functools.partial(place_kernel, capacity, n_cols), out_sha...  4.38 us
  transfers between devices with their start and end apart: 8, of which 6 were waited for; matrix products, arithmetic and copies ran while one was open for 0% of the time, Pallas kernels for 12%

profile of v6, /device:TPU:1, one launch (start us, length us, event | category | flops | bytes accessed | tf_op | source)
XLA Modules:
  0.0 83.6 jit_solution(2121675103290772552)
XLA Ops:
  0.6 3.5 %opening.1 = (f32[160,256]{1,0:T(8,128)S(1)}, f32[224,256]{1,0:T(8,128)S(1)}, f32[8,128]{1,0:T(8,128)S(1)}, bf16[1024,512]{1,0:T(8,128)(2,1)S(1)}, s32[8,128]{1,0:T(8,128)S(1)}, /*index=5*/f32[128,128]{1,0:T(8,128)S(1)}) custom-call(f32[8,128]{1,0:T(8,128)S(1)} %broadcast_in_dim.3.token_ref, f32[16,32,256]{2,1,0:T(8,128)} %lam_ref.3, ...), custom_call_target="tpu_custom_call" | custom-call | tf_op jit(solution)/shard_map/opening/pallas_call | solution.py:799
  4.2 3.0 %collective-permute-start.1 = (f32[224,256]{1,0:T(8,128)S(1)}, f32[224,256]{1,0:T(8,128)S(1)}, u32[]{:S(2)}, u32[]{:S(2)}) collective-permute-start(f32[224,256]{1,0:T(8,128)S(1)} %get-tuple-element.31), channel_id=1, source_target_pairs={{112,0},{0,16},{16,32},{32,48},{48,64},{64,80},{80,96},{96,112},{1... | collective-permute-start | bytes 688136 | tf_op jit(solution)/shard_map/ppermute | solution.py:566
  7.2 0.0 collective-permute-start
  7.2 4.4 %place_segments.1 = (f32[4608,128]{1,0:T(8,128)}, f32[8,128]{1,0:T(8,128)S(1)}) custom-call(bf16[1024,512]{1,0:T(8,128)(2,1)S(1)} %get-tuple-element.25.data_ref, s32[8,128]{1,0:T(8,128)S(1)} %get-tuple-element.26.place_ref, f32[128,128]{1,0:T(8,128)S(1)} %get-tuple-element.27.meta_ref, f32[8,128]{1,0:T(8,128)S(1)} %get-tuple-element.28.token_ref), custom_call_target="tpu_custom_call" | custom-call | tf_op jit(solution)/shard_map/place_segments/pallas_call | solution.py:178
  11.6 0.6 collective-permute-done.refs_6_
  12.2 0.0 collective-permute-done.1.refs_7_
  12.2 9.6 %all-to-all-start = ((f32[128,1,4608]{2,1,0:T(1,128)}), f32[128,1,4608]{2,1,0:T(1,128)S(1)}, u32[]{:S(2)}, u32[]{:S(2)}) async-start(f32[128,1,4608]{2,1,0:T(1,128)} %bitcast.11), calls=%async_computation | async-start | bytes 4718592 | tf_op jit(solution)/shard_map/all_to_all | solution.py:912
  21.8 5.1 %edge_columns.1 = (f32[168,128]{1,0:T(8,128)S(1)}, f32[16,9,40,256]{3,2,1,0:T(8,128)}, f32[4,48,256]{2,1,0:T(8,128)S(1)}, f32[2,32,256]{2,1,0:T(8,128)S(1)}) custom-call(f32[8,128]{1,0:T(8,128)S(1)} %get-tuple-element.33.token_ref, f32[16,32,256]{2,1,0:T(8,128)} %lam_ref.3, f32[2,16,32,256]{3,2,1,0:T(8,128)} %zonal_ref.3, f32[2,16,32,256]{3,2,1,0:T(8,128)} %merid_ref.3, ...), custom_call_target="tpu_custom_call" | custom-call | tf_op jit(solution)/shard_map/edge_columns/pallas_call | solution.py:831
  27.0 1.5 %collective-permute-start.3 = (f32[168,128]{1,0:T(8,128)S(1)}, f32[168,128]{1,0:T(8,128)S(1)}, u32[]{:S(2)}, u32[]{:S(2)}) collective-permute-start(f32[168,128]{1,0:T(8,128)S(1)} %get-tuple-element.38), channel_id=1, source_target_pairs={{15,0},{0,1},{1,2},{2,3},{3,4},{4,5},{5,6},{6,7},{7,8},{8,9},{9,10... | collective-permute-start | bytes 258056 | tf_op jit(solution)/shard_map/ppermute | solution.py:566
  28.5 3.5 %collective-permute-start.2 = (f32[168,128]{1,0:T(8,128)S(1)}, f32[168,128]{1,0:T(8,128)S(1)}, u32[]{:S(2)}, u32[]{:S(2)}) collective-permute-start(f32[168,128]{1,0:T(8,128)S(1)} %get-tuple-element.38), channel_id=1, source_target_pairs={{1,0},{2,1},{3,2},{4,3},{5,4},{6,5},{7,6},{8,7},{9,8},{10,9},{11,1... | collective-permute-start | bytes 258056 | tf_op jit(solution)/shard_map/ppermute | solution.py:566
  32.0 21.9 %collective-permute-done.3.w_ref = f32[168,128]{1,0:T(8,128)S(1)} collective-permute-done((f32[168,128]{1,0:T(8,128)S(1)}, f32[168,128]{1,0:T(8,128)S(1)}, u32[]{:S(2)}, u32[]{:S(2)}) %collective-permute-start.3) | collective-permute-done | bytes 86048 | tf_op jit(solution)/shard_map/ppermute | solution.py:566
  53.9 0.0 collective-permute-done.2.e_ref
  53.9 0.2 surface_halos.1
  54.0 0.8 all-to-all-done
  54.8 0.0 copy-start
  54.8 1.6 %forcing.1 = (f32[32,384]{1,0:T(8,128)S(1)}, f32[8,128]{1,0:T(8,128)S(1)}) custom-call(f32[4608,128]{1,0:T(8,128)S(1)} %bitcast.9, f32[2,32,384]{2,1,0:T(8,128)S(1)} %get-tuple-element.39.height_ref, f32[6,48,384]{2,1,0:T(8,128)S(1)} %get-tuple-element.40.face_ref, f32[8,128]{1,0:T(8,128)S(1)} %get-tuple-element.33.token_ref), custom_call_target="tpu_custom_call" | custom-call | tf_op jit(solution)/shard_map/forcing/pallas_call | solution.py:294
  56.4 1.5 %collective-permute-start.5 = (f32[8,384]{1,0:T(8,128)S(1)}, f32[8,384]{1,0:T(8,128)S(1)}, u32[]{:S(2)}, u32[]{:S(2)}) collective-permute-start(f32[8,384]{1,0:T(8,128)S(1)} %get-tuple-element.48), channel_id=1, source_target_pairs={{112,0},{0,16},{16,32},{32,48},{48,64},{64,80},{80,96},{96,112},{1... | collective-permute-start | bytes 36872 | tf_op jit(solution)/shard_map/ppermute | solution.py:566
  57.9 0.0 collective-permute-start.4
  57.9 0.8 collective-permute-done.5.south_ref
  58.7 2.3 %collective-permute-done.4.north_ref = f32[8,384]{1,0:T(8,128)S(1)} collective-permute-done((f32[8,384]{1,0:T(8,128)S(1)}, f32[8,384]{1,0:T(8,128)S(1)}, u32[]{:S(2)}, u32[]{:S(2)}) %collective-permute-start.4) | collective-permute-done | bytes 12320 | tf_op jit(solution)/shard_map/ppermute | solution.py:566
  61.0 1.8 %krylov_sums.1 = (f32[128,128]{1,0:T(8,128)}, f32[9,48,384]{2,1,0:T(8,128)S(1)}, f32[8,128]{1,0:T(8,128)S(1)}) custom-call(f32[32,384]{1,0:T(8,128)S(1)} %get-tuple-element.41.q_ref, f32[8,384]{1,0:T(8,128)S(1)} %collective-permute-done.4.north_ref, f32[8,384]{1,0:T(8,128)S(1)} %collective-permute-done.5.south_ref, ...), custom_call_target="tpu_custom_call" | custom-call | tf_op jit(solution)/shard_map/krylov_sums/pallas_call | solution.py:394
  62.8 6.7 %all-to-all-start.1 = ((f32[128,1,128]{2,1,0:T(1,128)}), f32[128,1,128]{2,1,0:T(1,128)S(1)}, u32[]{:S(2)}, u32[]{:S(2)}) async-start(f32[128,1,128]{2,1,0:T(1,128)} %bitcast.6), calls=%async_computation.1 | async-start | bytes 131072 | tf_op jit(solution)/shard_map/all_to_all | solution.py:920
  69.5 0.7 tracer_halos.1.side_ref
  70.2 8.8 %all-to-all-done.1 = f32[128,1,128]{2,1,0:T(1,128)S(1)} async-done(((f32[128,1,128]{2,1,0:T(1,128)}), f32[128,1,128]{2,1,0:T(1,128)S(1)}, u32[]{:S(2)}, u32[]{:S(2)}) %all-to-all-start.1) | async-done | bytes 65568 | tf_op jit(solution)/shard_map/all_to_all | solution.py:920
  79.0 0.0 copy-done
  79.0 4.6 %tracer_steps.1 = (f32[16,32,256]{2,1,0:T(8,128)}, f32[32,256]{1,0:T(8,128)}) custom-call(f32[16]{0:T(128)S(1)} %copy-done, f32[128,128]{1,0:T(8,128)S(1)} %bitcast.10, f32[9,48,384]{2,1,0:T(8,128)S(1)} %get-tuple-element.44.field_ref, f32[6,48,384]{2,1,0:T(8,128)S(1)} %get-tuple-element.40.face_ref, f32[16,9,40,256]{3,2,1,0:T(8,128)} %get-tuple-element.45.far_ref, ...), custom_call_target="tpu_custom_call" | custom-call | tf_op jit(solution)/shard_map/tracer_steps/pallas_call | solution.py:553
  (2 shorter events, 0.0 us)
Async XLA Ops:
  4.2 8.1 %collective-permute-start.1 = (f32[224,256]{1,0:T(8,128)S(1)}, f32[224,256]{1,0:T(8,128)S(1)}, u32[]{:S(2)}, u32[]{:S(2)}) collective-permute-start(f32[224,256]{1,0:T(8,128)S(1)} %get-tuple-element.31), channel_id=1, source_target_pairs={{112,0},{0,16},{16,32},{32,48},{48,64},{64,80},{80,96},{96,112},{1... | collective-permute-start | bytes 688136 | tf_op jit(solution)/shard_map/ppermute | solution.py:566
  7.2 5.0 %collective-permute-start = (f32[160,256]{1,0:T(8,128)S(1)}, f32[160,256]{1,0:T(8,128)S(1)}, u32[]{:S(2)}, u32[]{:S(2)}) collective-permute-start(f32[160,256]{1,0:T(8,128)S(1)} %get-tuple-element.30), channel_id=1, source_target_pairs={{16,0},{32,16},{48,32},{64,48},{80,64},{96,80},{112,96},{0,112},{1... | collective-permute-start | bytes 491528 | tf_op jit(solution)/shard_map/ppermute | solution.py:566
  12.2 42.6 %all-to-all-start = ((f32[128,1,4608]{2,1,0:T(1,128)}), f32[128,1,4608]{2,1,0:T(1,128)S(1)}, u32[]{:S(2)}, u32[]{:S(2)}) async-start(f32[128,1,4608]{2,1,0:T(1,128)} %bitcast.11), calls=%async_computation | async-start | bytes 4718592 | tf_op jit(solution)/shard_map/all_to_all | solution.py:912
  27.0 26.9 %collective-permute-start.3 = (f32[168,128]{1,0:T(8,128)S(1)}, f32[168,128]{1,0:T(8,128)S(1)}, u32[]{:S(2)}, u32[]{:S(2)}) collective-permute-start(f32[168,128]{1,0:T(8,128)S(1)} %get-tuple-element.38), channel_id=1, source_target_pairs={{15,0},{0,1},{1,2},{2,3},{3,4},{4,5},{5,6},{6,7},{7,8},{8,9},{9,10... | collective-permute-start | bytes 258056 | tf_op jit(solution)/shard_map/ppermute | solution.py:566
  28.5 25.4 %collective-permute-start.2 = (f32[168,128]{1,0:T(8,128)S(1)}, f32[168,128]{1,0:T(8,128)S(1)}, u32[]{:S(2)}, u32[]{:S(2)}) collective-permute-start(f32[168,128]{1,0:T(8,128)S(1)} %get-tuple-element.38), channel_id=1, source_target_pairs={{1,0},{2,1},{3,2},{4,3},{5,4},{6,5},{7,6},{8,7},{9,8},{10,9},{11,1... | collective-permute-start | bytes 258056 | tf_op jit(solution)/shard_map/ppermute | solution.py:566
  54.8 24.2 %copy-start = (f32[16]{0:T(128)S(1)}, f32[16]{0:T(128)}, u32[]{:S(2)}) copy-start(f32[16]{0:T(128)} %steric_ref.1) | copy-start | bytes 196
  56.4 2.3 %collective-permute-start.5 = (f32[8,384]{1,0:T(8,128)S(1)}, f32[8,384]{1,0:T(8,128)S(1)}, u32[]{:S(2)}, u32[]{:S(2)}) collective-permute-start(f32[8,384]{1,0:T(8,128)S(1)} %get-tuple-element.48), channel_id=1, source_target_pairs={{112,0},{0,16},{16,32},{32,48},{48,64},{64,80},{80,96},{96,112},{1... | collective-permute-start | bytes 36872 | tf_op jit(solution)/shard_map/ppermute | solution.py:566
  57.9 3.1 %collective-permute-start.4 = (f32[8,384]{1,0:T(8,128)S(1)}, f32[8,384]{1,0:T(8,128)S(1)}, u32[]{:S(2)}, u32[]{:S(2)}) collective-permute-start(f32[8,384]{1,0:T(8,128)S(1)} %get-tuple-element.49), channel_id=1, source_target_pairs={{16,0},{32,16},{48,32},{64,48},{80,64},{96,80},{112,96},{0,112},{1... | collective-permute-start | bytes 36872 | tf_op jit(solution)/shard_map/ppermute | solution.py:566
  62.8 16.2 %all-to-all-start.1 = ((f32[128,1,128]{2,1,0:T(1,128)}), f32[128,1,128]{2,1,0:T(1,128)S(1)}, u32[]{:S(2)}, u32[]{:S(2)}) async-start(f32[128,1,128]{2,1,0:T(1,128)} %bitcast.6), calls=%async_computation.1 | async-start | bytes 131072 | tf_op jit(solution)/shard_map/all_to_all | solution.py:920

commit v7 on v6

--- a/solution.py
+++ b/solution.py
@@ -337,8 +337,7 @@
     return (start, one, two), (first, second, apply(two))
 
 
-def sums_kernel(q_ref, north_ref, south_ref, face_ref, token_ref, row_ref, field_ref, next_ref, part_ref):
-    next_ref[...] = token_ref[...]
+def sums_kernel(q_ref, north_ref, south_ref, face_ref, token_ref, row_ref, field_ref, part_ref):
     rows, cols = q_ref.shape[0], q_ref.shape[1] - LANES
     high, wide = rows + 16, cols + LANES
     q = jnp.concatenate([q_ref[...], north_ref[...], south_ref[...]], axis=0)
@@ -393,9 +392,9 @@
     rows, wide = q.shape
     return pl.pallas_call(
         sums_kernel,
-        out_shape=(shape(LANES, LANES), shape(9, rows + 16, wide), shape(*token.shape)),
+        out_shape=(shape(LANES, LANES), shape(9, rows + 16, wide)),
         in_specs=[VMEM] * 5,
-        out_specs=(VMEM,) * 3,
+        out_specs=(VMEM,) * 2,
         scratch_shapes=[pltpu.VMEM((8 * LANES, LANES), F32)],
         compiler_params=params(8),
         name="krylov_sums",
@@ -757,7 +756,8 @@
         copy.wait()
 
 
-def side_kernel(strip_ref, token_ref, side_ref, flat_ref):
+def side_kernel(strip_ref, token_ref, side_ref, next_ref, flat_ref):
+    next_ref[...] = token_ref[...]
     levels, high = side_ref.shape[1:3]
     used = 2 * TRACER_WIDTH * len(SIDE)
     blocks = levels * high // LANES
@@ -868,9 +868,9 @@
     high = rows + 8
     return pl.pallas_call(
         side_kernel,
-        out_shape=shape(len(SIDE), levels, high, LANES),
+        out_shape=(shape(len(SIDE), levels, high, LANES), shape(*token.shape)),
         in_specs=[VMEM] * 2,
-        out_specs=VMEM,
+        out_specs=(VMEM, VMEM),
         scratch_shapes=[pltpu.VMEM((levels * high, LANES), F32)],
         compiler_params=params(8),
         name="tracer_halos",
@@ -916,11 +916,11 @@
     faces, heights, strips = faces_with_halo(token, faces, heights, *around_tx)
     rhs, token = unpack(got, heights, faces, token, capacity)
     north, south = beside(rhs[:8], "ty", 1), beside(rhs[-8:], "ty", -1)
-    mine, krylov_fields, token = sums(rhs, north, south, faces, token)
+    sides, token = tracer_sides(token, strips, levels, rows)
+    mine, krylov_fields = sums(rhs, north, south, faces, token)
     every = lax.all_to_all(
         mine.reshape(devices, 1, LANES), AXES, split_axis=0, concat_axis=0, tiled=True
     ).reshape(devices, LANES)
-    sides = tracer_sides(token, strips, levels, rows)
     return tracers(steric, every, krylov_fields, faces, tall, sides)
 
 

time: 84 us -> 83.2 us (level)
  blocking collectives: 0 us -> 16.1 us
  waiting for transfers between devices: 35.3 us -> 25.8 us
  starting transfers between devices: 25.7 us -> 19.1 us
    all_to_all x0 -> x1, blocking collectives: none -> 16.1 us  [on_device(): lax.all_to_all(mine.reshape(devices, 1, LANES), AXES, split_axis=0, conca...]
    all_to_all x1 -> x0, waiting for transfers between devices: 8.84 us -> none  [on_device(): lax.all_to_all(mine.reshape(devices, 1, LANES), AXES, split_axis=0, conca...]
    all_to_all x1 -> x0, starting transfers between devices: 6.68 us -> none  [on_device(): lax.all_to_all(mine.reshape(devices, 1, LANES), AXES, split_axis=0, conca...]
  transfers between devices with their start and end apart: 8 -> 7, of which waited for: 6 -> 5; matrix products, arithmetic and copies ran while one was open for 0% -> 0% of each run, Pallas kernels for 12% -> 13%
where the time goes in v7:
time: 83.2 us; the launch traced here: 82.9 us
  waiting for transfers between devices  25.8 us (31%)
  Pallas kernels  21.3 us (26%)
  starting transfers between devices  19.1 us (23%)
  blocking collectives  16.1 us (19%)
    ppermute x6, waiting for transfers between devices, beside(): lax.ppermute(cells, axis, [((i + step) % count, i) for i in range(count)])  25 us
    all_to_all x1, blocking collectives, on_device(): lax.all_to_all(mine.reshape(devices, 1, LANES), AXES, split_axis=0, conca...  16.1 us
    all_to_all x1, starting transfers between devices, on_device(): lax.all_to_all(sent.reshape(devices, 1, -1), AXES, split_axis=0, concat_a...  9.6 us
    ppermute x6, starting transfers between devices, beside(): lax.ppermute(cells, axis, [((i + step) % count, i) for i in range(count)])  9.45 us
    pallas_call x1, Pallas kernels, edges_to_tx(): pl.pallas_call(cols_kernel, out_shape=(shape(side_rows, LANES), far_shape...  5.15 us
    pallas_call x1, Pallas kernels, tracers(): pl.pallas_call(tracer_kernel, out_shape=(shape(levels, rows, cols), shape...  4.61 us
    pallas_call x1, Pallas kernels, placed(): pl.pallas_call(functools.partial(place_kernel, capacity, n_cols), out_sha...  4.39 us
    pallas_call x1, Pallas kernels, opening(): pl.pallas_call(functools.partial(opening_kernel, capacity), out_shape=(sh...  3.51 us
  transfers between devices with their start and end apart: 7, of which 5 were waited for; matrix products, arithmetic and copies ran while one was open for 0% of the time, Pallas kernels for 13%

profile of v7, /device:TPU:1, one launch (start us, length us, event | category | flops | bytes accessed | tf_op | source)
XLA Modules:
  0.0 82.9 jit_solution(12602568092588965480)
XLA Ops:
  0.6 3.5 %opening.1 = (f32[160,256]{1,0:T(8,128)S(1)}, f32[224,256]{1,0:T(8,128)S(1)}, f32[8,128]{1,0:T(8,128)S(1)}, bf16[1024,512]{1,0:T(8,128)(2,1)S(1)}, s32[8,128]{1,0:T(8,128)S(1)}, /*index=5*/f32[128,128]{1,0:T(8,128)S(1)}) custom-call(f32[8,128]{1,0:T(8,128)S(1)} %broadcast_in_dim.3.token_ref, f32[16,32,256]{2,1,0:T(8,128)} %lam_ref.3, ...), custom_call_target="tpu_custom_call" | custom-call | tf_op jit(solution)/shard_map/opening/pallas_call | solution.py:799
  4.2 3.0 %collective-permute-start.1 = (f32[224,256]{1,0:T(8,128)S(1)}, f32[224,256]{1,0:T(8,128)S(1)}, u32[]{:S(2)}, u32[]{:S(2)}) collective-permute-start(f32[224,256]{1,0:T(8,128)S(1)} %get-tuple-element.32), channel_id=1, source_target_pairs={{112,0},{0,16},{16,32},{32,48},{48,64},{64,80},{80,96},{96,112},{1... | collective-permute-start | bytes 688136 | tf_op jit(solution)/shard_map/ppermute | solution.py:565
  7.2 0.0 collective-permute-start
  7.2 4.4 %place_segments.1 = (f32[4608,128]{1,0:T(8,128)}, f32[8,128]{1,0:T(8,128)S(1)}) custom-call(bf16[1024,512]{1,0:T(8,128)(2,1)S(1)} %get-tuple-element.26.data_ref, s32[8,128]{1,0:T(8,128)S(1)} %get-tuple-element.27.place_ref, f32[128,128]{1,0:T(8,128)S(1)} %get-tuple-element.28.meta_ref, f32[8,128]{1,0:T(8,128)S(1)} %get-tuple-element.29.token_ref), custom_call_target="tpu_custom_call" | custom-call | tf_op jit(solution)/shard_map/place_segments/pallas_call | solution.py:178
  11.6 0.6 collective-permute-done.refs_6_
  12.2 0.0 collective-permute-done.1.refs_7_
  12.2 9.6 %all-to-all-start = ((f32[128,1,4608]{2,1,0:T(1,128)}), f32[128,1,4608]{2,1,0:T(1,128)S(1)}, u32[]{:S(2)}, u32[]{:S(2)}) async-start(f32[128,1,4608]{2,1,0:T(1,128)} %bitcast.12), calls=%async_computation | async-start | bytes 4718592 | tf_op jit(solution)/shard_map/all_to_all | solution.py:912
  21.9 5.2 %edge_columns.1 = (f32[168,128]{1,0:T(8,128)S(1)}, f32[16,9,40,256]{3,2,1,0:T(8,128)}, f32[4,48,256]{2,1,0:T(8,128)S(1)}, f32[2,32,256]{2,1,0:T(8,128)S(1)}) custom-call(f32[8,128]{1,0:T(8,128)S(1)} %get-tuple-element.34.token_ref, f32[16,32,256]{2,1,0:T(8,128)} %lam_ref.3, f32[2,16,32,256]{3,2,1,0:T(8,128)} %zonal_ref.3, f32[2,16,32,256]{3,2,1,0:T(8,128)} %merid_ref.3, ...), custom_call_target="tpu_custom_call" | custom-call | tf_op jit(solution)/shard_map/edge_columns/pallas_call | solution.py:831
  27.0 0.0 copy-start
  27.0 1.5 %collective-permute-start.3 = (f32[168,128]{1,0:T(8,128)S(1)}, f32[168,128]{1,0:T(8,128)S(1)}, u32[]{:S(2)}, u32[]{:S(2)}) collective-permute-start(f32[168,128]{1,0:T(8,128)S(1)} %get-tuple-element.39), channel_id=1, source_target_pairs={{15,0},{0,1},{1,2},{2,3},{3,4},{4,5},{5,6},{6,7},{7,8},{8,9},{9,10... | collective-permute-start | bytes 258056 | tf_op jit(solution)/shard_map/ppermute | solution.py:565
  28.5 3.5 %collective-permute-start.2 = (f32[168,128]{1,0:T(8,128)S(1)}, f32[168,128]{1,0:T(8,128)S(1)}, u32[]{:S(2)}, u32[]{:S(2)}) collective-permute-start(f32[168,128]{1,0:T(8,128)S(1)} %get-tuple-element.39), channel_id=1, source_target_pairs={{1,0},{2,1},{3,2},{4,3},{5,4},{6,5},{7,6},{8,7},{9,8},{10,9},{11,1... | collective-permute-start | bytes 258056 | tf_op jit(solution)/shard_map/ppermute | solution.py:565
  32.0 21.9 %collective-permute-done.3.w_ref = f32[168,128]{1,0:T(8,128)S(1)} collective-permute-done((f32[168,128]{1,0:T(8,128)S(1)}, f32[168,128]{1,0:T(8,128)S(1)}, u32[]{:S(2)}, u32[]{:S(2)}) %collective-permute-start.3) | collective-permute-done | bytes 86048 | tf_op jit(solution)/shard_map/ppermute | solution.py:565
  53.9 0.0 collective-permute-done.2.e_ref
  53.9 0.2 surface_halos.1
  54.1 0.8 all-to-all-done
  54.8 1.6 %forcing.1 = (f32[32,384]{1,0:T(8,128)S(1)}, f32[8,128]{1,0:T(8,128)S(1)}) custom-call(f32[4608,128]{1,0:T(8,128)S(1)} %bitcast.9, f32[2,32,384]{2,1,0:T(8,128)S(1)} %get-tuple-element.40.height_ref, f32[6,48,384]{2,1,0:T(8,128)S(1)} %get-tuple-element.41.face_ref, f32[8,128]{1,0:T(8,128)S(1)} %get-tuple-element.34.token_ref), custom_call_target="tpu_custom_call" | custom-call | tf_op jit(solution)/shard_map/forcing/pallas_call | solution.py:294
  56.4 1.4 %collective-permute-start.5 = (f32[8,384]{1,0:T(8,128)S(1)}, f32[8,384]{1,0:T(8,128)S(1)}, u32[]{:S(2)}, u32[]{:S(2)}) collective-permute-start(f32[8,384]{1,0:T(8,128)S(1)} %get-tuple-element.50), channel_id=1, source_target_pairs={{112,0},{0,16},{16,32},{32,48},{48,64},{64,80},{80,96},{96,112},{1... | collective-permute-start | bytes 36872 | tf_op jit(solution)/shard_map/ppermute | solution.py:565
  57.9 0.0 collective-permute-start.4
  57.9 0.7 tracer_halos.1
  58.6 0.2 collective-permute-done.5.south_ref
  58.7 2.3 %collective-permute-done.4.north_ref = f32[8,384]{1,0:T(8,128)S(1)} collective-permute-done((f32[8,384]{1,0:T(8,128)S(1)}, f32[8,384]{1,0:T(8,128)S(1)}, u32[]{:S(2)}, u32[]{:S(2)}) %collective-permute-start.4) | collective-permute-done | bytes 12320 | tf_op jit(solution)/shard_map/ppermute | solution.py:565
  61.0 1.2 %krylov_sums.1 = (f32[128,128]{1,0:T(8,128)S(1)}, f32[9,48,384]{2,1,0:T(8,128)S(1)}) custom-call(f32[32,384]{1,0:T(8,128)S(1)} %get-tuple-element.42.q_ref, f32[8,384]{1,0:T(8,128)S(1)} %collective-permute-done.4.north_ref, f32[8,384]{1,0:T(8,128)S(1)} %collective-permute-done.5.south_ref, f32[6,48,384]{2,1,0:T(8,128)S(1)} %get-tuple-element.41.face_ref, ...), custom_call_target="tpu_custom_call" | custom-call | tf_op jit(solution)/shard_map/krylov_sums/pallas_call | solution.py:393
  62.2 16.1 %all_to_all.10 = f32[128,1,128]{2,1,0:T(1,128)S(1)} all-to-all(f32[128,1,128]{2,1,0:T(1,128)S(1)} %bitcast.11), channel_id=1, replica_groups=mesh['ty'=8,'tx'=16] {'ty','tx'}, dimensions={0} | all-to-all | bytes 131072 | tf_op jit(solution)/shard_map/all_to_all | solution.py:921
  78.3 0.0 copy-done
  78.3 4.6 %tracer_steps.1 = (f32[16,32,256]{2,1,0:T(8,128)}, f32[32,256]{1,0:T(8,128)}) custom-call(f32[16]{0:T(128)S(1)} %copy-done, f32[128,128]{1,0:T(8,128)S(1)} %bitcast.10, f32[9,48,384]{2,1,0:T(8,128)S(1)} %get-tuple-element.47.field_ref, f32[6,48,384]{2,1,0:T(8,128)S(1)} %get-tuple-element.41.face_ref, f32[16,9,40,256]{3,2,1,0:T(8,128)} %get-tuple-element.48.far_ref, ...), custom_call_target="tpu_custom_call" | custom-call | tf_op jit(solution)/shard_map/tracer_steps/pallas_call | solution.py:552
  (2 shorter events, 0.0 us)
Async XLA Ops:
  4.2 8.1 %collective-permute-start.1 = (f32[224,256]{1,0:T(8,128)S(1)}, f32[224,256]{1,0:T(8,128)S(1)}, u32[]{:S(2)}, u32[]{:S(2)}) collective-permute-start(f32[224,256]{1,0:T(8,128)S(1)} %get-tuple-element.32), channel_id=1, source_target_pairs={{112,0},{0,16},{16,32},{32,48},{48,64},{64,80},{80,96},{96,112},{1... | collective-permute-start | bytes 688136 | tf_op jit(solution)/shard_map/ppermute | solution.py:565
  7.2 5.0 %collective-permute-start = (f32[160,256]{1,0:T(8,128)S(1)}, f32[160,256]{1,0:T(8,128)S(1)}, u32[]{:S(2)}, u32[]{:S(2)}) collective-permute-start(f32[160,256]{1,0:T(8,128)S(1)} %get-tuple-element.31), channel_id=1, source_target_pairs={{16,0},{32,16},{48,32},{64,48},{80,64},{96,80},{112,96},{0,112},{1... | collective-permute-start | bytes 491528 | tf_op jit(solution)/shard_map/ppermute | solution.py:565
  12.2 42.6 %all-to-all-start = ((f32[128,1,4608]{2,1,0:T(1,128)}), f32[128,1,4608]{2,1,0:T(1,128)S(1)}, u32[]{:S(2)}, u32[]{:S(2)}) async-start(f32[128,1,4608]{2,1,0:T(1,128)} %bitcast.12), calls=%async_computation | async-start | bytes 4718592 | tf_op jit(solution)/shard_map/all_to_all | solution.py:912
  27.0 51.3 %copy-start = (f32[16]{0:T(128)S(1)}, f32[16]{0:T(128)}, u32[]{:S(2)}) copy-start(f32[16]{0:T(128)} %steric_ref.1) | copy-start | bytes 196
  27.0 26.9 %collective-permute-start.3 = (f32[168,128]{1,0:T(8,128)S(1)}, f32[168,128]{1,0:T(8,128)S(1)}, u32[]{:S(2)}, u32[]{:S(2)}) collective-permute-start(f32[168,128]{1,0:T(8,128)S(1)} %get-tuple-element.39), channel_id=1, source_target_pairs={{15,0},{0,1},{1,2},{2,3},{3,4},{4,5},{5,6},{6,7},{7,8},{8,9},{9,10... | collective-permute-start | bytes 258056 | tf_op jit(solution)/shard_map/ppermute | solution.py:565
  28.5 25.4 %collective-permute-start.2 = (f32[168,128]{1,0:T(8,128)S(1)}, f32[168,128]{1,0:T(8,128)S(1)}, u32[]{:S(2)}, u32[]{:S(2)}) collective-permute-start(f32[168,128]{1,0:T(8,128)S(1)} %get-tuple-element.39), channel_id=1, source_target_pairs={{1,0},{2,1},{3,2},{4,3},{5,4},{6,5},{7,6},{8,7},{9,8},{10,9},{11,1... | collective-permute-start | bytes 258056 | tf_op jit(solution)/shard_map/ppermute | solution.py:565
  56.4 2.3 %collective-permute-start.5 = (f32[8,384]{1,0:T(8,128)S(1)}, f32[8,384]{1,0:T(8,128)S(1)}, u32[]{:S(2)}, u32[]{:S(2)}) collective-permute-start(f32[8,384]{1,0:T(8,128)S(1)} %get-tuple-element.50), channel_id=1, source_target_pairs={{112,0},{0,16},{16,32},{32,48},{48,64},{64,80},{80,96},{96,112},{1... | collective-permute-start | bytes 36872 | tf_op jit(solution)/shard_map/ppermute | solution.py:565
  57.9 3.1 %collective-permute-start.4 = (f32[8,384]{1,0:T(8,128)S(1)}, f32[8,384]{1,0:T(8,128)S(1)}, u32[]{:S(2)}, u32[]{:S(2)}) collective-permute-start(f32[8,384]{1,0:T(8,128)S(1)} %get-tuple-element.51), channel_id=1, source_target_pairs={{16,0},{32,16},{48,32},{64,48},{80,64},{96,80},{112,96},{0,112},{1... | collective-permute-start | bytes 36872 | tf_op jit(solution)/shard_map/ppermute | solution.py:565

commit v8 on v7

--- a/solution.py
+++ b/solution.py
@@ -148,9 +148,11 @@
                 jnp.take_along_axis(value[rows], ends, axis=1),
                 jnp.take_along_axis(weight[rows], ends, axis=1),
             )
-            for part, (index, mine) in zip(parts, lanes):
+            for part, (index, mine) in zip(parts[:2], lanes):
                 spread = jnp.where(mine, jnp.take_along_axis(both, index, axis=1), 0.0)
                 part.append(spread[:8] + spread[8:])
+            index, mine = lanes[2]
+            parts[2].append(jnp.where(mine[8:], jnp.take_along_axis(both[8:], index[8:], axis=1), 0.0))
         edges = [
             jnp.concatenate([folded(part[i : i + 8]) for i in range(0, n_cols, 8)], axis=0) for part in parts
         ]

time: 83.2 us -> 83 us (level)
  transfers between devices with their start and end apart: 7 -> 7, of which waited for: 5 -> 5; matrix products, arithmetic and copies ran while one was open for 0% -> 0% of each run, Pallas kernels for 13% -> 12%
where the time goes in v8:
time: 83 us; the launch traced here: 82.7 us
  waiting for transfers between devices  26.2 us (32%)
  Pallas kernels  20.9 us (25%)
  starting transfers between devices  18.8 us (23%)
  blocking collectives  16.1 us (19%)
    ppermute x6, waiting for transfers between devices, beside(): lax.ppermute(cells, axis, [((i + step) % count, i) for i in range(count)])  25.4 us
    all_to_all x1, blocking collectives, on_device(): lax.all_to_all(mine.reshape(devices, 1, LANES), AXES, split_axis=0, conca...  16.1 us
    ppermute x6, starting transfers between devices, beside(): lax.ppermute(cells, axis, [((i + step) % count, i) for i in range(count)])  9.45 us
    all_to_all x1, starting transfers between devices, on_device(): lax.all_to_all(sent.reshape(devices, 1, -1), AXES, split_axis=0, concat_a...  9.36 us
    pallas_call x1, Pallas kernels, edges_to_tx(): pl.pallas_call(cols_kernel, out_shape=(shape(side_rows, LANES), far_shape...  5.15 us
    pallas_call x1, Pallas kernels, tracers(): pl.pallas_call(tracer_kernel, out_shape=(shape(levels, rows, cols), shape...  4.61 us
    pallas_call x1, Pallas kernels, placed(): pl.pallas_call(functools.partial(place_kernel, capacity, n_cols), out_sha...  4.02 us
    pallas_call x1, Pallas kernels, opening(): pl.pallas_call(functools.partial(opening_kernel, capacity), out_shape=(sh...  3.51 us
  transfers between devices with their start and end apart: 7, of which 5 were waited for; matrix products, arithmetic and copies ran while one was open for 0% of the time, Pallas kernels for 12%

profile of v8, /device:TPU:1, one launch (start us, length us, event | category | flops | bytes accessed | tf_op | source)
XLA Modules:
  0.0 82.7 jit_solution(10009081665629834170)
XLA Ops:
  0.6 3.5 %opening.1 = (f32[160,256]{1,0:T(8,128)S(1)}, f32[224,256]{1,0:T(8,128)S(1)}, f32[8,128]{1,0:T(8,128)S(1)}, bf16[1024,512]{1,0:T(8,128)(2,1)S(1)}, s32[8,128]{1,0:T(8,128)S(1)}, /*index=5*/f32[128,128]{1,0:T(8,128)S(1)}) custom-call(f32[8,128]{1,0:T(8,128)S(1)} %broadcast_in_dim.3.token_ref, f32[16,32,256]{2,1,0:T(8,128)} %lam_ref.3, ...), custom_call_target="tpu_custom_call" | custom-call | tf_op jit(solution)/shard_map/opening/pallas_call | solution.py:801
  4.2 3.0 %collective-permute-start.1 = (f32[224,256]{1,0:T(8,128)S(1)}, f32[224,256]{1,0:T(8,128)S(1)}, u32[]{:S(2)}, u32[]{:S(2)}) collective-permute-start(f32[224,256]{1,0:T(8,128)S(1)} %get-tuple-element.32), channel_id=1, source_target_pairs={{112,0},{0,16},{16,32},{32,48},{48,64},{64,80},{80,96},{96,112},{1... | collective-permute-start | bytes 688136 | tf_op jit(solution)/shard_map/ppermute | solution.py:567
  7.2 0.0 collective-permute-start
  7.2 4.0 %place_segments.1 = (f32[4608,128]{1,0:T(8,128)}, f32[8,128]{1,0:T(8,128)S(1)}) custom-call(bf16[1024,512]{1,0:T(8,128)(2,1)S(1)} %get-tuple-element.26.data_ref, s32[8,128]{1,0:T(8,128)S(1)} %get-tuple-element.27.place_ref, f32[128,128]{1,0:T(8,128)S(1)} %get-tuple-element.28.meta_ref, f32[8,128]{1,0:T(8,128)S(1)} %get-tuple-element.29.token_ref), custom_call_target="tpu_custom_call" | custom-call | tf_op jit(solution)/shard_map/place_segments/pallas_call | solution.py:180
  11.2 1.0 %collective-permute-done.refs_6_ = f32[160,256]{1,0:T(8,128)S(1)} collective-permute-done((f32[160,256]{1,0:T(8,128)S(1)}, f32[160,256]{1,0:T(8,128)S(1)}, u32[]{:S(2)}, u32[]{:S(2)}) %collective-permute-start) | collective-permute-done | bytes 163872 | tf_op jit(solution)/shard_map/ppermute | solution.py:567
  12.2 0.0 collective-permute-done.1.refs_7_
  12.2 9.4 %all-to-all-start = ((f32[128,1,4608]{2,1,0:T(1,128)}), f32[128,1,4608]{2,1,0:T(1,128)S(1)}, u32[]{:S(2)}, u32[]{:S(2)}) async-start(f32[128,1,4608]{2,1,0:T(1,128)} %bitcast.12), calls=%async_computation | async-start | bytes 4718592 | tf_op jit(solution)/shard_map/all_to_all | solution.py:914
  21.6 5.2 %edge_columns.1 = (f32[168,128]{1,0:T(8,128)S(1)}, f32[16,9,40,256]{3,2,1,0:T(8,128)}, f32[4,48,256]{2,1,0:T(8,128)S(1)}, f32[2,32,256]{2,1,0:T(8,128)S(1)}) custom-call(f32[8,128]{1,0:T(8,128)S(1)} %get-tuple-element.34.token_ref, f32[16,32,256]{2,1,0:T(8,128)} %lam_ref.3, f32[2,16,32,256]{3,2,1,0:T(8,128)} %zonal_ref.3, f32[2,16,32,256]{3,2,1,0:T(8,128)} %merid_ref.3, ...), custom_call_target="tpu_custom_call" | custom-call | tf_op jit(solution)/shard_map/edge_columns/pallas_call | solution.py:833
  26.8 0.0 copy-start
  26.8 1.5 %collective-permute-start.3 = (f32[168,128]{1,0:T(8,128)S(1)}, f32[168,128]{1,0:T(8,128)S(1)}, u32[]{:S(2)}, u32[]{:S(2)}) collective-permute-start(f32[168,128]{1,0:T(8,128)S(1)} %get-tuple-element.39), channel_id=1, source_target_pairs={{15,0},{0,1},{1,2},{2,3},{3,4},{4,5},{5,6},{6,7},{7,8},{8,9},{9,10... | collective-permute-start | bytes 258056 | tf_op jit(solution)/shard_map/ppermute | solution.py:567
  28.2 3.5 %collective-permute-start.2 = (f32[168,128]{1,0:T(8,128)S(1)}, f32[168,128]{1,0:T(8,128)S(1)}, u32[]{:S(2)}, u32[]{:S(2)}) collective-permute-start(f32[168,128]{1,0:T(8,128)S(1)} %get-tuple-element.39), channel_id=1, source_target_pairs={{1,0},{2,1},{3,2},{4,3},{5,4},{6,5},{7,6},{8,7},{9,8},{10,9},{11,1... | collective-permute-start | bytes 258056 | tf_op jit(solution)/shard_map/ppermute | solution.py:567
  31.7 21.9 %collective-permute-done.3.w_ref = f32[168,128]{1,0:T(8,128)S(1)} collective-permute-done((f32[168,128]{1,0:T(8,128)S(1)}, f32[168,128]{1,0:T(8,128)S(1)}, u32[]{:S(2)}, u32[]{:S(2)}) %collective-permute-start.3) | collective-permute-done | bytes 86048 | tf_op jit(solution)/shard_map/ppermute | solution.py:567
  53.6 0.0 collective-permute-done.2.e_ref
  53.7 0.2 surface_halos.1
  53.8 0.8 all-to-all-done
  54.6 1.6 %forcing.1 = (f32[32,384]{1,0:T(8,128)S(1)}, f32[8,128]{1,0:T(8,128)S(1)}) custom-call(f32[4608,128]{1,0:T(8,128)S(1)} %bitcast.9, f32[2,32,384]{2,1,0:T(8,128)S(1)} %get-tuple-element.40.height_ref, f32[6,48,384]{2,1,0:T(8,128)S(1)} %get-tuple-element.41.face_ref, f32[8,128]{1,0:T(8,128)S(1)} %get-tuple-element.34.token_ref), custom_call_target="tpu_custom_call" | custom-call | tf_op jit(solution)/shard_map/forcing/pallas_call | solution.py:296
  56.2 1.4 %collective-permute-start.5 = (f32[8,384]{1,0:T(8,128)S(1)}, f32[8,384]{1,0:T(8,128)S(1)}, u32[]{:S(2)}, u32[]{:S(2)}) collective-permute-start(f32[8,384]{1,0:T(8,128)S(1)} %get-tuple-element.50), channel_id=1, source_target_pairs={{112,0},{0,16},{16,32},{32,48},{48,64},{64,80},{80,96},{96,112},{1... | collective-permute-start | bytes 36872 | tf_op jit(solution)/shard_map/ppermute | solution.py:567
  57.6 0.0 collective-permute-start.4
  57.7 0.7 tracer_halos.1
  58.3 0.2 collective-permute-done.5.south_ref
  58.5 2.3 %collective-permute-done.4.north_ref = f32[8,384]{1,0:T(8,128)S(1)} collective-permute-done((f32[8,384]{1,0:T(8,128)S(1)}, f32[8,384]{1,0:T(8,128)S(1)}, u32[]{:S(2)}, u32[]{:S(2)}) %collective-permute-start.4) | collective-permute-done | bytes 12320 | tf_op jit(solution)/shard_map/ppermute | solution.py:567
  60.8 1.2 %krylov_sums.1 = (f32[128,128]{1,0:T(8,128)S(1)}, f32[9,48,384]{2,1,0:T(8,128)S(1)}) custom-call(f32[32,384]{1,0:T(8,128)S(1)} %get-tuple-element.42.q_ref, f32[8,384]{1,0:T(8,128)S(1)} %collective-permute-done.4.north_ref, f32[8,384]{1,0:T(8,128)S(1)} %collective-permute-done.5.south_ref, f32[6,48,384]{2,1,0:T(8,128)S(1)} %get-tuple-element.41.face_ref, ...), custom_call_target="tpu_custom_call" | custom-call | tf_op jit(solution)/shard_map/krylov_sums/pallas_call | solution.py:395
  62.0 16.1 %all_to_all.10 = f32[128,1,128]{2,1,0:T(1,128)S(1)} all-to-all(f32[128,1,128]{2,1,0:T(1,128)S(1)} %bitcast.11), channel_id=1, replica_groups=mesh['ty'=8,'tx'=16] {'ty','tx'}, dimensions={0} | all-to-all | bytes 131072 | tf_op jit(solution)/shard_map/all_to_all | solution.py:923
  78.1 0.0 copy-done
  78.1 4.6 %tracer_steps.1 = (f32[16,32,256]{2,1,0:T(8,128)}, f32[32,256]{1,0:T(8,128)}) custom-call(f32[16]{0:T(128)S(1)} %copy-done, f32[128,128]{1,0:T(8,128)S(1)} %bitcast.10, f32[9,48,384]{2,1,0:T(8,128)S(1)} %get-tuple-element.47.field_ref, f32[6,48,384]{2,1,0:T(8,128)S(1)} %get-tuple-element.41.face_ref, f32[16,9,40,256]{3,2,1,0:T(8,128)} %get-tuple-element.48.far_ref, ...), custom_call_target="tpu_custom_call" | custom-call | tf_op jit(solution)/shard_map/tracer_steps/pallas_call | solution.py:554
  (2 shorter events, 0.0 us)
Async XLA Ops:
  4.2 8.1 %collective-permute-start.1 = (f32[224,256]{1,0:T(8,128)S(1)}, f32[224,256]{1,0:T(8,128)S(1)}, u32[]{:S(2)}, u32[]{:S(2)}) collective-permute-start(f32[224,256]{1,0:T(8,128)S(1)} %get-tuple-element.32), channel_id=1, source_target_pairs={{112,0},{0,16},{16,32},{32,48},{48,64},{64,80},{80,96},{96,112},{1... | collective-permute-start | bytes 688136 | tf_op jit(solution)/shard_map/ppermute | solution.py:567
  7.2 5.0 %collective-permute-start = (f32[160,256]{1,0:T(8,128)S(1)}, f32[160,256]{1,0:T(8,128)S(1)}, u32[]{:S(2)}, u32[]{:S(2)}) collective-permute-start(f32[160,256]{1,0:T(8,128)S(1)} %get-tuple-element.31), channel_id=1, source_target_pairs={{16,0},{32,16},{48,32},{64,48},{80,64},{96,80},{112,96},{0,112},{1... | collective-permute-start | bytes 491528 | tf_op jit(solution)/shard_map/ppermute | solution.py:567
  12.2 42.4 %all-to-all-start = ((f32[128,1,4608]{2,1,0:T(1,128)}), f32[128,1,4608]{2,1,0:T(1,128)S(1)}, u32[]{:S(2)}, u32[]{:S(2)}) async-start(f32[128,1,4608]{2,1,0:T(1,128)} %bitcast.12), calls=%async_computation | async-start | bytes 4718592 | tf_op jit(solution)/shard_map/all_to_all | solution.py:914
  26.8 51.3 %copy-start = (f32[16]{0:T(128)S(1)}, f32[16]{0:T(128)}, u32[]{:S(2)}) copy-start(f32[16]{0:T(128)} %steric_ref.1) | copy-start | bytes 196
  26.8 26.9 %collective-permute-start.3 = (f32[168,128]{1,0:T(8,128)S(1)}, f32[168,128]{1,0:T(8,128)S(1)}, u32[]{:S(2)}, u32[]{:S(2)}) collective-permute-start(f32[168,128]{1,0:T(8,128)S(1)} %get-tuple-element.39), channel_id=1, source_target_pairs={{15,0},{0,1},{1,2},{2,3},{3,4},{4,5},{5,6},{6,7},{7,8},{8,9},{9,10... | collective-permute-start | bytes 258056 | tf_op jit(solution)/shard_map/ppermute | solution.py:567
  28.2 25.4 %collective-permute-start.2 = (f32[168,128]{1,0:T(8,128)S(1)}, f32[168,128]{1,0:T(8,128)S(1)}, u32[]{:S(2)}, u32[]{:S(2)}) collective-permute-start(f32[168,128]{1,0:T(8,128)S(1)} %get-tuple-element.39), channel_id=1, source_target_pairs={{1,0},{2,1},{3,2},{4,3},{5,4},{6,5},{7,6},{8,7},{9,8},{10,9},{11,1... | collective-permute-start | bytes 258056 | tf_op jit(solution)/shard_map/ppermute | solution.py:567
  56.2 2.3 %collective-permute-start.5 = (f32[8,384]{1,0:T(8,128)S(1)}, f32[8,384]{1,0:T(8,128)S(1)}, u32[]{:S(2)}, u32[]{:S(2)}) collective-permute-start(f32[8,384]{1,0:T(8,128)S(1)} %get-tuple-element.50), channel_id=1, source_target_pairs={{112,0},{0,16},{16,32},{32,48},{48,64},{64,80},{80,96},{96,112},{1... | collective-permute-start | bytes 36872 | tf_op jit(solution)/shard_map/ppermute | solution.py:567
  57.6 3.1 %collective-permute-start.4 = (f32[8,384]{1,0:T(8,128)S(1)}, f32[8,384]{1,0:T(8,128)S(1)}, u32[]{:S(2)}, u32[]{:S(2)}) collective-permute-start(f32[8,384]{1,0:T(8,128)S(1)} %get-tuple-element.51), channel_id=1, source_target_pairs={{16,0},{32,16},{48,32},{64,48},{80,64},{96,80},{112,96},{0,112},{1... | collective-permute-start | bytes 36872 | tf_op jit(solution)/shard_map/ppermute | solution.py:567

commit v9 on v8

--- a/solution.py
+++ b/solution.py
@@ -495,14 +495,13 @@
     return c, small_solve(second[:6], second[6:])
 
 
-def tracer_kernel(steric_ref, every_ref, field_ref, face_ref, far_ref, side_ref, mu_ref, rho_ref, tall_ref, sems):
+def tracer_kernel(steric_ref, every_ref, field_ref, face_ref, token_ref, *refs):
+    tracer_refs, (fringe_ref, side_ref, mu_ref, rho_ref, held_ref, sems) = refs[:5], refs[5:]
     levels, rows, cols = mu_ref.shape
-
-    def copy(level):
-        return pltpu.make_async_copy(far_ref.at[level], tall_ref.at[level], sems.at[level])
-
-    for level in range(levels):
-        copy(level).start()
+    for group in range(levels // GROUP):
+        for copy in level_copies(group, tracer_refs, held_ref, sems):
+            copy.start()
+    keep = kept(token_ref, 0, rows, rows, cols)
     high, wide = rows + 8, cols + LANES
 
     def trim(v):
@@ -522,7 +521,9 @@
 
     def one_level(level):
         height = steric_ref[level]
-        full = lambda at: jnp.concatenate([tall_ref[level, at], side_ref[at, level]], axis=1)
+        fields = tracer_fields(keep, *[held_ref[i, level] for i in range(7)])
+        tall = lambda at: jnp.concatenate([fields[at], fringe_ref[level, at]], axis=0)
+        full = lambda at: jnp.concatenate([tall(at), side_ref[at, level]], axis=1)
         g = ocean * (full(0) + height * rho_1)
         dx = g - pltpu.roll(g, wide - 1, 1)
         dy = g - pltpu.roll(g, high - 1, 0)
@@ -533,14 +534,14 @@
         dx = (g - pltpu.roll(g, wide - 1, 1))[:rows]
         dy = (g - pltpu.roll(g, high - 1, 0))[:, :cols]
         back_x = pltpu.roll(full(5)[:rows] * dx, 1, 1)[:, :cols]
-        back_y = pltpu.roll(tall_ref[level, 6] * dy, 1, 0)[:rows]
+        back_y = pltpu.roll(tall(6) * dy, 1, 0)[:rows]
         mu_ref[level] = g[:rows, :cols] - (
-            tall_ref[level, 7, 0:rows, :] * dx[:, :cols] + back_x + tall_ref[level, 8, 0:rows, :] * dy[:rows] + back_y
+            fields[7] * dx[:, :cols] + back_x + fields[8] * dy[:rows] + back_y
         )
 
     def some_levels(group, carry):
-        for i in range(GROUP):
-            copy(group * GROUP + i).wait()
+        for copy in level_copies(group, tracer_refs, held_ref, sems):
+            copy.wait()
         for i in range(GROUP):
             one_level(group * GROUP + i)
         return carry
@@ -548,18 +549,17 @@
     lax.fori_loop(0, levels // GROUP, some_levels, 0)
 
 
-def tracers(steric, every, fields, faces, tall, side):
-    levels, count, high, cols = tall.shape
-    rows = high - 8
+def tracers(steric, every, fields, faces, token, tracer, fringe, side):
+    levels, rows, cols = tracer[0].shape
     return pl.pallas_call(
         tracer_kernel,
         out_shape=(shape(levels, rows, cols), shape(rows, cols)),
-        in_specs=[SCALAR] + [VMEM] * 3 + [HBM, VMEM],
+        in_specs=[SCALAR] + [VMEM] * 4 + [HBM] * 5 + [VMEM] * 2,
         out_specs=(VMEM, VMEM),
-        scratch_shapes=[pltpu.VMEM((levels, count, high, cols), F32), pltpu.SemaphoreType.DMA((levels,))],
+        scratch_shapes=[pltpu.VMEM((7, levels, rows, cols), F32), pltpu.SemaphoreType.DMA((7 * levels // GROUP,))],
         compiler_params=params(20),
         name="tracer_steps",
-    )(steric, every, fields, faces, *far((tall,)), side)
+    )(steric, every, fields, faces, token, *far(tracer), fringe, side)
 
 
 def beside(cells, axis, step):
@@ -698,26 +698,33 @@
 GROUP = 4
 
 
+def level_copies(group, refs, held_ref, sems):
+    lam_ref, zonal_ref, merid_ref, mix_x_ref, mix_y_ref = refs
+    block = pl.ds(group * GROUP, GROUP)
+    sources = (
+        lam_ref.at[block],
+        zonal_ref.at[1, block],
+        merid_ref.at[1, block],
+        zonal_ref.at[0, block],
+        merid_ref.at[0, block],
+        mix_x_ref.at[block],
+        mix_y_ref.at[block],
+    )
+    return [
+        pltpu.make_async_copy(source, held_ref.at[i, block], sems.at[7 * group + i]) for i, source in enumerate(sources)
+    ]
+
+
 def cols_kernel(token_ref, lam_ref, zonal_ref, merid_ref, mix_x_ref, mix_y_ref, *refs):
     surface_refs, height_refs, (n_ref, s_ref) = refs[:4], refs[4:6], refs[6:8]
-    out_ref, far_ref, face_ref, height_ref, held_ref, flat_ref, tall_ref, sems, far_sems = refs[8:]
+    out_ref, fringe_ref, face_ref, height_ref, held_ref, flat_ref, sems = refs[8:]
     levels, rows, cols = lam_ref.shape
+    tracer_refs = (lam_ref, zonal_ref, merid_ref, mix_x_ref, mix_y_ref)
     copies = []
     for group in range(levels // GROUP):
-        block = pl.ds(group * GROUP, GROUP)
-        for i, source in enumerate(
-            (
-                lam_ref.at[block],
-                zonal_ref.at[1, block],
-                merid_ref.at[1, block],
-                zonal_ref.at[0, block],
-                merid_ref.at[0, block],
-                mix_x_ref.at[block],
-                mix_y_ref.at[block],
-            )
-        ):
-            copies.append(pltpu.make_async_copy(source, held_ref.at[i, block], sems.at[len(copies)]))
-            copies[-1].start()
+        copies += level_copies(group, tracer_refs, held_ref, sems)
+    for copy in copies:
+        copy.start()
     keep = kept(token_ref, 0, rows, rows, cols)
     high = rows + 8
     used = 2 * TRACER_WIDTH * len(SIDE)
@@ -735,27 +742,21 @@
         height_ref[at] = ref[...]
         talls.append(jnp.concatenate([ref[...], jnp.zeros((16, cols), F32)], axis=0))
     out_ref[base : base + rows + 16, :] = gathered(talls, FACE_WIDTH)
-    far = []
     for level in range(levels):
         if level % GROUP == 0:
             for copy in copies[7 * (level // GROUP) : 7 * (level // GROUP) + 7]:
                 copy.wait()
         fields = tracer_fields(keep, *[held_ref[i, level] for i in range(7)])
         talls = []
-        for pick, field in enumerate(fields):
-            tall_ref[level, pick, 0:rows, :] = field
+        for pick, field in enumerate(fields[:7]):
             edge = edge_rows(n_ref, s_ref, pick, levels, level, cols)
-            tall_ref[level, pick, rows:high, :] = edge
+            fringe_ref[level, pick] = edge
             if pick in SIDE:
                 talls.append(jnp.concatenate([field, edge], axis=0))
         flat_ref[level * high : (level + 1) * high, :] = gathered(talls, TRACER_WIDTH)
-        far.append(pltpu.make_async_copy(tall_ref.at[level], far_ref.at[level], far_sems.at[level]))
-        far[-1].start()
     for b in range(blocks):
         turned = jnp.transpose(flat_ref[b * LANES : (b + 1) * LANES, :])
         out_ref[b * used : (b + 1) * used, :] = turned[:used]
-    for copy in far:
-        copy.wait()
 
 
 def side_kernel(strip_ref, token_ref, side_ref, next_ref, flat_ref):
@@ -830,27 +831,25 @@
     levels, rows, cols = tracer[0].shape
     high = rows + 8
     side_rows = 2 * TRACER_WIDTH * len(SIDE) * levels * high // LANES + rows + 16
-    sides, tall, faces, heights = pl.pallas_call(
+    sides, fringe, faces, heights = pl.pallas_call(
         cols_kernel,
         out_shape=(
             shape(side_rows, LANES),
-            far_shape(levels, 9, high, cols),
+            shape(levels, 7, 8, cols),
             shape(4, rows + 16, cols),
             shape(2, rows, cols),
         ),
         in_specs=[VMEM] + [HBM] * 5 + [VMEM] * 8,
-        out_specs=(VMEM, HBM, VMEM, VMEM),
+        out_specs=(VMEM,) * 4,
         scratch_shapes=[
             pltpu.VMEM((7, levels, rows, cols), F32),
             pltpu.VMEM((levels * high, LANES), F32),
-            pltpu.VMEM((levels, 9, high, cols), F32),
             pltpu.SemaphoreType.DMA((7 * levels // GROUP,)),
-            pltpu.SemaphoreType.DMA((levels,)),
         ],
         compiler_params=params(24),
         name="edge_columns",
     )(token, *far(tracer), *far(surface), *far(heights), north, south)
-    return (beside(sides, "tx", 1), beside(sides, "tx", -1)), tall, faces, heights
+    return (beside(sides, "tx", 1), beside(sides, "tx", -1)), fringe, faces, heights
 
 
 def faces_with_halo(token, tall, heights, east, west):
@@ -914,7 +913,7 @@
     got = lax.all_to_all(
         sent.reshape(devices, 1, -1), AXES, split_axis=0, concat_axis=0, tiled=True
     ).reshape(sent.shape)
-    around_tx, tall, faces, heights = edges_to_tx(token, tracer, surface, (lam_eta, eta_saved), *around_ty)
+    around_tx, fringe, faces, heights = edges_to_tx(token, tracer, surface, (lam_eta, eta_saved), *around_ty)
     faces, heights, strips = faces_with_halo(token, faces, heights, *around_tx)
     rhs, token = unpack(got, heights, faces, token, capacity)
     north, south = beside(rhs[:8], "ty", 1), beside(rhs[-8:], "ty", -1)
@@ -923,7 +922,7 @@
     every = lax.all_to_all(
         mine.reshape(devices, 1, LANES), AXES, split_axis=0, concat_axis=0, tiled=True
     ).reshape(devices, LANES)
-    return tracers(steric, every, krylov_fields, faces, tall, sides)
+    return tracers(steric, every, krylov_fields, faces, token, tracer, fringe, sides)
 
 
 def solution(mesh):

time: 83 us -> 83.1 us (level)
  Pallas kernels: 20.9 us -> 19.2 us
  local copies, waits for them, and re-layouts: 0.01 us -> 0.95 us
  waiting for transfers between devices: 26.2 us -> 27.1 us
    pallas_call x1, Pallas kernels: 5.15 us -> 3.46 us  [edges_to_tx(): pl.pallas_call(cols_kernel, out_shape=(shape(side_rows, LANES), shape(lev...]
    ppermute x6, waiting for transfers between devices: 25.4 us -> 26.3 us  [beside(): lax.ppermute(cells, axis, [((i + step) % count, i) for i in range(count)])]
    unnamed x2 -> x6, local copies, waits for them, and re-layouts: 0.01 us -> 0.95 us
  transfers between devices with their start and end apart: 7 -> 7, of which waited for: 5 -> 5; matrix products, arithmetic and copies ran while one was open for 0% -> 0% of each run, Pallas kernels for 12% -> 10%
where the time goes in v9:
time: 83.1 us; the launch traced here: 82.8 us
  waiting for transfers between devices  27.1 us (33%)
  Pallas kernels  19.2 us (23%)
  starting transfers between devices  18.7 us (23%)
  blocking collectives  16.1 us (19%)
  local copies, waits for them, and re-layouts  0.95 us (1%)
    ppermute x6, waiting for transfers between devices, beside(): lax.ppermute(cells, axis, [((i + step) % count, i) for i in range(count)])  26.3 us
    all_to_all x1, blocking collectives, on_device(): lax.all_to_all(mine.reshape(devices, 1, LANES), AXES, split_axis=0, conca...  16.1 us
    all_to_all x1, starting transfers between devices, on_device(): lax.all_to_all(sent.reshape(devices, 1, -1), AXES, split_axis=0, concat_a...  9.36 us
    ppermute x6, starting transfers between devices, beside(): lax.ppermute(cells, axis, [((i + step) % count, i) for i in range(count)])  9.31 us
    pallas_call x1, Pallas kernels, tracers(): pl.pallas_call(tracer_kernel, out_shape=(shape(levels, rows, cols), shape...  4.74 us
    pallas_call x1, Pallas kernels, placed(): pl.pallas_call(functools.partial(place_kernel, capacity, n_cols), out_sha...  3.96 us
    pallas_call x1, Pallas kernels, opening(): pl.pallas_call(functools.partial(opening_kernel, capacity), out_shape=(sh...  3.47 us
    pallas_call x1, Pallas kernels, edges_to_tx(): pl.pallas_call(cols_kernel, out_shape=(shape(side_rows, LANES), shape(lev...  3.46 us
  transfers between devices with their start and end apart: 7, of which 5 were waited for; matrix products, arithmetic and copies ran while one was open for 0% of the time, Pallas kernels for 10%

profile of v9, /device:TPU:1, one launch (start us, length us, event | category | flops | bytes accessed | tf_op | source)
XLA Modules:
  0.0 82.8 jit_solution(12846675221524278287)
XLA Ops:
  0.6 3.5 %opening.1 = (f32[160,256]{1,0:T(8,128)S(1)}, f32[224,256]{1,0:T(8,128)S(1)}, f32[8,128]{1,0:T(8,128)S(1)}, bf16[1024,512]{1,0:T(8,128)(2,1)S(1)}, s32[8,128]{1,0:T(8,128)S(1)}, /*index=5*/f32[128,128]{1,0:T(8,128)S(1)}) custom-call(f32[8,128]{1,0:T(8,128)S(1)} %broadcast_in_dim.3.token_ref, f32[16,32,256]{2,1,0:T(8,128)} %refs_0_.5, ...), custom_call_target="tpu_custom_call" | custom-call | tf_op jit(solution)/shard_map/opening/pallas_call | solution.py:802
  4.1 3.0 %collective-permute-start.1 = (f32[224,256]{1,0:T(8,128)S(1)}, f32[224,256]{1,0:T(8,128)S(1)}, u32[]{:S(2)}, u32[]{:S(2)}) collective-permute-start(f32[224,256]{1,0:T(8,128)S(1)} %get-tuple-element.32), channel_id=1, source_target_pairs={{112,0},{0,16},{16,32},{32,48},{48,64},{64,80},{80,96},{96,112},{1... | collective-permute-start | bytes 688136 | tf_op jit(solution)/shard_map/ppermute | solution.py:567
  7.2 0.0 collective-permute-start
  7.2 4.0 %place_segments.1 = (f32[4608,128]{1,0:T(8,128)}, f32[8,128]{1,0:T(8,128)S(1)}) custom-call(bf16[1024,512]{1,0:T(8,128)(2,1)S(1)} %get-tuple-element.26.data_ref, s32[8,128]{1,0:T(8,128)S(1)} %get-tuple-element.27.place_ref, f32[128,128]{1,0:T(8,128)S(1)} %get-tuple-element.28.meta_ref, f32[8,128]{1,0:T(8,128)S(1)} %get-tuple-element.29.token_ref), custom_call_target="tpu_custom_call" | custom-call | tf_op jit(solution)/shard_map/place_segments/pallas_call | solution.py:180
  11.1 1.1 %collective-permute-done.refs_6_ = f32[160,256]{1,0:T(8,128)S(1)} collective-permute-done((f32[160,256]{1,0:T(8,128)S(1)}, f32[160,256]{1,0:T(8,128)S(1)}, u32[]{:S(2)}, u32[]{:S(2)}) %collective-permute-start) | collective-permute-done | bytes 163872 | tf_op jit(solution)/shard_map/ppermute | solution.py:567
  12.2 0.0 collective-permute-done.1.refs_7_
  12.2 9.4 %all-to-all-start = ((f32[128,1,4608]{2,1,0:T(1,128)}), f32[128,1,4608]{2,1,0:T(1,128)S(1)}, u32[]{:S(2)}, u32[]{:S(2)}) async-start(f32[128,1,4608]{2,1,0:T(1,128)} %bitcast.12), calls=%async_computation | async-start | bytes 4718592 | tf_op jit(solution)/shard_map/all_to_all | solution.py:913
  21.6 3.5 %edge_columns.1 = (f32[168,128]{1,0:T(8,128)S(1)}, f32[16,7,8,256]{3,2,1,0:T(8,128)S(1)}, f32[4,48,256]{2,1,0:T(8,128)S(1)}, f32[2,32,256]{2,1,0:T(8,128)S(1)}) custom-call(f32[8,128]{1,0:T(8,128)S(1)} %get-tuple-element.34.token_ref, f32[16,32,256]{2,1,0:T(8,128)} %refs_0_.5, f32[2,16,32,256]{3,2,1,0:T(8,128)} %refs_1_.5, f32[2,16,32,256]{3,2,1,0:T(8,128)} %refs_2_.5, ...), custom_call_target="tpu_custom_call" | custom-call | tf_op jit(solution)/shard_map/edge_columns/pallas_call | solution.py:834
  25.0 0.0 copy-start
  25.1 0.9 %copy-done = f32[16,7,8,256]{3,2,1,0:T(8,128)} copy-done((f32[16,7,8,256]{3,2,1,0:T(8,128)}, f32[16,7,8,256]{3,2,1,0:T(8,128)S(1)}, u32[]{:S(2)}) %copy-start) | copy-done | bytes 917528
  26.0 0.0 copy-start.2
  26.0 1.4 %collective-permute-start.3 = (f32[168,128]{1,0:T(8,128)S(1)}, f32[168,128]{1,0:T(8,128)S(1)}, u32[]{:S(2)}, u32[]{:S(2)}) collective-permute-start(f32[168,128]{1,0:T(8,128)S(1)} %get-tuple-element.39), channel_id=1, source_target_pairs={{15,0},{0,1},{1,2},{2,3},{3,4},{4,5},{5,6},{6,7},{7,8},{8,9},{9,10... | collective-permute-start | bytes 258056 | tf_op jit(solution)/shard_map/ppermute | solution.py:567
  27.4 3.4 %collective-permute-start.2 = (f32[168,128]{1,0:T(8,128)S(1)}, f32[168,128]{1,0:T(8,128)S(1)}, u32[]{:S(2)}, u32[]{:S(2)}) collective-permute-start(f32[168,128]{1,0:T(8,128)S(1)} %get-tuple-element.39), channel_id=1, source_target_pairs={{1,0},{2,1},{3,2},{4,3},{5,4},{6,5},{7,6},{8,7},{9,8},{10,9},{11,1... | collective-permute-start | bytes 258056 | tf_op jit(solution)/shard_map/ppermute | solution.py:567
  30.8 22.8 %collective-permute-done.3.w_ref = f32[168,128]{1,0:T(8,128)S(1)} collective-permute-done((f32[168,128]{1,0:T(8,128)S(1)}, f32[168,128]{1,0:T(8,128)S(1)}, u32[]{:S(2)}, u32[]{:S(2)}) %collective-permute-start.3) | collective-permute-done | bytes 86048 | tf_op jit(solution)/shard_map/ppermute | solution.py:567
  53.6 0.0 collective-permute-done.2.e_ref
  53.6 0.2 surface_halos.1
  53.8 0.8 all-to-all-done
  54.6 0.0 copy-start.1
  54.6 1.6 %forcing.1 = (f32[32,384]{1,0:T(8,128)S(1)}, f32[8,128]{1,0:T(8,128)S(1)}) custom-call(f32[4608,128]{1,0:T(8,128)S(1)} %bitcast.9, f32[2,32,384]{2,1,0:T(8,128)S(1)} %get-tuple-element.40.height_ref, f32[6,48,384]{2,1,0:T(8,128)S(1)} %get-tuple-element.41.face_ref, f32[8,128]{1,0:T(8,128)S(1)} %get-tuple-element.34.token_ref), custom_call_target="tpu_custom_call" | custom-call | tf_op jit(solution)/shard_map/forcing/pallas_call | solution.py:296
  56.2 1.5 %collective-permute-start.5 = (f32[8,384]{1,0:T(8,128)S(1)}, f32[8,384]{1,0:T(8,128)S(1)}, u32[]{:S(2)}, u32[]{:S(2)}) collective-permute-start(f32[8,384]{1,0:T(8,128)S(1)} %get-tuple-element.50), channel_id=1, source_target_pairs={{112,0},{0,16},{16,32},{32,48},{48,64},{64,80},{80,96},{96,112},{1... | collective-permute-start | bytes 36872 | tf_op jit(solution)/shard_map/ppermute | solution.py:567
  57.6 0.0 collective-permute-start.4
  57.6 0.7 tracer_halos.1
  58.3 0.2 collective-permute-done.5.south_ref
  58.5 2.3 %collective-permute-done.4.north_ref = f32[8,384]{1,0:T(8,128)S(1)} collective-permute-done((f32[8,384]{1,0:T(8,128)S(1)}, f32[8,384]{1,0:T(8,128)S(1)}, u32[]{:S(2)}, u32[]{:S(2)}) %collective-permute-start.4) | collective-permute-done | bytes 12320 | tf_op jit(solution)/shard_map/ppermute | solution.py:567
  60.7 1.2 %krylov_sums.1 = (f32[128,128]{1,0:T(8,128)S(1)}, f32[9,48,384]{2,1,0:T(8,128)S(1)}) custom-call(f32[32,384]{1,0:T(8,128)S(1)} %get-tuple-element.42.q_ref, f32[8,384]{1,0:T(8,128)S(1)} %collective-permute-done.4.north_ref, f32[8,384]{1,0:T(8,128)S(1)} %collective-permute-done.5.south_ref, f32[6,48,384]{2,1,0:T(8,128)S(1)} %get-tuple-element.41.face_ref, ...), custom_call_target="tpu_custom_call" | custom-call | tf_op jit(solution)/shard_map/krylov_sums/pallas_call | solution.py:395
  61.9 16.1 %all_to_all.10 = f32[128,1,128]{2,1,0:T(1,128)S(1)} all-to-all(f32[128,1,128]{2,1,0:T(1,128)S(1)} %bitcast.11), channel_id=1, replica_groups=mesh['ty'=8,'tx'=16] {'ty','tx'}, dimensions={0} | all-to-all | bytes 131072 | tf_op jit(solution)/shard_map/all_to_all | solution.py:922
  78.0 0.0 copy-done.2
  78.0 0.0 copy-done.1
  78.0 4.7 %tracer_steps.1 = (f32[16,32,256]{2,1,0:T(8,128)}, f32[32,256]{1,0:T(8,128)}) custom-call(f32[16]{0:T(128)S(1)} %copy-done.2, f32[128,128]{1,0:T(8,128)S(1)} %bitcast.10, f32[9,48,384]{2,1,0:T(8,128)S(1)} %get-tuple-element.47.field_ref, f32[6,48,384]{2,1,0:T(8,128)S(1)} %get-tuple-element.41.face_ref, f32[8,128]{1,0:T(8,128)S(1)} %get-tuple-element.45.token_ref, ...), custom_call_target="tpu_custom_call" | custom-call | tf_op jit(solution)/shard_map/tracer_steps/pallas_call | solution.py:554
  (2 shorter events, 0.0 us)
Async XLA Ops:
  4.1 8.1 %collective-permute-start.1 = (f32[224,256]{1,0:T(8,128)S(1)}, f32[224,256]{1,0:T(8,128)S(1)}, u32[]{:S(2)}, u32[]{:S(2)}) collective-permute-start(f32[224,256]{1,0:T(8,128)S(1)} %get-tuple-element.32), channel_id=1, source_target_pairs={{112,0},{0,16},{16,32},{32,48},{48,64},{64,80},{80,96},{96,112},{1... | collective-permute-start | bytes 688136 | tf_op jit(solution)/shard_map/ppermute | solution.py:567
  7.2 5.0 %collective-permute-start = (f32[160,256]{1,0:T(8,128)S(1)}, f32[160,256]{1,0:T(8,128)S(1)}, u32[]{:S(2)}, u32[]{:S(2)}) collective-permute-start(f32[160,256]{1,0:T(8,128)S(1)} %get-tuple-element.31), channel_id=1, source_target_pairs={{16,0},{32,16},{48,32},{64,48},{80,64},{96,80},{112,96},{0,112},{1... | collective-permute-start | bytes 491528 | tf_op jit(solution)/shard_map/ppermute | solution.py:567
  12.2 42.4 %all-to-all-start = ((f32[128,1,4608]{2,1,0:T(1,128)}), f32[128,1,4608]{2,1,0:T(1,128)S(1)}, u32[]{:S(2)}, u32[]{:S(2)}) async-start(f32[128,1,4608]{2,1,0:T(1,128)} %bitcast.12), calls=%async_computation | async-start | bytes 4718592 | tf_op jit(solution)/shard_map/all_to_all | solution.py:913
  25.0 0.9 %copy-start = (f32[16,7,8,256]{3,2,1,0:T(8,128)}, f32[16,7,8,256]{3,2,1,0:T(8,128)S(1)}, u32[]{:S(2)}) copy-start(f32[16,7,8,256]{3,2,1,0:T(8,128)S(1)} %get-tuple-element.48.refs_5_) | copy-start | bytes 2752516
  26.0 52.0 %copy-start.2 = (f32[16]{0:T(128)S(1)}, f32[16]{0:T(128)}, u32[]{:S(2)}) copy-start(f32[16]{0:T(128)} %steric_ref.1) | copy-start | bytes 196
  26.0 27.6 %collective-permute-start.3 = (f32[168,128]{1,0:T(8,128)S(1)}, f32[168,128]{1,0:T(8,128)S(1)}, u32[]{:S(2)}, u32[]{:S(2)}) collective-permute-start(f32[168,128]{1,0:T(8,128)S(1)} %get-tuple-element.39), channel_id=1, source_target_pairs={{15,0},{0,1},{1,2},{2,3},{3,4},{4,5},{5,6},{6,7},{7,8},{8,9},{9,10... | collective-permute-start | bytes 258056 | tf_op jit(solution)/shard_map/ppermute | solution.py:567
  27.4 26.2 %collective-permute-start.2 = (f32[168,128]{1,0:T(8,128)S(1)}, f32[168,128]{1,0:T(8,128)S(1)}, u32[]{:S(2)}, u32[]{:S(2)}) collective-permute-start(f32[168,128]{1,0:T(8,128)S(1)} %get-tuple-element.39), channel_id=1, source_target_pairs={{1,0},{2,1},{3,2},{4,3},{5,4},{6,5},{7,6},{8,7},{9,8},{10,9},{11,1... | collective-permute-start | bytes 258056 | tf_op jit(solution)/shard_map/ppermute | solution.py:567
  54.6 23.5 %copy-start.1 = (f32[16,7,8,256]{3,2,1,0:T(8,128)S(1)}, f32[16,7,8,256]{3,2,1,0:T(8,128)}, u32[]{:S(2)}) copy-start(f32[16,7,8,256]{3,2,1,0:T(8,128)} %copy-done) | copy-start | bytes 2752516
  56.2 2.3 %collective-permute-start.5 = (f32[8,384]{1,0:T(8,128)S(1)}, f32[8,384]{1,0:T(8,128)S(1)}, u32[]{:S(2)}, u32[]{:S(2)}) collective-permute-start(f32[8,384]{1,0:T(8,128)S(1)} %get-tuple-element.50), channel_id=1, source_target_pairs={{112,0},{0,16},{16,32},{32,48},{48,64},{64,80},{80,96},{96,112},{1... | collective-permute-start | bytes 36872 | tf_op jit(solution)/shard_map/ppermute | solution.py:567
  57.6 3.1 %collective-permute-start.4 = (f32[8,384]{1,0:T(8,128)S(1)}, f32[8,384]{1,0:T(8,128)S(1)}, u32[]{:S(2)}, u32[]{:S(2)}) collective-permute-start(f32[8,384]{1,0:T(8,128)S(1)} %get-tuple-element.51), channel_id=1, source_target_pairs={{16,0},{32,16},{48,32},{64,48},{80,64},{96,80},{112,96},{0,112},{1... | collective-permute-start | bytes 36872 | tf_op jit(solution)/shard_map/ppermute | solution.py:567
